TPU v7x, 32 devices: a whole 2x2x4 slice. The times are simulated.
32 devices in a mesh: section: 2 (over x), row: 4 (over z), col: 4 (over y, core).
Axes of the slice: x: 2, y: 2, z: 4, core: 2. Of those that a mesh axis runs over, the one named last changes fastest.
Arguments:
- tokens_in: bfloat16 [2, 1024, 4096], P(None, 'row', 'col'), may hold values from -6 to 6
- doc_ids: int32 [2, 4, 1024], P(None, 'col'), may hold values from 0 to 7, never falling along the last dimension, each value on 1 to 512 neighbouring positions
- cotangent: bfloat16 [2, 1024, 4096], P(None, 'row', 'col'), may hold values from -6 to 6
- qkv_master: float32 [2, 3, 1024, 1024], P('section', None, 'row', 'col'), may hold values from -0.25 to 0.25
- out_master: float32 [2, 1024, 1024], P('section', 'row', 'col'), may hold values from -0.5 to 0.5
- unit_master: float32 [2, 1024, 4096], P('section', 'row', 'col'), may hold values from -0.1875 to 0.1875
- down_master: float32 [2, 1024, 4096], P('section', 'row', 'col'), may hold values from -0.09375 to 0.09375
- unit_bias: float32 [2, 4096], P('section', 'col'), may hold values from -3 to 3
- width_bias: float32 [2, 6, 1024], P('section', None, 'row'), may hold values from -2 to 2
- norm_gain: float32 [2, 2, 1024], P('section', None, 'row'), may hold values from 0.25 to 1.75
Outputs:
- layer_out: float32 [2, 2, 1024, 4096], P('section', None, 'row', 'col')
- input_grad: float32 [2, 2, 1024, 4096], P('section', None, 'row', 'col')
- grad_qkv: float32 [2, 3, 1024, 1024], P('section', None, 'row', 'col')
- grad_out: float32 [2, 1024, 1024], P('section', 'row', 'col')
- grad_unit: float32 [2, 1024, 4096], P('section', 'row', 'col')
- grad_down: float32 [2, 1024, 4096], P('section', 'row', 'col')
- grad_unit_bias: float32 [2, 4096], P('section', 'col')
- grad_width_bias: float32 [2, 6, 1024], P('section', None, 'row')
- grad_gain: float32 [2, 2, 1024], P('section', None, 'row')
Inputs may be any that keep to these rules, and one draw needn't show every extreme that they name: `doc_ids`: within each sequence the document numbers never fall, each of the 8 documents has 1 to 512 tokens, and one has exactly 512.
All inputs are finite; a program needn't handle non-finite values.
Results may differ from a plain program's by a relative error of at most 0.04.
Values may be sent and summed in bfloat16 or wider, within the bound.
A program may use at most 192 MiB of HBM per device.

v0:
```python
import jax
import jax.numpy as jnp
from jax import lax
from jax.sharding import PartitionSpec as P

HD = 64


EPSILON = 1e-05
NEG_BIG = -1e30


def from_behind(array, axis, by):
    peers = lax.axis_size(axis)
    return lax.ppermute(array, axis, [(i, (i + by) % peers) for i in range(peers)])


def gelu_exact(values):
    return jax.nn.gelu(values, approximate=False)


def attend_forward(seq_items):
    query_matrix, key_matrix, value_matrix, doc_row = seq_items
    same_doc = doc_row[:, None] == doc_row[None, :]
    logit_scores = jnp.einsum(
        "xgj,igj->gxi", query_matrix, key_matrix, preferred_element_type=jnp.float32
    )
    logit_scores = jnp.where(same_doc[None], logit_scores, NEG_BIG)
    row_max = jnp.max(logit_scores, axis=2, keepdims=True)
    expo_rows = jnp.exp(logit_scores - row_max)
    row_total = jnp.sum(expo_rows, axis=2, keepdims=True)
    probability_half = (expo_rows / row_total).astype(jnp.bfloat16)
    attended_rows = jnp.einsum(
        "bgy,ybt->gbt", probability_half, value_matrix, preferred_element_type=jnp.float32
    )
    return (attended_rows, (row_max + jnp.log(row_total))[:, :, 0])


def attend_backward(seq_items):
    query_matrix, key_matrix, value_matrix, gradient_row_block, log_total, doc_row = seq_items
    same_doc = doc_row[:, None] == doc_row[None, :]
    logit_scores = jnp.einsum(
        "xgj,igj->gxi", query_matrix, key_matrix, preferred_element_type=jnp.float32
    )
    logit_scores = jnp.where(same_doc[None], logit_scores, NEG_BIG)
    prob_rows = jnp.where(same_doc[None], jnp.exp(logit_scores - log_total[:, :, None]), 0.0)
    grad_value = jnp.einsum(
        "jsn,sju->nju",
        prob_rows.astype(jnp.bfloat16),
        gradient_row_block,
        preferred_element_type=jnp.float32,
    )
    grad_prob = jnp.einsum(
        "xgj,igj->gxi", gradient_row_block, value_matrix, preferred_element_type=jnp.float32
    )
    inner_sum = jnp.sum(prob_rows * grad_prob, axis=2, keepdims=True)
    score_gradient = (prob_rows * (grad_prob - inner_sum)).astype(jnp.bfloat16)
    grad_query = jnp.einsum(
        "bgy,ybt->gbt", score_gradient, key_matrix, preferred_element_type=jnp.float32
    )
    grad_key = jnp.einsum(
        "jsn,sju->nju", score_gradient, query_matrix, preferred_element_type=jnp.float32
    )
    return (grad_query, grad_key, grad_value)


def put_slot(buffer, slot_index, values, is_live):
    previous = lax.dynamic_index_in_dim(buffer, slot_index, 0, keepdims=False)
    return lax.dynamic_update_index_in_dim(
        buffer, jnp.where(is_live, values, previous), slot_index, 0
    )


def take_slot(buffer, slot_index):
    return lax.dynamic_index_in_dim(buffer, slot_index, 0, keepdims=False)


def local(
    tokens_in,
    doc_ids,
    cotangent,
    qkv_master,
    out_master,
    unit_master,
    down_master,
    unit_bias,
    width_bias,
    norm_gain,
):
    micro_count = tokens_in.shape[0]
    narrow = tokens_in.shape[1]
    tok_here = tokens_in.shape[2]
    row_count = lax.axis_size("row")
    full_width = narrow * row_count
    seq_here = doc_ids.shape[1]
    seq_len = doc_ids.shape[2]
    heads_here = narrow // HD
    head_scale = HD ** (-0.5)
    head_shape = (seq_here, seq_len, heads_here, HD)
    section_index = lax.axis_index("section")
    units_here = unit_master.shape[2]
    qkv_bf, out_bf = (
        lax.all_gather(qkv_master[0].astype(jnp.bfloat16), "col", axis=2, tiled=True),
        lax.all_gather(out_master[0].astype(jnp.bfloat16), "col", axis=1, tiled=True),
    )
    unit_bf, down_bf = (
        lax.all_gather(unit_master[0].astype(jnp.bfloat16), "row", axis=0, tiled=True),
        lax.all_gather(down_master[0].astype(jnp.bfloat16), "row", axis=0, tiled=True),
    )
    bias_rows = width_bias[0]
    gain_rows = norm_gain[0]
    unit_shift = unit_bias[0]

    def wide_rows(part):
        return lax.all_gather(part, "row", axis=1, tiled=True)

    def head_total(term):
        return lax.psum_scatter(
            term.astype(jnp.bfloat16), "row", scatter_dimension=1, tiled=True
        ).astype(jnp.float32)

    def row_pair(first, second):
        return lax.psum((first, second), "row")

    def col_tokens(part):
        return lax.all_gather(part, "col", axis=0, tiled=True)

    def token_block(rows_in):
        return lax.all_to_all(rows_in, "row", split_axis=0, concat_axis=1, tiled=True)

    def width_back(term):
        return lax.all_to_all(
            term.astype(jnp.bfloat16), "row", split_axis=1, concat_axis=0, tiled=True
        ).astype(term.dtype)

    def col_total(term):
        return lax.psum_scatter(
            term.astype(jnp.bfloat16), "col", scatter_dimension=0, tiled=True
        ).astype(jnp.float32)

    def section_send(values):
        return from_behind(values, "section", 1)

    def norm_forward(hidden, gain_row, bias_row):
        total_sum, square_sum = row_pair(jnp.sum(hidden, axis=1), jnp.sum(hidden * hidden, axis=1))
        mean_row = total_sum / full_width
        var_row = square_sum / full_width - mean_row * mean_row
        scale_row = lax.rsqrt(var_row + EPSILON)
        normed = (hidden - mean_row[:, None]) * scale_row[:, None]
        return (normed * gain_row + bias_row, normed, scale_row)

    def norm_backward(grad_out, normed, scale_row, gain_row):
        scaled = grad_out * gain_row
        first_sum, second_sum = row_pair(jnp.sum(scaled, axis=1), jnp.sum(scaled * normed, axis=1))
        return scale_row[:, None] * (
            scaled - first_sum[:, None] / full_width - normed * (second_sum[:, None] / full_width)
        )

    outputs = jnp.zeros((micro_count, tok_here, narrow), jnp.float32)
    grads_in = jnp.zeros((micro_count, tok_here, narrow), jnp.float32)
    saved_store = None
    received = jnp.zeros((tok_here, narrow), jnp.bfloat16)
    for clock_tick in range(micro_count + 1):
        micro_index = clock_tick - section_index
        is_live = (micro_index >= 0) & (micro_index < micro_count)
        slot_index = jnp.clip(micro_index, 0, micro_count - 1)
        section_input = jnp.where(
            section_index == 0, tokens_in[min(clock_tick, micro_count - 1)].T, received
        )
        doc_rows = take_slot(doc_ids, slot_index)
        layer_widened = wide_rows(section_input)
        projected = jnp.einsum(
            "td,ked->kte", layer_widened, qkv_bf, preferred_element_type=jnp.float32
        )
        layer_query_bf = ((projected[0] + bias_rows[0]) * head_scale).astype(jnp.bfloat16)
        layer_key_bf = projected[1].astype(jnp.bfloat16)
        layer_value_bf = (projected[2] + bias_rows[1]).astype(jnp.bfloat16)
        attended_rows, layer_log_total = lax.map(
            attend_forward,
            (
                layer_query_bf.reshape(head_shape),
                layer_key_bf.reshape(head_shape),
                layer_value_bf.reshape(head_shape),
                doc_rows,
            ),
        )
        layer_mixed_bf = attended_rows.reshape(tok_here, narrow).astype(jnp.bfloat16)
        attn_out = (
            head_total(jnp.dot(layer_mixed_bf, out_bf, preferred_element_type=jnp.float32))
            + bias_rows[2]
        )
        normed_one, layer_hat_one, layer_scale_one = norm_forward(
            section_input.astype(jnp.float32) + attn_out, gain_rows[0], bias_rows[3]
        )
        layer_block_rows = token_block(col_tokens(normed_one.astype(jnp.bfloat16)))
        layer_unit_pre = (
            jnp.dot(layer_block_rows, unit_bf, preferred_element_type=jnp.float32) + unit_shift
        )
        unit_act = gelu_exact(layer_unit_pre).astype(jnp.bfloat16)
        down_part = jnp.einsum("tf,df->td", unit_act, down_bf, preferred_element_type=jnp.float32)
        down_out = col_total(width_back(down_part)) + bias_rows[4]
        result, layer_hat_two, layer_scale_two = norm_forward(
            normed_one + down_out, gain_rows[1], bias_rows[5]
        )
        layer_saved_state = (
            layer_widened,
            layer_query_bf,
            layer_key_bf,
            layer_value_bf,
            layer_mixed_bf,
            layer_log_total,
            layer_hat_one,
            layer_scale_one,
            layer_hat_two,
            layer_scale_two,
            layer_block_rows,
            layer_unit_pre,
        )
        result, saved_state = (result, layer_saved_state)
        outputs = put_slot(outputs, slot_index, result, is_live)
        if saved_store is None:
            saved_store = tuple(
                (
                    jnp.zeros((micro_count,) + saved_item.shape, saved_item.dtype)
                    for saved_item in saved_state
                )
            )
        saved_store = tuple(
            (
                put_slot(buffer, slot_index, saved_item, is_live)
                for buffer, saved_item in zip(saved_store, saved_state)
            )
        )
        received = section_send(result.astype(jnp.bfloat16))
    totals = None
    back_received = jnp.zeros((tok_here, narrow), jnp.bfloat16)
    for clock_tick in range(micro_count + 1):
        micro_index = clock_tick - (1 - section_index)
        is_live = (micro_index >= 0) & (micro_index < micro_count)
        slot_index = jnp.clip(micro_index, 0, micro_count - 1)
        incoming = jnp.where(
            section_index == 1,
            cotangent[min(clock_tick, micro_count - 1)].T.astype(jnp.float32),
            back_received.astype(jnp.float32),
        )
        doc_rows = take_slot(doc_ids, slot_index)
        saved_state = tuple((take_slot(buffer, slot_index) for buffer in saved_store))
        (
            widened,
            query_bf,
            key_bf,
            value_bf,
            mixed_bf,
            log_total,
            hat_one,
            scale_one,
            hat_two,
            scale_two,
            block_rows,
            unit_pre,
        ) = saved_state
        grad_two = norm_backward(incoming, hat_two, scale_two, gain_rows[1])
        gain_two = jnp.sum(incoming * hat_two, axis=0)
        shift_two = jnp.sum(incoming, axis=0)
        grad_down = grad_two.astype(jnp.bfloat16)
        down_shift = jnp.sum(grad_down.astype(jnp.float32), axis=0)
        grad_block = token_block(col_tokens(grad_down))
        gelu_out, gelu_pull = jax.vjp(gelu_exact, unit_pre)
        act_bf = gelu_out.astype(jnp.bfloat16)
        layer_down_grad = jnp.einsum(
            "td,tf->df", grad_block, act_bf, preferred_element_type=jnp.float32
        )
        grad_act = jnp.einsum("td,df->tf", grad_block, down_bf, preferred_element_type=jnp.float32)
        grad_pre = gelu_pull(grad_act)[0].astype(jnp.bfloat16)
        layer_unit_grad_sum = jnp.sum(grad_pre.astype(jnp.float32), axis=0)
        layer_unit_grad = jnp.einsum(
            "td,tf->df", block_rows, grad_pre, preferred_element_type=jnp.float32
        )
        back_rows = jnp.einsum("tf,df->td", grad_pre, unit_bf, preferred_element_type=jnp.float32)
        grad_x1 = grad_two + col_total(width_back(back_rows))
        grad_one = norm_backward(grad_x1, hat_one, scale_one, gain_rows[0])
        gain_one = jnp.sum(grad_x1 * hat_one, axis=0)
        shift_one = jnp.sum(grad_x1, axis=0)
        grad_attn = grad_one.astype(jnp.bfloat16)
        out_shift = jnp.sum(grad_attn.astype(jnp.float32), axis=0)
        grad_wide = wide_rows(grad_attn)
        layer_out_grad = jnp.einsum(
            "th,td->hd", mixed_bf, grad_wide, preferred_element_type=jnp.float32
        )
        grad_mixed = jnp.einsum(
            "td,hd->th", grad_wide, out_bf, preferred_element_type=jnp.float32
        ).astype(jnp.bfloat16)
        grad_query, grad_key, grad_value = lax.map(
            attend_backward,
            (
                query_bf.reshape(head_shape),
                key_bf.reshape(head_shape),
                value_bf.reshape(head_shape),
                grad_mixed.reshape(head_shape),
                log_total,
                doc_rows,
            ),
        )
        query_term = grad_query.reshape(tok_here, narrow).astype(jnp.bfloat16) * head_scale
        key_term = grad_key.reshape(tok_here, narrow).astype(jnp.bfloat16)
        value_term = grad_value.reshape(tok_here, narrow).astype(jnp.bfloat16)
        grad_proj = jnp.stack([query_term, key_term, value_term])
        layer_qkv_grad = jnp.einsum(
            "kte,td->ked", grad_proj, widened, preferred_element_type=jnp.float32
        )
        back_wide = jnp.einsum("kte,ked->td", grad_proj, qkv_bf, preferred_element_type=jnp.float32)
        grad_input = grad_one + head_total(back_wide)
        query_shift = jnp.sum(query_term.astype(jnp.float32), axis=0)
        value_shift = jnp.sum(value_term.astype(jnp.float32), axis=0)
        layer_width_sums = jnp.stack(
            [
                query_shift,
                value_shift,
                out_shift,
                shift_one,
                down_shift,
                shift_two,
                gain_one,
                gain_two,
            ]
        )
        grad_input, grad_parts = (
            grad_input,
            (
                layer_qkv_grad,
                layer_out_grad,
                layer_unit_grad,
                layer_down_grad,
                layer_unit_grad_sum,
                layer_width_sums,
            ),
        )
        grads_in = put_slot(grads_in, slot_index, grad_input, is_live)
        grad_parts = tuple((jnp.where(is_live, grad_part, 0.0) for grad_part in grad_parts))
        if totals is None:
            totals = grad_parts
        else:
            totals = tuple(
                (total_part + grad_part for total_part, grad_part in zip(totals, grad_parts))
            )
        back_received = section_send(grad_input.astype(jnp.bfloat16))
    qkv_grad, out_grad, unit_grad, down_grad, unit_grad_sum, width_sums = totals
    qkv_sum = lax.psum_scatter(
        qkv_grad.astype(jnp.bfloat16), "col", scatter_dimension=2, tiled=True
    ).astype(jnp.float32)
    out_sum = lax.psum_scatter(
        out_grad.astype(jnp.bfloat16), "col", scatter_dimension=1, tiled=True
    ).astype(jnp.float32)
    packed = jnp.concatenate(
        [
            unit_grad.reshape(row_count, narrow, units_here),
            jnp.broadcast_to(unit_grad_sum, (row_count, 1, units_here)),
        ],
        axis=1,
    )
    packed = packed.reshape(row_count * (narrow + 1), units_here)
    unit_sum = lax.psum_scatter(
        packed.astype(jnp.bfloat16), "row", scatter_dimension=0, tiled=True
    ).astype(jnp.float32)
    down_sum = lax.psum_scatter(
        down_grad.astype(jnp.bfloat16), "row", scatter_dimension=0, tiled=True
    ).astype(jnp.float32)
    width_total = lax.psum(width_sums, "col")
    totals = (qkv_sum, out_sum, unit_sum[:narrow], down_sum, unit_sum[narrow], width_total)
    qkv_sum, out_sum, unit_sum, down_sum, unit_bias_sum, width_total = totals
    layer_result = jnp.swapaxes(outputs, 1, 2)
    grad_result = jnp.swapaxes(grads_in, 1, 2)
    return (
        layer_result[None],
        grad_result[None],
        qkv_sum[None],
        out_sum[None],
        unit_sum[None],
        down_sum[None],
        unit_bias_sum[None],
        width_total[:6][None],
        width_total[6:][None],
    )


def solution(mesh):
    placed = (
        P(None, "row", "col"),
        P(None, "col", None),
        P(None, "row", "col"),
        P("section", None, "row", "col"),
        P("section", "row", "col"),
        P("section", "row", "col"),
        P("section", "row", "col"),
        P("section", "col"),
        P("section", None, "row"),
        P("section", None, "row"),
    )
    return jax.shard_map(
        local,
        mesh=mesh,
        in_specs=placed,
        out_specs=(
            P("section", None, "row", "col"),
            P("section", None, "row", "col"),
            P("section", None, "row", "col"),
            P("section", "row", "col"),
            P("section", "row", "col"),
            P("section", "row", "col"),
            P("section", "col"),
            P("section", None, "row"),
            P("section", None, "row"),
        ),
        check_vma=False,
    )
```

profile of v0, /device:TPU:10, one launch (start us, length us, event | category | flops | bytes accessed | tf_op | source)
XLA Modules:
  0.0 2347.8 jit_solution(14002747826447599713)
XLA Ops:
  31.2 45.7 %all-gather.20.cloned.1.call-done = bf16[1024,1024]{1,0:T(8,128)(2,1)} async-done(((bf16[1024,256]{1,0:T(8,128)(2,1)}), bf16[1024,1024]{1,0:T(8,128)(2,1)}) %all-gather.20.cloned.1.call-update) | async-done | bytes 2097168 | tf_op jit(solution)/shard_map/all_gather | solution.py:115
  111.5 42.6 %reduce-scatter.18.cloned.1.call-done = bf16[1024,256]{1,0:T(8,128)(2,1)} async-done(((bf16[1024,1024]{1,0:T(8,128)(2,1)}), bf16[1024,256]{1,0:T(8,128)(2,1)}) %reduce-scatter.18.cloned.1.call-update) | async-done | bytes 524304 | tf_op jit(solution)/shard_map/reduce_scatter | solution.py:118
  203.0 72.0 %all-gather.46.cloned.1.call-done = bf16[1,1024,1024]{2,1,0:T(8,128)(2,1)} async-done(((bf16[1,256,1024]{2,1,0:T(8,128)(2,1)}), bf16[1,1024,1024]{2,1,0:T(8,128)(2,1)}) %all-gather.46.cloned.1.call-update) | async-done | bytes 2097168 | tf_op jit(solution)/shard_map/all_gather | solution.py:107
  290.0 33.6 %all-gather.48.cloned.1.call-done = bf16[1,1024,1024]{2,1,0:T(8,128)(2,1)} async-done(((bf16[1,256,1024]{2,1,0:T(8,128)(2,1)}), bf16[1,1024,1024]{2,1,0:T(8,128)(2,1)}) %all-gather.48.cloned.1.call-update) | async-done | bytes 2097168 | tf_op jit(solution)/shard_map/all_gather | solution.py:108
  340.5 52.1 %all_to_all.234 = bf16[1024,4,256]{2,0,1:T(8,128)(2,1)} all-to-all(bf16[1024,4,256]{2,0,1:T(8,128)(2,1)S(1)} %copy.154), channel_id=1, replica_groups=mesh['section'=2,'row'=4,'col'=4] {'row'}, dimensions={1} | all-to-all | bytes 4194304 | tf_op jit(solution)/shard_map/all_to_all | solution.py:132
  392.6 31.8 %reduce-scatter.20.cloned.1.call-done = bf16[1024,256]{1,0:T(8,128)(2,1)} async-done(((bf16[4096,256]{1,0:T(8,128)(2,1)}), bf16[1024,256]{1,0:T(8,128)(2,1)}) %reduce-scatter.20.cloned.1.call-update) | async-done | bytes 524304 | tf_op jit(solution)/shard_map/reduce_scatter | solution.py:137
  457.4 35.9 %all-gather.24.cloned.1.call-done = bf16[1024,1024]{1,0:T(8,128)(2,1)} async-done(((bf16[1024,256]{1,0:T(8,128)(2,1)}), bf16[1024,1024]{1,0:T(8,128)(2,1)}) %all-gather.24.cloned.1.call-update) | async-done | bytes 2097168 | tf_op jit(solution)/shard_map/all_gather | solution.py:115
  534.0 37.0 %reduce-scatter.22.cloned.1.call-done = bf16[1024,256]{1,0:T(8,128)(2,1)} async-done(((bf16[1024,1024]{1,0:T(8,128)(2,1)}), bf16[1024,256]{1,0:T(8,128)(2,1)}) %reduce-scatter.22.cloned.1.call-update) | async-done | bytes 524304 | tf_op jit(solution)/shard_map/reduce_scatter | solution.py:118
  621.5 40.6 %all-to-all-done.2 = bf16[4,1024,256]{1,2,0:T(8,128)(2,1)} async-done(((bf16[4,1024,256]{1,2,0:T(8,128)(2,1)}), bf16[4,1024,256]{1,2,0:T(8,128)(2,1)}, u32[]{:S(2)}, u32[]{:S(2)}) %all-to-all-start.2) | async-done | bytes 2097184 | tf_op jit(solution)/shard_map/all_to_all | solution.py:129
  686.3 53.9 %all_to_all.235 = bf16[1024,4,256]{2,0,1:T(8,128)(2,1)} all-to-all(bf16[1024,4,256]{2,0,1:T(8,128)(2,1)} %copy.159), channel_id=1, replica_groups=mesh['section'=2,'row'=4,'col'=4] {'row'}, dimensions={1} | all-to-all | bytes 4194304 | tf_op jit(solution)/shard_map/all_to_all | solution.py:132
  799.9 42.7 %all-gather.28.cloned.1.call-done = bf16[1024,1024]{1,0:T(8,128)(2,1)} async-done(((bf16[1024,256]{1,0:T(8,128)(2,1)}), bf16[1024,1024]{1,0:T(8,128)(2,1)}) %all-gather.28.cloned.1.call-update) | async-done | bytes 2097168 | tf_op jit(solution)/shard_map/all_gather | solution.py:115
  885.7 35.0 %reduce-scatter.26.cloned.1.call-done = bf16[1024,256]{1,0:T(8,128)(2,1)} async-done(((bf16[1024,1024]{1,0:T(8,128)(2,1)}), bf16[1024,256]{1,0:T(8,128)(2,1)}) %reduce-scatter.26.cloned.1.call-update) | async-done | bytes 524304 | tf_op jit(solution)/shard_map/reduce_scatter | solution.py:118
  972.7 40.6 %all-to-all-done.4 = bf16[4,1024,256]{1,2,0:T(8,128)(2,1)} async-done(((bf16[4,1024,256]{1,2,0:T(8,128)(2,1)}), bf16[4,1024,256]{1,2,0:T(8,128)(2,1)}, u32[]{:S(2)}, u32[]{:S(2)}) %all-to-all-start.4) | async-done | bytes 2097184 | tf_op jit(solution)/shard_map/all_to_all | solution.py:129
  1037.6 53.9 %all_to_all.236 = bf16[1024,4,256]{2,0,1:T(8,128)(2,1)} all-to-all(bf16[1024,4,256]{2,0,1:T(8,128)(2,1)} %copy.164), channel_id=1, replica_groups=mesh['section'=2,'row'=4,'col'=4] {'row'}, dimensions={1} | all-to-all | bytes 4194304 | tf_op jit(solution)/shard_map/all_to_all | solution.py:132
  1189.0 52.1 %all_to_all.237 = bf16[4,1024,256]{1,2,0:T(8,128)(2,1)S(1)} all-to-all(bf16[4,1024,256]{1,2,0:T(8,128)(2,1)} %copy.174), channel_id=1, replica_groups=mesh['section'=2,'row'=4,'col'=4] {'row'}, dimensions={0} | all-to-all | bytes 4194304 | tf_op jit(solution)/shard_map/all_to_all | solution.py:129
  1263.7 52.2 %all_to_all.238 = bf16[1024,4,256]{2,0,1:T(8,128)(2,1)} all-to-all(bf16[1024,4,256]{2,0,1:T(8,128)(2,1)} %copy.175), channel_id=1, replica_groups=mesh['section'=2,'row'=4,'col'=4] {'row'}, dimensions={1} | all-to-all | bytes 4194304 | tf_op jit(solution)/shard_map/all_to_all | solution.py:132
  1369.8 35.3 %all-gather.34.cloned.1.call-done = bf16[1024,1024]{1,0:T(8,128)(2,1)} async-done(((bf16[1024,256]{1,0:T(8,128)(2,1)}), bf16[1024,1024]{1,0:T(8,128)(2,1)}) %all-gather.34.cloned.1.call-update) | async-done | bytes 2097168 | tf_op jit(solution)/shard_map/all_gather | solution.py:115
  1450.7 42.6 %reduce-scatter.32.cloned.1.call-done = bf16[1024,256]{1,0:T(8,128)(2,1)} async-done(((bf16[1024,1024]{1,0:T(8,128)(2,1)}), bf16[1024,256]{1,0:T(8,128)(2,1)}) %reduce-scatter.32.cloned.1.call-update) | async-done | bytes 524304 | tf_op jit(solution)/shard_map/reduce_scatter | solution.py:118
  1552.5 52.1 %all_to_all.239 = bf16[4,1024,256]{1,2,0:T(8,128)(2,1)S(1)} all-to-all(bf16[4,1024,256]{1,2,0:T(8,128)(2,1)} %copy.191), channel_id=1, replica_groups=mesh['section'=2,'row'=4,'col'=4] {'row'}, dimensions={0} | all-to-all | bytes 4194304 | tf_op jit(solution)/shard_map/all_to_all | solution.py:129
  1627.2 52.2 %all_to_all.240 = bf16[1024,4,256]{2,0,1:T(8,128)(2,1)} all-to-all(bf16[1024,4,256]{2,0,1:T(8,128)(2,1)} %copy.192), channel_id=1, replica_groups=mesh['section'=2,'row'=4,'col'=4] {'row'}, dimensions={1} | all-to-all | bytes 4194304 | tf_op jit(solution)/shard_map/all_to_all | solution.py:132
  1726.4 42.1 %all-gather.38.cloned.1.call-done = bf16[1024,1024]{1,0:T(8,128)(2,1)} async-done(((bf16[1024,256]{1,0:T(8,128)(2,1)}), bf16[1024,1024]{1,0:T(8,128)(2,1)}) %all-gather.38.cloned.1.call-update) | async-done | bytes 2097168 | tf_op jit(solution)/shard_map/all_gather | solution.py:115
  1819.3 37.5 %reduce-scatter.36.cloned.1.call-done = bf16[1024,256]{1,0:T(8,128)(2,1)} async-done(((bf16[1024,1024]{1,0:T(8,128)(2,1)}), bf16[1024,256]{1,0:T(8,128)(2,1)}) %reduce-scatter.36.cloned.1.call-update) | async-done | bytes 524304 | tf_op jit(solution)/shard_map/reduce_scatter | solution.py:118
  1920.1 43.8 %all-to-all-done.10 = bf16[4,1024,256]{1,2,0:T(8,128)(2,1)} async-done(((bf16[4,1024,256]{1,2,0:T(8,128)(2,1)}), bf16[4,1024,256]{1,2,0:T(8,128)(2,1)}, u32[]{:S(2)}, u32[]{:S(2)}) %all-to-all-start.10) | async-done | bytes 2097184 | tf_op jit(solution)/shard_map/all_to_all | solution.py:129
  2239.9 72.9 %fusion = bf16[264,1024]{1,0:T(8,128)(2,1)S(1)} fusion(bf16[1028,1024]{1,0:T(8,128)(2,1)} %convert_element_type.731), kind=kCustom, calls=%all-reduce-scatter | all-reduce-scatter fusion | flops 1081345 | bytes 2646528
  (689 shorter events, 1229.9 us)
Async XLA Ops:
  12.4 141.7 %reduce-scatter.18.cloned.1.call-start = ((), (), s32[]{:S(2)}) async-start(), calls=%async_computation.28 | async-start | bytes 2621440 | tf_op jit(solution)/shard_map/reduce_scatter | solution.py:118
  169.6 105.4 %all-gather.46.cloned.1.call-start = ((), (), s32[]{:S(2)}) async-start(), calls=%async_computation.55 | async-start | bytes 2621440 | tf_op jit(solution)/shard_map/all_gather | solution.py:107
  200.8 122.8 %all-gather.48.cloned.1.call-start = ((), (), s32[]{:S(2)}) async-start(), calls=%async_computation.56 | async-start | bytes 2621440 | tf_op jit(solution)/shard_map/all_gather | solution.py:108
  203.0 221.5 %reduce-scatter.20.cloned.1.call-start = ((), (), s32[]{:S(2)}) async-start(), calls=%async_computation.30 | async-start | bytes 2621440 | tf_op jit(solution)/shard_map/reduce_scatter | solution.py:137
  392.6 100.8 %all-gather.24.cloned.1.call-start = ((), (), s32[]{:S(2)}) async-start(), calls=%async_computation.31 | async-start | bytes 2621440 | tf_op jit(solution)/shard_map/all_gather | solution.py:115
  449.7 121.3 %reduce-scatter.22.cloned.1.call-start = ((), (), s32[]{:S(2)}) async-start(), calls=%async_computation.32 | async-start | bytes 2621440 | tf_op jit(solution)/shard_map/reduce_scatter | solution.py:118
  616.7 154.5 %reduce-scatter.24.cloned.1.call-start = ((), (), s32[]{:S(2)}) async-start(), calls=%async_computation.34 | async-start | bytes 2621440 | tf_op jit(solution)/shard_map/reduce_scatter | solution.py:137
  740.2 102.4 %all-gather.28.cloned.1.call-start = ((), (), s32[]{:S(2)}) async-start(), calls=%async_computation.35 | async-start | bytes 2621440 | tf_op jit(solution)/shard_map/all_gather | solution.py:115
  799.0 121.7 %reduce-scatter.26.cloned.1.call-start = ((), (), s32[]{:S(2)}) async-start(), calls=%async_computation.36 | async-start | bytes 2621440 | tf_op jit(solution)/shard_map/reduce_scatter | solution.py:118
  967.9 154.6 %reduce-scatter.28.cloned.1.call-start = ((), (), s32[]{:S(2)}) async-start(), calls=%async_computation.38 | async-start | bytes 2621440 | tf_op jit(solution)/shard_map/reduce_scatter | solution.py:137
  1091.5 93.5 %all-gather.32.cloned.1.call-start = ((), (), s32[]{:S(2)}) async-start(), calls=%async_computation.39 | async-start | bytes 2621440 | tf_op jit(solution)/shard_map/all_gather | solution.py:126
  1164.1 182.8 %reduce-scatter.30.cloned.1.call-start = ((), (), s32[]{:S(2)}) async-start(), calls=%async_computation.40 | async-start | bytes 2621440 | tf_op jit(solution)/shard_map/reduce_scatter | solution.py:137
  1315.9 89.2 %all-gather.34.cloned.1.call-start = ((), (), s32[]{:S(2)}) async-start(), calls=%async_computation.41 | async-start | bytes 2621440 | tf_op jit(solution)/shard_map/all_gather | solution.py:115
  1361.4 132.0 %reduce-scatter.32.cloned.1.call-start = ((), (), s32[]{:S(2)}) async-start(), calls=%async_computation.42 | async-start | bytes 2621440 | tf_op jit(solution)/shard_map/reduce_scatter | solution.py:118
  1450.6 97.9 %all-gather.36.cloned.1.call-start = ((), (), s32[]{:S(2)}) async-start(), calls=%async_computation.43 | async-start | bytes 2621440 | tf_op jit(solution)/shard_map/all_gather | solution.py:126
  1526.2 184.2 %reduce-scatter.34.cloned.1.call-start = ((), (), s32[]{:S(2)}) async-start(), calls=%async_computation.44 | async-start | bytes 2621440 | tf_op jit(solution)/shard_map/reduce_scatter | solution.py:137
  1679.4 89.1 %all-gather.38.cloned.1.call-start = ((), (), s32[]{:S(2)}) async-start(), calls=%async_computation.45 | async-start | bytes 2621440 | tf_op jit(solution)/shard_map/all_gather | solution.py:115
  1724.7 132.1 %reduce-scatter.36.cloned.1.call-start = ((), (), s32[]{:S(2)}) async-start(), calls=%async_computation.46 | async-start | bytes 2621440 | tf_op jit(solution)/shard_map/reduce_scatter | solution.py:118
  1814.2 95.2 %all-gather.40.cloned.1.call-start = ((), (), s32[]{:S(2)}) async-start(), calls=%async_computation.47 | async-start | bytes 2621440 | tf_op jit(solution)/shard_map/all_gather | solution.py:126
  2039.2 93.5 %all-gather.42.cloned.1.call-start = ((), (), s32[]{:S(2)}) async-start(), calls=%async_computation.49 | async-start | bytes 2621440 | tf_op jit(solution)/shard_map/all_gather | solution.py:115
  2090.8 231.2 %reduce-scatter.46.cloned.1.call-start = ((), (), s32[]{:S(2)}) async-start(), calls=%async_computation.53 | async-start | bytes 2621440 | tf_op jit(solution)/shard_map/reduce_scatter | solution.py:365
  2105.7 225.8 %reduce-scatter.44.cloned.1.call-start = ((), (), s32[]{:S(2)}) async-start(), calls=%async_computation.52 | async-start | bytes 655360 | tf_op jit(solution)/shard_map/reduce_scatter | solution.py:351
  2180.8 152.3 %reduce-scatter.42.cloned.1.call-start = ((), (), s32[]{:S(2)}) async-start(), calls=%async_computation.51 | async-start | bytes 1966080 | tf_op jit(solution)/shard_map/reduce_scatter | solution.py:348
  2195.2 139.8 %reduce-scatter.40.cloned.1.call-start = ((), (), s32[]{:S(2)}) async-start(), calls=%async_computation.50 | async-start | bytes 2621440 | tf_op jit(solution)/shard_map/reduce_scatter | solution.py:118
  (165 other events, 4582.7 us)
Sparse Core Ops, SparseCore 0:
  33.3 43.5 all-gather.19
  111.5 42.5 reduce-scatter.17
  193.2 81.7 all-gather.45
  277.1 46.4 all-gather.47
  392.7 31.7 reduce-scatter.19
  449.8 43.4 all-gather.23
  527.4 43.5 reduce-scatter.21
  740.4 30.8 reduce-scatter.23
  799.1 43.4 all-gather.27
  878.1 42.5 reduce-scatter.25
  1091.7 30.8 reduce-scatter.27
  1316.0 30.8 reduce-scatter.29
  1361.5 43.6 all-gather.33
  1450.8 42.5 reduce-scatter.31
  1526.4 22.1 all-gather.35
  1679.6 30.8 reduce-scatter.33
  1724.9 43.6 all-gather.37
  1814.3 42.5 reduce-scatter.35
  2039.3 32.3 reduce-scatter.37
  2090.9 41.7 all-gather.41
  2135.0 42.5 reduce-scatter.45
  2180.9 22.6 reduce-scatter.43
  2206.3 28.1 reduce-scatter.41
  2236.7 72.6 reduce-scatter.39
  (6 shorter events, 129.6 us)
where the time goes:
time: 2360 us; the launch traced here: 2350 us
  waiting for transfers between devices  960 us (41%)
  blocking collectives  579 us (25%)
  matrix products  376 us (16%)
  local copies, waits for them, and re-layouts  209 us (9%)
  other arithmetic  170 us (7%)
  starting transfers between devices  36.5 us (2%)
    all_to_all x5, blocking collectives, width_back(): lax.all_to_all(term.astype(jnp.bfloat16), 'row', split_axis=1, concat_axi...  264 us
    all_gather x6, waiting for transfers between devices, wide_rows(): return lax.all_gather(part, 'row', axis=1, tiled=True)  229 us
    reduce_scatter x6, waiting for transfers between devices, head_total(): lax.psum_scatter(term.astype(jnp.bfloat16), 'row', scatter_dimension=1, t...  195 us
    all_gather x6, waiting for transfers between devices, col_tokens(): return lax.all_gather(part, 'col', axis=0, tiled=True)  131 us
    all_to_all x4, waiting for transfers between devices, token_block(): lax.all_to_all(rows_in, 'row', split_axis=0, concat_axis=1, tiled=True)  130 us
    psum x12, blocking collectives, row_pair(): return lax.psum((first, second), 'row')  125 us
    reduce_scatter x6, waiting for transfers between devices, col_total(): lax.psum_scatter(term.astype(jnp.bfloat16), 'col', scatter_dimension=0, t...  106 us
    all_to_all x2, blocking collectives, token_block(): lax.all_to_all(rows_in, 'row', split_axis=0, concat_axis=1, tiled=True)  104 us
  transfers between devices with their start and end apart: 40, of which 35 were waited for; matrix products, arithmetic and copies ran while one was open for 17% of the time, Pallas kernels for 0%

commit v1 on v0

v1 whole, which is shorter than its diff:
```python
import jax
import jax.numpy as jnp
from jax import lax
from jax.sharding import Mesh
from jax.sharding import PartitionSpec as P

HD = 64
EPSILON = 1e-05
NEG_BIG = -1e30
CORES = 2
PLANE = ("row", "high", "core")
F32 = jnp.float32
BF16 = jnp.bfloat16


def gelu_exact(values):
    return jax.nn.gelu(values, approximate=False)


def dot(pattern, left, right):
    return jnp.einsum(pattern, left, right, preferred_element_type=F32)


class Layout:
    def __init__(self, tokens_in, doc_ids):
        self.micro, self.narrow, _ = tokens_in.shape
        self.seq_here, self.seq_len = doc_ids.shape[1:]
        self.rows = lax.axis_size("row")
        self.highs = lax.axis_size("high")
        self.cols = self.highs * CORES
        self.width = self.narrow * self.rows
        self.places = self.rows * CORES
        self.sequences = self.micro * self.seq_here * CORES
        self.group = self.places // self.sequences
        self.part = self.seq_len // self.group
        place = lax.axis_index("row") * CORES + lax.axis_index("core")
        self.row = lax.axis_index("row")
        self.sequence = place // self.group
        self.position = place % self.group
        self.block = (self.sequence // CORES) * self.group + self.position

    def routes(self, shift):
        pairs = []
        for source in range(self.places):
            row, core = divmod(source, CORES)
            block = (row + shift) % self.rows
            sequence = (block // self.group) * CORES + core
            pairs.append((source, sequence * self.group + block % self.group))
        return pairs

    def to_tokens(self, array):
        blocks = array.reshape(self.micro, self.narrow, self.seq_here * self.group, self.part)
        blocks = blocks.transpose(0, 2, 1, 3).reshape(self.rows, self.narrow, self.part)
        got = []
        for shift in range(self.rows):
            block = lax.dynamic_index_in_dim(blocks, (self.row + shift) % self.rows, 0, False)
            got.append(lax.ppermute(block, ("row", "core"), self.routes(shift)))
        order = (self.block - jnp.arange(self.rows)) % self.rows
        whole = jnp.take(jnp.stack(got), order, axis=0)
        return whole.reshape(self.width, self.part).T

    def to_features(self, array):
        blocks = array.T.reshape(self.rows, self.narrow, self.part)
        got = []
        for shift in range(self.rows):
            block = lax.dynamic_index_in_dim(blocks, (self.block - shift) % self.rows, 0, False)
            pairs = [(there, here) for here, there in self.routes(shift)]
            got.append(lax.ppermute(block, ("row", "core"), pairs))
        order = (jnp.arange(self.rows) - self.row) % self.rows
        whole = jnp.take(jnp.stack(got), order, axis=0)
        whole = whole.reshape(self.micro, self.seq_here * self.group, self.narrow, self.part)
        return whole.transpose(0, 2, 1, 3).reshape(self.micro, self.narrow, self.seq_here * self.seq_len)

    def within(self, step):
        return [
            (place, place // self.group * self.group + (place + step) % self.group)
            for place in range(self.places)
        ]

    def share(self, array):
        return [array] + [
            lax.ppermute(array, ("row", "core"), self.within(step)) for step in range(1, self.group)
        ]

    def give_back(self, blocks):
        total = blocks[0].astype(F32)
        for step in range(1, self.group):
            total += lax.ppermute(
                blocks[step].astype(BF16), ("row", "core"), self.within(self.group - step)
            ).astype(F32)
        return total

    def documents(self, doc_ids):
        other = lax.ppermute(doc_ids, "core", [(i, (i + 1) % CORES) for i in range(CORES)])
        here = lax.axis_index("core")
        pair = jnp.stack([jnp.where(here == c, doc_ids, other) for c in range(CORES)], axis=2)
        rows = pair.reshape(self.sequences, self.group, self.part)
        mine = lax.dynamic_index_in_dim(rows, self.sequence, 0, False)
        order = (self.position - jnp.arange(self.group)) % self.group
        ordered = jnp.take(mine, order, axis=0)
        return ordered[0], ordered.reshape(-1)


def attend(query, key, value, doc_query, doc_key):
    same = (doc_query[:, None] == doc_key[None, :])[None]
    scores = jnp.where(same, dot("qhj,khj->hqk", query, key), NEG_BIG)
    row_max = jnp.max(scores, axis=2, keepdims=True)
    expo = jnp.exp(scores - row_max)
    row_total = jnp.sum(expo, axis=2, keepdims=True)
    prob = (expo / row_total).astype(BF16)
    return dot("hqk,khj->qhj", prob, value), row_max + jnp.log(row_total)


def attend_back(query, key, value, grad_mixed, log_total, doc_query, doc_key):
    same = (doc_query[:, None] == doc_key[None, :])[None]
    scores = jnp.where(same, dot("qhj,khj->hqk", query, key), NEG_BIG)
    prob = jnp.where(same, jnp.exp(scores - log_total), 0.0)
    grad_value = dot("hqk,qhj->khj", prob.astype(BF16), grad_mixed)
    grad_prob = dot("qhj,khj->hqk", grad_mixed, value)
    inner = jnp.sum(prob * grad_prob, axis=2, keepdims=True)
    grad_scores = (prob * (grad_prob - inner)).astype(BF16)
    grad_query = dot("hqk,khj->qhj", grad_scores, key)
    grad_key = dot("hqk,qhj->khj", grad_scores, query)
    return grad_query, grad_key, grad_value


def norm_forward(hidden, gain, bias):
    center = hidden - jnp.mean(hidden, axis=1, keepdims=True)
    scale = lax.rsqrt(jnp.mean(center * center, axis=1, keepdims=True) + EPSILON)
    normed = center * scale
    return normed * gain + bias, normed, scale


def norm_backward(grad_out, normed, scale, gain):
    scaled = grad_out * gain
    first = jnp.mean(scaled, axis=1, keepdims=True)
    second = jnp.mean(scaled * normed, axis=1, keepdims=True)
    return scale * (scaled - first - normed * second)


def local(tokens_in, doc_ids, cotangent, qkv_master, out_master, unit_master, down_master, unit_bias, width_bias, norm_gain):
    at = Layout(tokens_in, doc_ids)
    section = lax.axis_index("section")
    rows, cols, width = at.rows, at.cols, at.width
    units = unit_master.shape[2] * cols
    heads = width // HD
    head_scale = HD**-0.5

    def gathered(weight):
        whole = lax.all_gather(weight.astype(BF16), PLANE, axis=0)
        return whole.reshape((rows, cols) + weight.shape)

    def square(weight):
        whole = gathered(weight)
        return whole.transpose(0, 2, 1, 3).reshape(width, -1)

    qkv_bf = gathered(qkv_master[0]).transpose(2, 0, 3, 1, 4).reshape(3, width, width)
    out_bf = square(out_master[0])
    unit_bf = square(unit_master[0])
    down_bf = square(down_master[0])
    unit_shift = lax.all_gather(unit_bias[0], ("high", "core"), axis=0, tiled=True)
    small = lax.all_gather(jnp.concatenate([width_bias[0], norm_gain[0]]), "row", axis=1, tiled=True)
    bias, gain = small[:6], small[6:]

    first_in = at.to_tokens(tokens_in)
    last_grad = at.to_tokens(cotangent)
    doc_query, doc_key = at.documents(doc_ids)

    def by_head(array):
        return array.reshape(array.shape[0], heads, HD)

    def forward(layer_in):
        projected = dot("td,ked->kte", layer_in, qkv_bf)
        query = ((projected[0] + bias[0]) * head_scale).astype(BF16)
        key = jnp.concatenate(at.share(projected[1].astype(BF16)))
        value = jnp.concatenate(at.share((projected[2] + bias[1]).astype(BF16)))
        mixed, log_total = attend(by_head(query), by_head(key), by_head(value), doc_query, doc_key)
        mixed = mixed.reshape(-1, width).astype(BF16)
        attn = dot("th,hd->td", mixed, out_bf) + bias[2]
        x1, hat_one, scale_one = norm_forward(layer_in.astype(F32) + attn, gain[0], bias[3])
        x1_bf = x1.astype(BF16)
        pre = dot("td,df->tf", x1_bf, unit_bf) + unit_shift
        act = gelu_exact(pre).astype(BF16)
        down = dot("tf,df->td", act, down_bf) + bias[4]
        y, hat_two, scale_two = norm_forward(x1 + down, gain[1], bias[5])
        saved = (layer_in, query, key, value, mixed, log_total, x1_bf, hat_one, scale_one, pre, hat_two, scale_two)
        return y, saved

    def backward(dy, saved, weights_too):
        layer_in, query, key, value, mixed, log_total, x1_bf, hat_one, scale_one, pre, hat_two, scale_two = saved
        dh2 = norm_backward(dy, hat_two, scale_two, gain[1])
        ddown = dh2.astype(BF16)
        act, pull = jax.vjp(gelu_exact, pre)
        dact = dot("td,df->tf", ddown, down_bf)
        dpre = pull(dact)[0].astype(BF16)
        dx1 = dh2 + dot("tf,df->td", dpre, unit_bf)
        dh1 = norm_backward(dx1, hat_one, scale_one, gain[0])
        dattn = dh1.astype(BF16)
        dmixed = dot("td,hd->th", dattn, out_bf).astype(BF16)
        dquery, dkey, dvalue = attend_back(
            by_head(query), by_head(key), by_head(value), by_head(dmixed), log_total, doc_query, doc_key
        )
        dquery = dquery.reshape(-1, width).astype(BF16) * head_scale
        dkey = at.give_back(jnp.split(dkey.reshape(-1, width), at.group)).astype(BF16)
        dvalue = at.give_back(jnp.split(dvalue.reshape(-1, width), at.group)).astype(BF16)
        dproj = jnp.stack([dquery, dkey, dvalue])
        dx = dh1 + dot("kte,ked->td", dproj, qkv_bf)
        if not weights_too:
            return dx, None
        sums = jnp.stack(
            [
                jnp.sum(dquery.astype(F32), axis=0),
                jnp.sum(dvalue.astype(F32), axis=0),
                jnp.sum(dattn.astype(F32), axis=0),
                jnp.sum(dx1, axis=0),
                jnp.sum(ddown.astype(F32), axis=0),
                jnp.sum(dy, axis=0),
                jnp.sum(dx1 * hat_one, axis=0),
                jnp.sum(dy * hat_two, axis=0),
            ]
        )
        grads = (
            dot("kte,td->ked", dproj, layer_in),
            dot("th,td->hd", mixed, dattn),
            dot("td,tf->df", x1_bf, dpre),
            dot("td,tf->df", ddown, act.astype(BF16)),
            jnp.sum(dpre.astype(F32), axis=0),
            sums,
        )
        return dx, grads

    def scattered(grad):
        blocks = grad.astype(BF16).reshape(rows, grad.shape[0] // rows, cols, grad.shape[1] // cols)
        blocks = blocks.transpose(0, 2, 1, 3).reshape(rows * cols, grad.shape[0] // rows, grad.shape[1] // cols)
        return lax.psum_scatter(blocks, PLANE, scatter_dimension=0, tiled=True)[0].astype(F32)

    early, _ = forward(first_in)
    passed = lax.ppermute(early.astype(BF16), "section", [(0, 1)])
    layer_out, saved = forward(jnp.where(section == 0, first_in, passed))
    early_grad, _ = backward(last_grad.astype(F32), saved, False)
    passed = lax.ppermute(early_grad.astype(BF16), "section", [(1, 0)])
    dy = jnp.where(section == 0, passed, last_grad).astype(F32)
    input_grad, (qkv_grad, out_grad, unit_grad, down_grad, pre_sum, sums) = backward(dy, saved, True)

    qkv_blocks = qkv_grad.astype(BF16).reshape(3, rows, width // rows, cols, width // cols)
    qkv_blocks = qkv_blocks.transpose(1, 3, 0, 2, 4).reshape((rows * cols, 3, width // rows, width // cols))
    qkv_sum = lax.psum_scatter(qkv_blocks, PLANE, scatter_dimension=0, tiled=True)[0].astype(F32)
    out_sum, unit_sum, down_sum = scattered(out_grad), scattered(unit_grad), scattered(down_grad)
    pre_sum, sums = lax.psum((pre_sum, sums), PLANE)
    here = lax.axis_index("high") * CORES + lax.axis_index("core")
    pre_sum = lax.dynamic_slice_in_dim(pre_sum, here * (units // cols), units // cols)
    sums = lax.dynamic_slice_in_dim(sums, at.row * at.narrow, at.narrow, axis=1)
    layer_out = at.to_features(layer_out.astype(BF16)).astype(F32)
    input_grad = at.to_features(input_grad.astype(BF16)).astype(F32)
    return (
        layer_out[None],
        input_grad[None],
        qkv_sum[None],
        out_sum[None],
        unit_sum[None],
        down_sum[None],
        pre_sum[None],
        sums[:6][None],
        sums[6:][None],
    )


def solution(mesh):
    sections, rows, cols = (mesh.shape[name] for name in ("section", "row", "col"))
    fine = Mesh(
        mesh.devices.reshape(sections, rows, cols // CORES, CORES), ("section", "row", "high", "core")
    )
    col = ("high", "core")
    block = P("section", "row", col)
    stream = P("section", None, "row", col)
    return jax.shard_map(
        local,
        mesh=fine,
        in_specs=(
            P(None, "row", col),
            P(None, col, None),
            P(None, "row", col),
            P("section", None, "row", col),
            block,
            block,
            block,
            P("section", col),
            P("section", None, "row"),
            P("section", None, "row"),
        ),
        out_specs=(
            stream,
            stream,
            stream,
            block,
            block,
            block,
            P("section", col),
            P("section", None, "row"),
            P("section", None, "row"),
        ),
        check_vma=False,
    )
```

time: 2360 us -> 1210 us (0.51)
  waiting for transfers between devices: 960 us -> 255 us
  blocking collectives: 579 us -> 98 us
  local copies, waits for them, and re-layouts: 209 us -> 251 us
    all_gather x15 -> x4, waiting for transfers between devices: 475 us -> 29.6 us  [gathered(): whole = lax.all_gather(weight.astype(BF16), PLANE, axis=0)]
    all_to_all x7 -> x0, blocking collectives: 368 us -> none  [the longest x5 264 us: width_back(): lax.all_to_all(term.astype(jnp.bfloat16), 'row', split_axis=1, concat_axi...]
    reduce_scatter x15 -> x4, waiting for transfers between devices: 301 us -> 121 us  [the longest x3 121 us: scattered(): lax.psum_scatter(blocks, PLANE, scatter_dimension=0, tiled=True)[0]]
    all_to_all x5 -> x0, waiting for transfers between devices: 137 us -> none  [the longest x4 130 us: token_block(): lax.all_to_all(rows_in, 'row', split_axis=0, concat_axis=1, tiled=True)]
    reshape x0 -> x14, local copies, waits for them, and re-layouts: none -> 97.5 us  [the longest x4 38.2 us: gathered(): return whole.reshape((rows, cols) + weight.shape)]
    psum x13 -> x1, blocking collectives: 130 us -> 54.1 us  [local(): pre_sum, sums = lax.psum((pre_sum, sums), PLANE)]
    unnamed x1 -> x0, blocking collectives: 72.9 us -> none
    dynamic_slice x36 -> x1, local copies, waits for them, and re-layouts: 62.5 us -> 0.59 us  [local(): lax.dynamic_slice_in_dim(pre_sum, here * (units // cols), units // cols)]
  transfers between devices with their start and end apart: 40 -> 35, of which waited for: 35 -> 10; matrix products, arithmetic and copies ran while one was open for 17% -> 39% of each run, Pallas kernels for 0% -> 0%
where the time goes in v1:
time: 1210 us; the launch traced here: 1200 us
  matrix products  375 us (31%)
  waiting for transfers between devices  255 us (21%)
  local copies, waits for them, and re-layouts  251 us (21%)
  other arithmetic  175 us (14%)
  blocking collectives  98 us (8%)
  starting transfers between devices  29.9 us (2%)
  between operations  15.8 us (1%)
    dot_general x30, matrix products, dot(): return jnp.einsum(pattern, left, right, preferred_element_type=F32)  375 us
    reduce_scatter x3, waiting for transfers between devices, scattered(): lax.psum_scatter(blocks, PLANE, scatter_dimension=0, tiled=True)[0]  121 us
    convert_element_type x2, other arithmetic, attend_back(): grad_scores = (prob * (grad_prob - inner)).astype(BF16)  56.8 us
    psum x1, blocking collectives, local(): pre_sum, sums = lax.psum((pre_sum, sums), PLANE)  54.1 us
    unnamed x147, local copies, waits for them, and re-layouts  44.2 us
    sub x1, other arithmetic, attend(): expo = jnp.exp(scores - row_max)  39.7 us
    reshape x4, local copies, waits for them, and re-layouts, gathered(): return whole.reshape((rows, cols) + weight.shape)  38.2 us
    all_gather x1, blocking collectives, local(): lax.all_gather(jnp.concatenate([width_bias[0], norm_gain[0]]), 'row', axi...  37 us
  transfers between devices with their start and end apart: 35, of which 10 were waited for; matrix products, arithmetic and copies ran while one was open for 39% of the time, Pallas kernels for 0%

profile of v1, /device:TPU:10, one launch (start us, length us, event | category | flops | bytes accessed | tf_op | source)
XLA Modules:
  0.0 1200.3 jit_solution(13899123804457080315)
XLA Ops:
  26.2 37.0 %all_gather.23 = f32[8,1024]{1,0:T(8,128)S(1)} all-gather(f32[8,256]{1,0:T(8,128)S(1)} %pad_maximum_fusion.13), channel_id=1, replica_groups=mesh['section'=2,'row'=4,'high'=2,'core'=2] {'row'}, dimensions={1}, use_global_device_ids=true | all-gather | bytes 40960 | tf_op jit(solution)/shard_map/all_gather | solution.py:162
  74.3 21.2 %collective-permute-done.15 = bf16[256,512]{1,0:T(8,128)(2,1)} collective-permute-done((bf16[256,512]{1,0:T(8,128)(2,1)S(1)}, bf16[256,512]{1,0:T(8,128)(2,1)}, u32[]{:S(2)}, u32[]{:S(2)}) %collective-permute-start.15) | collective-permute-done | bytes 262176 | tf_op jit(solution)/shard_map/ppermute | solution.py:57
  176.6 19.0 %fusion.100 = f32[16,512,1024]{2,1,0:T(8,128)} fusion(bf16[1024,16,64]{0,2,1:T(8,128)(2,1)} %bitcast.296, f32[512,16,64]{0,2,1:T(8,128)} %bitcast.295, f32[16,64]{1,0:T(8,128)S(1)} %add.377), kind=kOutput, calls=%fused_computation.197 | convolution fusion | flops 1075314688 | bytes 37752832 | tf_op jit(solution)/shard_map/qhj,khj->hqk/dot_general | solution.py:21
  195.6 39.7 %fusion.186 = (f32[16,512]{1,0:T(8,128)S(1)}, f32[16,512,1024]{2,1,0:T(8,128)}) fusion(f32[16,512,1024]{2,1,0:T(8,128)} %fusion.100, pred[512,1024]{1,0:T(8,128)(4,1)S(1)} %broadcast_compare_fusion), kind=kOutput, calls=%fused_computation.351 | output fusion | flops 33555456 | bytes 67665920 | tf_op jit(solution)/shard_map/sub | solution.py:108
  235.3 15.5 %fusion.96 = bf16[16,64,512]{2,1,0:T(8,128)(2,1)} fusion(bf16[1024,16,64]{0,2,1:T(8,128)(2,1)} %bitcast.342, f32[16,512,1024]{2,1,0:T(8,128)} %get-tuple-element.87, f32[16,512]{1,0:T(8,128)S(1)} %get-tuple-element.86), kind=kOutput, calls=%fused_computation.193 | convolution fusion | flops 1091043328 | bytes 36732928 | tf_op jit(solution)/shard_map/hqk,khj->qhj/dot_general | solution.py:21
  280.2 23.8 %all-gather.12.cloned.1.call-done = bf16[16,256,1024]{2,1,0:T(8,128)(2,1)} async-done(((bf16[1,256,1024]{2,1,0:T(8,128)(2,1)}), bf16[16,256,1024]{2,1,0:T(8,128)(2,1)}) %all-gather.12.cloned.1.call-update) | async-done | bytes 8388624 | tf_op jit(solution)/shard_map/all_gather | solution.py:150
  328.3 33.8 %fusion.188 = (f32[512]{0:T(512)S(1)}, f32[512,1024]{1,0:T(8,128)}) fusion(f32[1024]{0:T(1024)S(1)} %bitcast.383, bf16[1024,4096]{1,0:T(8,128)(2,1)} %bitcast.305, bf16[1024,4096]{1,0:T(8,128)(2,1)} %bitcast.299, f32[4096]{0:T(1024)S(1)} %bitcast.371, f32[512,1024]{1,0:T(8,128)} %copy-done.16, f32[1024]{0:T(1024)S(1)} %bitcast.377, ...), kind=kOutput, calls=%fused_computation.353 | convolution fusion | flops 8734638080 | bytes 21006336 | tf_op jit(solution)/shard_map/tf,df->td/dot_general | solution.py:21
  367.4 26.0 %collective-permute-done.7 = bf16[512,1024]{1,0:T(8,128)(2,1)} collective-permute-done((bf16[512,1024]{1,0:T(8,128)(2,1)S(1)}, bf16[512,1024]{1,0:T(8,128)(2,1)}, u32[]{:S(2)}, u32[]{:S(2)}) %collective-permute-start.7) | collective-permute-done | bytes 1048608 | tf_op jit(solution)/shard_map/ppermute | solution.py:238
  421.5 15.5 %select_reduce_fusion.1 = (f32[16,512]{1,0:T(8,128)S(1)}, f32[16,512,1024]{2,1,0:T(8,128)}) fusion(pred[512,1024]{1,0:T(8,128)(4,1)S(1)} %broadcast_compare_fusion, bf16[512,16,64]{0,2,1:T(8,128)(2,1)} %multiply_convert_fusion.3, bf16[1024,16,64]{0,2,1:T(8,128)(2,1)S(1)} %bitcast.285), kind=kOutput, calls=%fused_computation.18 | convolution fusion | flops 1090510848 | bytes 37257216 | tf_op jit(solution)/shard_map/qhj,khj->hqk/dot_general | solution.py:21
  473.8 28.5 %multiply_convert_fusion.2 = (bf16[512,4096]{1,0:T(8,128)(2,1)}, f32[512,4096]{1,0:T(8,128)}, f32[512,4096]{1,0:T(8,128)}) fusion(f32[4096]{0:T(1024)S(1)} %bitcast.372, bf16[1024,4096]{1,0:T(8,128)(2,1)} %bitcast.300, f32[1024]{0:T(1024)S(1)} %bitcast.378, f32[1024]{0:T(1024)S(1)} %bitcast.360, f32[512]{0:T(512)S(1)} %add_rsqrt_fusion.1, ...), kind=kOutput, calls=%fused_computation.36 | convolution fusion | flops 4436000768 | bytes 31485952 | tf_op jit(solution)/shard_map/td,df->tf/dot_general | solution.py:21
  511.3 26.1 %fusion.180 = (f32[512]{0:T(512)S(1)}, f32[512]{0:T(512)S(1)}, f32[512,1024]{1,0:T(8,128)}) fusion(f32[512]{0:T(512)S(1)} %add_rsqrt_fusion.1, f32[512,1024]{1,0:T(8,128)} %copy-done.5, f32[512]{0:T(512)S(1)} %broadcast_multiply_fusion.9, f32[1024]{0:T(1024)S(1)} %bitcast.362, bf16[1024,4096]{1,0:T(8,128)(2,1)} %bitcast.301, ...), kind=kOutput, calls=%fused_computation.347 | convolution fusion | flops 8633974784 | bytes 40935424 | tf_op jit(solution)/shard_map/tf,df->td/dot_general | solution.py:21
  545.0 25.8 %multiply_reduce_fusion.1 = (f32[16,512]{1,0:T(8,128)S(1)}, f32[16,512,1024]{2,1,0:T(8,128)}) fusion(f32[16,512]{1,0:T(8,128)S(1)} %copy-done.25, f32[16,512,1024]{2,1,0:T(8,128)} %get-tuple-element.93, pred[512,1024]{1,0:T(8,128)(4,1)S(1)} %broadcast_compare_fusion, bf16[512,16,64]{0,2,1:T(8,128)(2,1)} %bitcast.321, bf16[1024,16,64]{0,2,1:T(8,128)(2,1)S(1)} %bitcast.277), kind=kOutput, calls=%fused_computation.9 | convolution fusion | flops 1115676672 | bytes 70844416 | tf_op jit(solution)/shard_map/qhj,khj->hqk/dot_general | solution.py:21
  570.8 27.9 %multiply_convert_fusion.1 = bf16[16,512,1024]{2,1,0:T(8,128)(2,1)} fusion(f32[16,512,1024]{2,1,0:T(8,128)} %get-tuple-element.101, f32[16,512]{1,0:T(8,128)S(1)} %get-tuple-element.100, f32[16,512]{1,0:T(8,128)S(1)} %copy-done.25, f32[16,512,1024]{2,1,0:T(8,128)} %get-tuple-element.93, pred[512,1024]{1,0:T(8,128)(4,1)S(1)} %broadcast_compare_fusion), kind=kLoop, calls=%fused_computation.8 | loop fusion | flops 50331648 | bytes 84475904 | tf_op jit(solution)/shard_map/convert_element_type | solution.py:121
  613.3 17.0 %fusion.72 = f32[1024,16,64]{0,2,1:T(8,128)} fusion(bf16[512,16,64]{0,2,1:T(8,128)(2,1)} %bitcast.322, f32[16,512,1024]{2,1,0:T(8,128)} %get-tuple-element.93, f32[16,512]{1,0:T(8,128)S(1)} %copy-done.25, pred[512,1024]{1,0:T(8,128)(4,1)S(1)} %broadcast_compare_fusion), kind=kOutput, calls=%fused_computation.119 | convolution fusion | flops 1107296256 | bytes 39354368 | tf_op jit(solution)/shard_map/hqk,qhj->khj/dot_general | solution.py:21
  675.9 22.8 %collective-permute-done.20 = bf16[512,1024]{1,0:T(8,128)(2,1)S(1)} collective-permute-done((bf16[512,1024]{1,0:T(8,128)(2,1)S(1)}, bf16[512,1024]{1,0:T(8,128)(2,1)S(1)}, u32[]{:S(2)}, u32[]{:S(2)}) %collective-permute-start.20) | collective-permute-done | bytes 1048608 | tf_op jit(solution)/shard_map/ppermute | solution.py:241
  702.9 15.8 %convert_reduce_fusion = (f32[4096]{0:T(1024)}, bf16[512,4096]{1,0:T(8,128)(2,1)}) fusion(f32[512,4096]{1,0:T(8,128)} %get-tuple-element.48, bf16[1024,4096]{1,0:T(8,128)(2,1)} %bitcast.307, f32[512,1024]{1,0:T(8,128)S(1)} %get-tuple-element.43, f32[512,4096]{1,0:T(8,128)} %get-tuple-element.96, f32[4096]{0:T(1024)S(1)} %bitcast.374), kind=kOutput, calls=%fused_computation.29 | convolution fusion | flops 4331139072 | bytes 31490048 | tf_op jit(solution)/shard_map/td,df->tf/dot_general | solution.py:21
  733.6 25.9 %multiply_reduce_fusion = (f32[16,512]{1,0:T(8,128)S(1)}, f32[16,512,1024]{2,1,0:T(8,128)}) fusion(f32[16,512]{1,0:T(8,128)S(1)} %copy-done.25, f32[16,512,1024]{2,1,0:T(8,128)} %get-tuple-element.93, pred[512,1024]{1,0:T(8,128)(4,1)S(1)} %broadcast_compare_fusion, bf16[512,16,64]{0,2,1:T(8,128)(2,1)} %bitcast.323, bf16[1024,16,64]{0,2,1:T(8,128)(2,1)S(1)} %bitcast.278), kind=kOutput, calls=%fused_computation.7 | convolution fusion | flops 1115676672 | bytes 70844416 | tf_op jit(solution)/shard_map/qhj,khj->hqk/dot_general | solution.py:21
  759.5 16.5 %fusion.75 = f32[1024,16,64]{0,2,1:T(8,128)} fusion(bf16[512,16,64]{0,2,1:T(8,128)(2,1)S(1)} %bitcast.324, f32[16,512,1024]{2,1,0:T(8,128)} %get-tuple-element.93, f32[16,512]{1,0:T(8,128)S(1)} %copy-done.25, pred[512,1024]{1,0:T(8,128)(4,1)S(1)} %broadcast_compare_fusion), kind=kOutput, calls=%fused_computation.120 | convolution fusion | flops 1107296256 | bytes 39354368 | tf_op jit(solution)/shard_map/hqk,qhj->khj/dot_general | solution.py:21
  788.1 28.9 %multiply_convert_fusion = bf16[16,512,1024]{2,1,0:T(8,128)(2,1)} fusion(f32[16,512,1024]{2,1,0:T(8,128)} %get-tuple-element.104, f32[16,512]{1,0:T(8,128)S(1)} %get-tuple-element.103, f32[16,512]{1,0:T(8,128)S(1)} %copy-done.25, f32[16,512,1024]{2,1,0:T(8,128)} %get-tuple-element.93, pred[512,1024]{1,0:T(8,128)(4,1)S(1)} %broadcast_compare_fusion), kind=kLoop, calls=%fused_computation.6 | loop fusion | flops 50331648 | bytes 84475904 | tf_op jit(solution)/shard_map/convert_element_type | solution.py:121
  888.8 14.9 %reshape.440 = bf16[4,256,4,1024]{3,2,1,0:T(4,128)(2,1)} reshape(bf16[1024,4096]{1,0:T(8,128)(2,1)} %convolution_convert_fusion) | data formatting | bytes 16777216 | tf_op jit(solution)/shard_map/reshape | solution.py:233
  976.9 16.8 %collective-permute-done.12 = bf16[256,512]{1,0:T(8,128)(2,1)} collective-permute-done((bf16[256,512]{1,0:T(8,128)(2,1)}, bf16[256,512]{1,0:T(8,128)(2,1)}, u32[]{:S(2)}, u32[]{:S(2)}) %collective-permute-start.12) | collective-permute-done | bytes 262176 | tf_op jit(solution)/shard_map/ppermute | solution.py:68
  995.9 54.1 %all-reduce = (f32[4096]{0:T(1024)S(1)}, f32[8,1024]{1,0:T(8,128)S(1)}) all-reduce(f32[4096]{0:T(1024)S(1)} %copy-done.52, f32[8,1024]{1,0:T(8,128)S(1)} %stack.153), channel_id=1, replica_groups=mesh['section'=2,'row'=4,'high'=2,'core'=2] {'row','high','core'}, use_global_device_ids=true, to_apply=%region_27.29 | all-reduce | flops 12288 | bytes 98304 | tf_op jit(solution)/shard_map/psum | solution.py:249
  1067.8 15.0 %reduce-scatter.11.cloned.1.call-done = bf16[1,256,1024]{2,1,0:T(8,128)(2,1)} async-done(((bf16[16,256,1024]{2,1,0:T(8,128)(2,1)}), bf16[1,256,1024]{2,1,0:T(8,128)(2,1)}) %reduce-scatter.11.cloned.1.call-update) | async-done | bytes 524304 | tf_op jit(solution)/shard_map/reduce_scatter | solution.py:235
  1084.9 106.3 %reduce-scatter.9.cloned.1.call-done = bf16[1,256,1024]{2,1,0:T(8,128)(2,1)} async-done(((bf16[16,256,1024]{2,1,0:T(8,128)(2,1)}), bf16[1,256,1024]{2,1,0:T(8,128)(2,1)}) %reduce-scatter.9.cloned.1.call-update) | async-done | bytes 524304 | tf_op jit(solution)/shard_map/reduce_scatter | solution.py:235
  (381 shorter events, 510.8 us)
Async XLA Ops:
  7.2 102.6 %all-gather.6.cloned.1.call-start = ((), (), s32[]{:S(2)}) async-start(), calls=%async_computation.4 | async-start | bytes 6684672 | tf_op jit(solution)/shard_map/all_gather | solution.py:150
  9.3 142.6 %all-gather.8.cloned.1.call-start = ((), (), s32[]{:S(2)}) async-start(), calls=%async_computation.5 | async-start | bytes 2228224 | tf_op jit(solution)/shard_map/all_gather | solution.py:150
  11.0 244.4 %all-gather.10.cloned.1.call-start = ((), (), s32[]{:S(2)}) async-start(), calls=%async_computation.6 | async-start | bytes 8912896 | tf_op jit(solution)/shard_map/all_gather | solution.py:150
  13.2 290.7 %all-gather.12.cloned.1.call-start = ((), (), s32[]{:S(2)}) async-start(), calls=%async_computation.7 | async-start | bytes 8912896 | tf_op jit(solution)/shard_map/all_gather | solution.py:150
  15.4 1048.8 %reduce-scatter.7.cloned.1.call-start = ((), (), s32[]{:S(2)}) async-start(), calls=%async_computation.9 | async-start | bytes 2228224 | tf_op jit(solution)/shard_map/reduce_scatter | solution.py:235
  15.8 48.6 %collective-permute-start = (bf16[256,512]{1,0:T(8,128)(2,1)S(1)}, bf16[256,512]{1,0:T(8,128)(2,1)S(1)}, u32[]{:S(2)}, u32[]{:S(2)}) collective-permute-start(bf16[256,512]{1,0:T(8,128)(2,1)S(1)} %get-tuple-element.66), channel_id=1, source_target_pairs={{0,0},{1,4},{4,1},{5,5},{8,8},{9,12},{12,9},{13,13},{2,2},{3,6},{6... | collective-permute-start | bytes 786440 | tf_op jit(solution)/shard_map/ppermute | solution.py:57
  17.7 46.8 %collective-permute-start.1 = (bf16[256,512]{1,0:T(8,128)(2,1)S(1)}, bf16[256,512]{1,0:T(8,128)(2,1)}, u32[]{:S(2)}, u32[]{:S(2)}) collective-permute-start(bf16[256,512]{1,0:T(8,128)(2,1)S(1)} %get-tuple-element.69), channel_id=1, source_target_pairs={{0,1},{1,5},{4,8},{5,12},{8,9},{9,13},{12,0},{13,4},{2,3},{3,7},{6... | collective-permute-start | bytes 786440 | tf_op jit(solution)/shard_map/ppermute | solution.py:57
  18.1 46.5 %collective-permute-start.2 = (bf16[256,512]{1,0:T(8,128)(2,1)S(1)}, bf16[256,512]{1,0:T(8,128)(2,1)}, u32[]{:S(2)}, u32[]{:S(2)}) collective-permute-start(bf16[256,512]{1,0:T(8,128)(2,1)S(1)} %get-tuple-element.68), channel_id=1, source_target_pairs={{0,8},{1,12},{4,9},{5,13},{8,0},{9,4},{12,1},{13,5},{2,10},{3,14},... | collective-permute-start | bytes 786440 | tf_op jit(solution)/shard_map/ppermute | solution.py:57
  20.7 51.3 %collective-permute-start.3 = (bf16[256,512]{1,0:T(8,128)(2,1)S(1)}, bf16[256,512]{1,0:T(8,128)(2,1)}, u32[]{:S(2)}, u32[]{:S(2)}) collective-permute-start(bf16[256,512]{1,0:T(8,128)(2,1)S(1)} %get-tuple-element.67), channel_id=1, source_target_pairs={{0,9},{1,13},{4,0},{5,4},{8,1},{9,5},{12,8},{13,12},{2,11},{3,15},... | collective-permute-start | bytes 786440 | tf_op jit(solution)/shard_map/ppermute | solution.py:57
  22.7 51.5 %collective-permute-start.14 = (bf16[256,512]{1,0:T(8,128)(2,1)S(1)}, bf16[256,512]{1,0:T(8,128)(2,1)}, u32[]{:S(2)}, u32[]{:S(2)}) collective-permute-start(bf16[256,512]{1,0:T(8,128)(2,1)S(1)} %get-tuple-element.56), channel_id=1, source_target_pairs={{0,0},{1,4},{4,1},{5,5},{8,8},{9,12},{12,9},{13,13},{2,2},{3,6},{6... | collective-permute-start | bytes 786440 | tf_op jit(solution)/shard_map/ppermute | solution.py:57
  64.5 42.2 %collective-permute-start.16 = (bf16[256,512]{1,0:T(8,128)(2,1)S(1)}, bf16[256,512]{1,0:T(8,128)(2,1)}, u32[]{:S(2)}, u32[]{:S(2)}) collective-permute-start(bf16[256,512]{1,0:T(8,128)(2,1)S(1)} %get-tuple-element.58), channel_id=1, source_target_pairs={{0,8},{1,12},{4,9},{5,13},{8,0},{9,4},{12,1},{13,5},{2,10},{3,14},... | collective-permute-start | bytes 786440 | tf_op jit(solution)/shard_map/ppermute | solution.py:57
  64.6 42.1 %collective-permute-start.17 = (bf16[256,512]{1,0:T(8,128)(2,1)S(1)}, bf16[256,512]{1,0:T(8,128)(2,1)}, u32[]{:S(2)}, u32[]{:S(2)}) collective-permute-start(bf16[256,512]{1,0:T(8,128)(2,1)S(1)} %get-tuple-element.57), channel_id=1, source_target_pairs={{0,9},{1,13},{4,0},{5,4},{8,1},{9,5},{12,8},{13,12},{2,11},{3,15},... | collective-permute-start | bytes 786440 | tf_op jit(solution)/shard_map/ppermute | solution.py:57
  72.0 71.5 %collective-permute-start.5 = (s32[2,1,1024]{2,1,0:T(1,128)S(1)}, s32[2,1,1024]{2,1,0:T(1,128)S(1)}, u32[]{:S(2)}, u32[]{:S(2)}) collective-permute-start(s32[2,1,1024]{2,1,0:T(1,128)S(1)} %copy-done.54), channel_id=1, source_target_pairs={{0,1},{1,0},{2,3},{3,2},{4,5},{5,4},{6,7},{7,6},{8,9},{9,8},{10,11... | collective-permute-start | bytes 24584 | tf_op jit(solution)/shard_map/ppermute | solution.py:94
  413.8 38.3 %collective-permute-start.8 = (bf16[512,1024]{1,0:T(8,128)(2,1)}, bf16[512,1024]{1,0:T(8,128)(2,1)}, u32[]{:S(2)}, u32[]{:S(2)}) collective-permute-start(bf16[512,1024]{1,0:T(8,128)(2,1)} %fusion.83), channel_id=1, source_target_pairs={{0,1},{1,0},{4,5},{5,4},{8,9},{9,8},{12,13},{13,12},{2,3},{3,2},{6... | collective-permute-start | bytes 3145736 | tf_op jit(solution)/shard_map/ppermute | solution.py:82
  613.3 49.9 %collective-permute-start.18 = (bf16[512,1024]{1,0:T(8,128)(2,1)}, bf16[512,1024]{1,0:T(8,128)(2,1)}, u32[]{:S(2)}, u32[]{:S(2)}) collective-permute-start(bf16[512,1024]{1,0:T(8,128)(2,1)} %copy.145), channel_id=1, source_target_pairs={{0,1},{1,0},{4,5},{5,4},{8,9},{9,8},{12,13},{13,12},{2,3},{3,2},{6... | collective-permute-start | bytes 3145736 | tf_op jit(solution)/shard_map/ppermute | solution.py:88
  782.9 66.6 %collective-permute-start.22 = (bf16[512,1024]{1,0:T(8,128)(2,1)}, bf16[512,1024]{1,0:T(8,128)(2,1)}, u32[]{:S(2)}, u32[]{:S(2)}) collective-permute-start(bf16[512,1024]{1,0:T(8,128)(2,1)} %copy.153), channel_id=1, source_target_pairs={{0,1},{1,0},{4,5},{5,4},{8,9},{9,8},{12,13},{13,12},{2,3},{3,2},{6... | collective-permute-start | bytes 3145736 | tf_op jit(solution)/shard_map/ppermute | solution.py:88
  788.0 277.8 %reduce-scatter.5.cloned.1.call-start = ((), (), s32[]{:S(2)}) async-start(), calls=%async_computation.8 | async-start | bytes 6684672 | tf_op jit(solution)/shard_map/reduce_scatter | solution.py:247
  878.3 204.5 %reduce-scatter.11.cloned.1.call-start = ((), (), s32[]{:S(2)}) async-start(), calls=%async_computation.11 | async-start | bytes 8912896 | tf_op jit(solution)/shard_map/reduce_scatter | solution.py:235
  913.5 277.7 %reduce-scatter.9.cloned.1.call-start = ((), (), s32[]{:S(2)}) async-start(), calls=%async_computation.10 | async-start | bytes 8912896 | tf_op jit(solution)/shard_map/reduce_scatter | solution.py:235
  956.1 37.6 %collective-permute-start.12 = (bf16[256,512]{1,0:T(8,128)(2,1)}, bf16[256,512]{1,0:T(8,128)(2,1)}, u32[]{:S(2)}, u32[]{:S(2)}) collective-permute-start(bf16[256,512]{1,0:T(8,128)(2,1)} %get-tuple-element.64), channel_id=1, source_target_pairs={{8,0},{12,1},{9,4},{13,5},{0,8},{4,9},{1,12},{5,13},{10,2},{14,3},... | collective-permute-start | bytes 786440 | tf_op jit(solution)/shard_map/ppermute | solution.py:68
  964.9 87.0 %collective-permute-start.23 = (bf16[256,512]{1,0:T(8,128)(2,1)S(1)}, bf16[256,512]{1,0:T(8,128)(2,1)}, u32[]{:S(2)}, u32[]{:S(2)}) collective-permute-start(bf16[256,512]{1,0:T(8,128)(2,1)S(1)} %get-tuple-element.52), channel_id=1, source_target_pairs={{0,0},{4,1},{1,4},{5,5},{8,8},{12,9},{9,12},{13,13},{2,2},{6,3},{3... | collective-permute-start | bytes 786440 | tf_op jit(solution)/shard_map/ppermute | solution.py:68
  970.3 81.6 %collective-permute-start.24 = (bf16[256,512]{1,0:T(8,128)(2,1)S(1)}, bf16[256,512]{1,0:T(8,128)(2,1)}, u32[]{:S(2)}, u32[]{:S(2)}) collective-permute-start(bf16[256,512]{1,0:T(8,128)(2,1)S(1)} %get-tuple-element.55), channel_id=1, source_target_pairs={{1,0},{5,1},{8,4},{12,5},{9,8},{13,9},{0,12},{4,13},{3,2},{7,3},{1... | collective-permute-start | bytes 786440 | tf_op jit(solution)/shard_map/ppermute | solution.py:68
  976.9 75.0 %collective-permute-start.25 = (bf16[256,512]{1,0:T(8,128)(2,1)S(1)}, bf16[256,512]{1,0:T(8,128)(2,1)}, u32[]{:S(2)}, u32[]{:S(2)}) collective-permute-start(bf16[256,512]{1,0:T(8,128)(2,1)S(1)} %get-tuple-element.54), channel_id=1, source_target_pairs={{8,0},{12,1},{9,4},{13,5},{0,8},{4,9},{1,12},{5,13},{10,2},{14,3},... | collective-permute-start | bytes 786440 | tf_op jit(solution)/shard_map/ppermute | solution.py:68
  993.7 58.2 %collective-permute-start.26 = (bf16[256,512]{1,0:T(8,128)(2,1)S(1)}, bf16[256,512]{1,0:T(8,128)(2,1)}, u32[]{:S(2)}, u32[]{:S(2)}) collective-permute-start(bf16[256,512]{1,0:T(8,128)(2,1)S(1)} %get-tuple-element.53), channel_id=1, source_target_pairs={{9,0},{13,1},{0,4},{4,5},{1,8},{5,9},{8,12},{12,13},{11,2},{15,3},... | collective-permute-start | bytes 786440 | tf_op jit(solution)/shard_map/ppermute | solution.py:68
  (81 other events, 2589.5 us)
Sparse Core Ops, SparseCore 0:
  10.9 94.0 all-gather.5
  107.8 44.0 all-gather.7
  154.0 74.0 all-gather.9
  230.7 73.1 all-gather.11
  788.1 61.4 reduce-scatter.6
  878.4 89.6 reduce-scatter.4
  972.1 110.5 reduce-scatter.10
  1086.8 104.3 reduce-scatter.8

commit v2 on v1

v2 whole, which is shorter than its diff:
```python
import functools

import jax
import jax.numpy as jnp
from jax import lax
from jax.experimental import pallas as pl
from jax.experimental.pallas import tpu as pltpu
from jax.sharding import Mesh
from jax.sharding import PartitionSpec as P

HD = 64
EPSILON = 1e-05
NEG_BIG = -1e30
CORES = 2
PAIR = 128
PLANE = ("row", "high", "core")
MESH = pl.DeviceIdType.MESH
F32 = jnp.float32
BF16 = jnp.bfloat16
VMEM_BYTES = 56 * 1024 * 1024
LOW_VMEM = 63 * 1024 * 1024


def nn(left, right):
    return lax.dot_general(left, right, (((1,), (0,)), ((), ())), preferred_element_type=F32)


def nt(left, right):
    return lax.dot_general(left, right, (((1,), (1,)), ((), ())), preferred_element_type=F32)


def held(shape):
    return pl.BlockSpec(shape, lambda *_: (0,) * len(shape), pipeline_mode=pl.Buffered(1))


def call(kernel, grid, in_specs, out_specs, out_shape, scratch, name, flops, moved, args):
    return pl.pallas_call(
        kernel,
        grid=grid,
        in_specs=in_specs,
        out_specs=out_specs,
        out_shape=out_shape,
        scratch_shapes=scratch,
        name=name,
        compiler_params=pltpu.CompilerParams(
            vmem_limit_bytes=VMEM_BYTES, dimension_semantics=("arbitrary",) * len(grid)
        ),
        cost_estimate=pl.CostEstimate(flops=flops, bytes_accessed=moved, transcendentals=0),
    )(*args)


def shaped(shape, dtype):
    return jax.ShapeDtypeStruct(shape, dtype)


def row_blocks(rows, narrow):
    take = min(rows, max(1, 256 // narrow))
    while rows % take:
        take += 1
    return take


def side_by_side(blocks):
    take, cols, narrow, deep = blocks.shape
    return jnp.concatenate([blocks[:, k].reshape(take * narrow, deep) for k in range(cols)], axis=1)


def project_kernel(x_ref, w_ref, b_ref, o_ref, *, scale):
    out = nt(x_ref[...], side_by_side(w_ref[...])) + b_ref[0]
    o_ref[0] = (out * scale).astype(BF16)


QKV, OUT, UNIT = 0, 3, 4
FEED_BLOCKS = 2


def project(x, weight, bias, first, count, scale):
    tokens, width = x.shape
    rows, cols, _, deep = weight.shape
    narrow = width // rows
    take = row_blocks(rows, narrow)
    return call(
        functools.partial(project_kernel, scale=scale),
        (count, rows // take),
        [
            held((tokens, width)),
            pl.BlockSpec((take, cols, narrow, deep), lambda k, r: (r, 0, QKV + k + first, 0)),
            pl.BlockSpec((1, 1, take * narrow), lambda k, r: (k, 0, r)),
        ],
        pl.BlockSpec((1, tokens, take * narrow), lambda k, r: (k, 0, r)),
        shaped((count, tokens, width), BF16),
        [],
        "project",
        2 * count * tokens * width * width,
        2 * count * width * width,
        (x, weight, bias),
    )


def head_lanes(shape, axis):
    return lax.broadcasted_iota(jnp.int32, shape, axis) < HD


def pair_front(query, keys, values, bias_ref):
    values_t = values.T
    lanes = head_lanes(query.shape, 1)
    outs, log_rows = [], []
    for h in range(2):
        mine = jnp.where(lanes if h == 0 else ~lanes, query, 0)
        scores = nt(keys, mine) + bias_ref[...]
        top = jnp.max(scores, axis=0, keepdims=True)
        expo = jnp.exp(scores - top)
        total = jnp.sum(expo, axis=0, keepdims=True)
        outs.append(nn(values_t, expo.astype(BF16)) / total)
        log_rows.append(top + jnp.log(total))
    mixed_t = jnp.where(head_lanes(outs[0].shape, 0), outs[0], outs[1])
    return mixed_t.T.astype(BF16), log_rows


def attend_kernel(*refs, group):
    q_ref, kv_refs = refs[0], refs[1 : 1 + group]
    dq_ref, dk_ref, o_ref, l_ref, bias_ref = refs[1 + group :]

    @pl.when(pl.program_id(0) == 0)
    def _():
        bias_ref[...] = jnp.where(dk_ref[...] == dq_ref[...], 0.0, NEG_BIG)

    keys = jnp.concatenate([ref[0] for ref in kv_refs], axis=0)
    values = jnp.concatenate([ref[1] for ref in kv_refs], axis=0)
    o_ref[...], log_rows = pair_front(q_ref[0], keys, values, bias_ref)
    for h in range(2):
        l_ref[0, h : h + 1, :] = log_rows[h]


def attend(query, shared, doc_query, doc_key):
    _, tokens, width = query.shape
    group = len(shared)
    keys = group * tokens
    pairs = width // PAIR
    kv_spec = pl.BlockSpec((2, tokens, PAIR), lambda p: (0, 0, p))
    return call(
        functools.partial(attend_kernel, group=group),
        (pairs,),
        [pl.BlockSpec((1, tokens, PAIR), lambda p: (0, 0, p))]
        + [kv_spec] * group
        + [held((1, tokens)), held((keys, 1))],
        [
            pl.BlockSpec((tokens, PAIR), lambda p: (0, p)),
            pl.BlockSpec((1, 2, tokens), lambda p: (p, 0, 0)),
        ],
        [shaped((tokens, width), BF16), shaped((pairs, 2, tokens), F32)],
        [pltpu.VMEM((keys, tokens), F32)],
        "attend",
        16 * tokens * keys * width,
        10 * tokens * width,
        (query, *shared, doc_query, doc_key),
    )


def pair_back(query, grad, mixed, log_rows, keys, values, bias_ref, tile):
    tokens = query.shape[0]
    keys_t = keys.T
    lanes = head_lanes((tile, PAIR), 1)
    low_t = head_lanes(keys_t.shape, 0)
    products = (grad.astype(F32) * mixed.astype(F32)).T
    grad_query = []
    grad_key = jnp.zeros(keys.shape, F32)
    grad_value = jnp.zeros(keys.shape, F32)
    for at in range(0, tokens, tile):
        some = slice(at, at + tile)
        grad_some = jnp.zeros((PAIR, tile), F32)
        for h in range(2):
            here = lanes if h == 0 else ~lanes
            mine = jnp.where(here, query[some], 0)
            grad_mine = jnp.where(here, grad[some], 0)
            inner = jnp.sum(products[h * HD : (h + 1) * HD, some], axis=0, keepdims=True)
            prob = jnp.exp(nt(keys, mine) + bias_ref[:, some] - log_rows[h][:, some])
            grad_value += nn(prob.astype(BF16), grad_mine)
            grad_scores = (prob * (nt(values, grad_mine) - inner)).astype(BF16)
            grad_key += nn(grad_scores, mine)
            keys_mine = jnp.where(low_t if h == 0 else ~low_t, keys_t, 0)
            grad_some += nn(keys_mine, grad_scores)
        grad_query.append(grad_some)
    grad_query = jnp.concatenate(grad_query, axis=1).T.astype(BF16) * HD**-0.5
    return grad_query, grad_key.astype(BF16), grad_value.astype(BF16)


def attend_back_kernel(*refs, group):
    q_ref, g_ref, o_ref, l_ref, kv_refs = refs[0], refs[1], refs[2], refs[3], refs[4 : 4 + group]
    dq_doc, dk_doc, dq_ref, dkv_ref, bias_ref = refs[4 + group :]

    @pl.when(pl.program_id(0) == 0)
    def _():
        bias_ref[...] = jnp.where(dk_doc[...] == dq_doc[...], 0.0, NEG_BIG)

    tokens = q_ref.shape[1]
    keys = jnp.concatenate([ref[0] for ref in kv_refs], axis=0)
    values = jnp.concatenate([ref[1] for ref in kv_refs], axis=0)
    log_rows = [l_ref[0, h : h + 1, :] for h in range(2)]
    grad_query, grad_key, grad_value = pair_back(
        q_ref[0], g_ref[...], o_ref[...], log_rows, keys, values, bias_ref, tokens
    )
    dq_ref[...] = grad_query
    for part in range(group):
        dkv_ref[part, 0] = grad_key[part * tokens : (part + 1) * tokens]
        dkv_ref[part, 1] = grad_value[part * tokens : (part + 1) * tokens]


def attend_back(query, grad_mixed, mixed, log_total, shared, doc_query, doc_key):
    _, tokens, width = query.shape
    group = len(shared)
    keys = group * tokens
    pairs = width // PAIR
    flat = pl.BlockSpec((tokens, PAIR), lambda p: (0, p))
    kv_spec = pl.BlockSpec((2, tokens, PAIR), lambda p: (0, 0, p))
    return call(
        functools.partial(attend_back_kernel, group=group),
        (pairs,),
        [
            pl.BlockSpec((1, tokens, PAIR), lambda p: (0, 0, p)),
            flat,
            flat,
            pl.BlockSpec((1, 2, tokens), lambda p: (p, 0, 0)),
        ]
        + [kv_spec] * group
        + [held((1, tokens)), held((keys, 1))],
        [flat, pl.BlockSpec((group, 2, tokens, PAIR), lambda p: (0, 0, 0, p))],
        [shaped((tokens, width), BF16), shaped((group, 2, tokens, width), BF16)],
        [pltpu.VMEM((keys, tokens), F32)],
        "attend_back",
        40 * tokens * keys * width,
        20 * tokens * width,
        (query, grad_mixed, mixed, log_total, *shared, doc_query, doc_key),
    )


def normed_of(hidden):
    center = hidden - jnp.mean(hidden, axis=1, keepdims=True)
    scale = lax.rsqrt(jnp.mean(center * center, axis=1, keepdims=True) + EPSILON)
    return center * scale, scale


def norm_back(grad_out, normed, scale, gain):
    scaled = grad_out * gain
    first = jnp.mean(scaled, axis=1, keepdims=True)
    second = jnp.mean(scaled * normed, axis=1, keepdims=True)
    return scale * (scaled - first - normed * second)


SLICE = 128


def by_tokens(tokens, body):
    step = min(SLICE, tokens)
    for at in range(0, tokens, step):
        body(pl.ds(at, step))


def out_kernel(m_ref, w_ref, x_ref, b_ref, n_ref, x1_ref, xb_ref, hat_ref, scale_ref, acc_ref, *, cols, deep):
    k = pl.program_id(0)
    rows, _, narrow, _ = w_ref.shape
    acc_ref[k] = nn(m_ref[...], w_ref[...].reshape(rows * narrow, deep))

    @pl.when(k == cols - 1)
    def _():
        def some(at):
            attn = jnp.concatenate([acc_ref[j, at] for j in range(cols)], axis=1)
            normed, scale = normed_of(x_ref[at].astype(F32) + (attn + b_ref[2:3]))
            x1 = normed * n_ref[0:1] + b_ref[3:4]
            x1_ref[at] = x1
            xb_ref[at] = x1.astype(BF16)
            hat_ref[at] = normed
            scale_ref[at] = jnp.broadcast_to(scale, scale_ref[at].shape)

        by_tokens(x_ref.shape[0], some)


def out_norm(mixed, weight, x, bias, gain):
    tokens, width = x.shape
    rows, cols, _, deep = weight.shape
    narrow = width // rows
    flat = held((tokens, width))
    return call(
        functools.partial(out_kernel, cols=cols, deep=deep),
        (cols,),
        [
            flat,
            pl.BlockSpec((rows, 1, narrow, deep), lambda k: (0, k, OUT, 0)),
            flat,
            held(bias.shape),
            held(gain.shape),
        ],
        [flat, flat, flat, held((tokens, 128))],
        [
            shaped((tokens, width), F32),
            shaped((tokens, width), BF16),
            shaped((tokens, width), F32),
            shaped((tokens, 128), F32),
        ],
        [pltpu.VMEM((cols, tokens, deep), F32)],
        "out_norm",
        2 * tokens * width * width,
        2 * width * width + 12 * tokens * width,
        (mixed, weight, x, bias, gain),
    )


def gelu_parts(pre):
    below = 0.5 * (1.0 + lax.erf(pre * 0.5**0.5))
    return pre * below, below + pre * jnp.exp(-0.5 * pre * pre) * (2.0 * jnp.pi) ** -0.5


def hidden_columns(block, width):
    rows, _, tall, deep = block.shape
    narrow = width // rows
    parts = [block[:, 0, i * narrow : (i + 1) * narrow].reshape(width, deep) for i in range(FEED_BLOCKS)]
    return jnp.concatenate(parts, axis=1)


def feed_kernel(xb_ref, wu_ref, wd_ref, ub_ref, x1_ref, b_ref, n_ref, y_ref, *rest, steps, saving):
    acc_ref = rest[-1]
    s = pl.program_id(0)
    width = xb_ref.shape[1]
    pre = nn(xb_ref[...], hidden_columns(wu_ref[...], width)) + ub_ref[...]
    act, slope = gelu_parts(pre)
    act = act.astype(BF16)
    if saving:
        rest[0][...] = act
        rest[1][...] = slope.astype(BF16)
    down = nt(act, hidden_columns(wd_ref[...], width))

    @pl.when(s == 0)
    def _():
        acc_ref[...] = down

    @pl.when(s > 0)
    def _():
        acc_ref[...] += down

    @pl.when(s == steps - 1)
    def _():
        def some(at):
            normed, scale = normed_of(x1_ref[at] + (acc_ref[at] + b_ref[4:5]))
            y_ref[at] = (normed * n_ref[1:2] + b_ref[5:6]).astype(BF16)
            if saving:
                rest[2][at] = normed
                rest[3][at] = jnp.broadcast_to(scale, rest[3][at].shape)

        by_tokens(xb_ref.shape[0], some)


def feed_specs(weight, tokens, width, units):
    rows, cols, _, deep = weight.shape
    tall = FEED_BLOCKS * (width // rows)
    block = FEED_BLOCKS * deep
    per = units // cols // block

    def at(first):
        return pl.BlockSpec((rows, 1, tall, deep), lambda s: (0, s // per, first // FEED_BLOCKS + s % per, 0))

    wide = pl.BlockSpec((tokens, block), lambda s: (0, s))
    line = pl.BlockSpec((1, block), lambda s: (0, s))
    return cols * per, at(UNIT), at(UNIT + per * FEED_BLOCKS), wide, line


def feed(x1_bf, weight, unit_shift, x1, bias, gain, saving):
    tokens, width = x1.shape
    units = unit_shift.shape[1]
    steps, first, second, wide, line = feed_specs(weight, tokens, width, units)
    flat = held((tokens, width))
    out_specs, out_shape = [flat], [shaped((tokens, width), BF16)]
    if saving:
        out_specs += [wide, wide, flat, held((tokens, 128))]
        out_shape += [
            shaped((tokens, units), BF16),
            shaped((tokens, units), BF16),
            shaped((tokens, width), F32),
            shaped((tokens, 128), F32),
        ]
    return call(
        functools.partial(feed_kernel, steps=steps, saving=saving),
        (steps,),
        [flat, first, second, line, flat, held(bias.shape), held(gain.shape)],
        out_specs,
        out_shape,
        [pltpu.VMEM((tokens, width), F32)],
        "feed",
        4 * tokens * width * units,
        4 * width * units,
        (x1_bf, weight, weight, unit_shift, x1, bias, gain),
    )


def column_sum(value):
    return jnp.sum(value, axis=0, keepdims=True)


def top_back_kernel(dy_ref, hat_ref, scale_ref, n_ref, dh2_ref, ddown_ref, *sums_ref):
    for ref in sums_ref:
        ref[...] = jnp.zeros_like(ref)

    def some(at):
        dy, hat = dy_ref[at].astype(F32), hat_ref[at]
        dh2 = norm_back(dy, hat, scale_ref[at][:, :1], n_ref[1:2])
        dh2_ref[at] = dh2
        ddown = dh2.astype(BF16)
        ddown_ref[at] = ddown
        for ref in sums_ref:
            ref[0:1] += column_sum(ddown.astype(F32))
            ref[1:2] += column_sum(dy)
            ref[2:3] += column_sum(dy * hat)

    by_tokens(dy_ref.shape[0], some)


def top_back(dy, hat2, scale2, gain, sums_too):
    tokens, width = hat2.shape
    flat = held((tokens, width))
    return call(
        top_back_kernel,
        (1,),
        [flat, flat, held((tokens, 128)), held(gain.shape)],
        [flat, flat] + [held((8, width))] * sums_too,
        [shaped((tokens, width), F32), shaped((tokens, width), BF16)] + [shaped((8, width), F32)] * sums_too,
        [],
        "top_back",
        20 * tokens * width,
        12 * tokens * width,
        (dy, hat2, scale2, gain),
    )


def feed_back_kernel(*refs, steps, sums_too):
    dh2_ref, ddown_ref, hat1_ref, scale1_ref, slope_ref, wu_ref, wd_ref, n_ref, dattn_ref = refs[:9]
    acc_ref = refs[-1]
    s = pl.program_id(0)
    tokens, width = dh2_ref.shape
    dact = nn(ddown_ref[...], hidden_columns(wd_ref[...], width))
    dpre = (dact * slope_ref[...].astype(F32)).astype(BF16)
    back = nt(dpre, hidden_columns(wu_ref[...], width))
    if sums_too:
        dpre_ref, pre_ref, sums_ref = refs[9:12]
        dpre_ref[...] = dpre
        pre_ref[...] = column_sum(dpre.astype(F32))

    @pl.when(s == 0)
    def _():
        acc_ref[...] = back

    @pl.when(s > 0)
    def _():
        acc_ref[...] += back

    @pl.when(s == steps - 1)
    def _():
        if sums_too:
            sums_ref[...] = jnp.zeros_like(sums_ref)

        def some(at):
            dx1, hat = dh2_ref[at] + acc_ref[at], hat1_ref[at]
            dattn = norm_back(dx1, hat, scale1_ref[at][:, :1], n_ref[0:1]).astype(BF16)
            dattn_ref[at] = dattn
            if sums_too:
                sums_ref[0:1] += column_sum(dattn.astype(F32))
                sums_ref[1:2] += column_sum(dx1)
                sums_ref[2:3] += column_sum(dx1 * hat)

        by_tokens(tokens, some)


def feed_back(dh2, ddown, hat1, scale1, slope, weight, gain, sums_too):
    tokens, width = dh2.shape
    units = slope.shape[1]
    steps, first, second, wide, line = feed_specs(weight, tokens, width, units)
    flat = held((tokens, width))
    out_specs, out_shape = [flat], [shaped((tokens, width), BF16)]
    if sums_too:
        out_specs += [wide, line, held((8, width))]
        out_shape += [shaped((tokens, units), BF16), shaped((1, units), F32), shaped((8, width), F32)]
    return call(
        functools.partial(feed_back_kernel, steps=steps, sums_too=sums_too),
        (steps,),
        [flat, flat, flat, held((tokens, 128)), wide, first, second, held(gain.shape)],
        out_specs,
        out_shape,
        [pltpu.VMEM((tokens, width), F32)],
        "feed_back",
        4 * tokens * width * units,
        4 * width * units,
        (dh2, ddown, hat1, scale1, slope, weight, weight, gain),
    )


def mixed_back_kernel(g_ref, w_ref, o_ref):
    o_ref[...] = nt(g_ref[...], side_by_side(w_ref[...])).astype(BF16)


def mixed_back(grad, weight):
    tokens, width = grad.shape
    rows, cols, _, deep = weight.shape
    narrow = width // rows
    take = row_blocks(rows, narrow)
    return call(
        mixed_back_kernel,
        (rows // take,),
        [held((tokens, width)), pl.BlockSpec((take, cols, narrow, deep), lambda r: (r, 0, OUT, 0))],
        pl.BlockSpec((tokens, take * narrow), lambda r: (0, r)),
        shaped((tokens, width), BF16),
        [],
        "mixed_back",
        2 * tokens * width * width,
        2 * width * width,
        (grad, weight),
    )


def input_back_kernel(*refs, group):
    dq_ref, own_ref, others, (w_ref, dattn_ref, dx_ref, dp_ref) = refs[0], refs[1], refs[2 : 1 + group], refs[1 + group :]
    tokens, width = dq_ref.shape
    rows, _, tall, deep = w_ref.shape
    narrow = tall // 3

    @pl.when(pl.program_id(0) == 0)
    def _():
        def some(at):
            dp_ref[0, at] = dq_ref[at]
            for j in range(2):
                total = own_ref[0, j, at].astype(F32)
                for other in others:
                    total += other[j, at].astype(F32)
                dp_ref[1 + j, at] = total.astype(BF16)

        by_tokens(tokens, some)

    total = dattn_ref[...].astype(F32)
    for j in range(3):
        total += nn(dp_ref[j], w_ref[:, 0, j * narrow : (j + 1) * narrow].reshape(width, deep))
    dx_ref[...] = total.astype(BF16)


def input_back(dq, dkv, others, weight, dattn):
    tokens, width = dq.shape
    group = dkv.shape[0]
    rows, cols, _, deep = weight.shape
    part = pl.BlockSpec((tokens, deep), lambda k: (0, k))
    return call(
        functools.partial(input_back_kernel, group=group),
        (cols,),
        [held((tokens, width)), held((1, 2, tokens, width))]
        + [held((2, tokens, width))] * (group - 1)
        + [pl.BlockSpec((rows, 1, 3 * (width // rows), deep), lambda k: (0, k, 0, 0)), part],
        part,
        shaped((tokens, width), BF16),
        [pltpu.VMEM((3, tokens, width), BF16)],
        "input_back",
        6 * tokens * width * width,
        6 * width * width,
        (dq, dkv, *others, weight, dattn),
    )


class Layout:
    def __init__(self, tokens_in, doc_ids):
        self.micro, self.narrow, _ = tokens_in.shape
        self.seq_here, self.seq_len = doc_ids.shape[1:]
        self.rows = lax.axis_size("row")
        self.cols = lax.axis_size("high") * CORES
        self.width = self.narrow * self.rows
        self.places = self.rows * CORES
        self.sequences = self.micro * self.seq_here * CORES
        self.group = self.places // self.sequences
        self.part = self.seq_len // self.group
        self.row = lax.axis_index("row")
        place = self.row * CORES + lax.axis_index("core")
        self.sequence = place // self.group
        self.position = place % self.group
        self.block = (self.sequence // CORES) * self.group + self.position

    def routes(self, shift):
        pairs = []
        for source in range(self.places):
            row, core = divmod(source, CORES)
            block = (row + shift) % self.rows
            sequence = (block // self.group) * CORES + core
            pairs.append((source, sequence * self.group + block % self.group))
        return pairs

    def to_features(self, array):
        blocks = array.T.reshape(self.rows, self.narrow, self.part)
        got = []
        for shift in range(self.rows):
            block = lax.dynamic_index_in_dim(blocks, (self.block - shift) % self.rows, 0, False)
            pairs = [(there, here) for here, there in self.routes(shift)]
            got.append(lax.ppermute(block, ("row", "core"), pairs))
        order = (jnp.arange(self.rows) - self.row) % self.rows
        whole = jnp.take(jnp.stack(got), order, axis=0)
        whole = whole.reshape(self.micro, self.seq_here * self.group, self.narrow, self.part)
        return whole.transpose(0, 2, 1, 3).reshape(self.micro, self.narrow, self.seq_here * self.seq_len)

    def within(self, step):
        return [
            (place, place // self.group * self.group + (place + step) % self.group)
            for place in range(self.places)
        ]

    def share(self, array):
        return [array] + [
            lax.ppermute(array, ("row", "core"), self.within(step)) for step in range(1, self.group)
        ]

    def give_back(self, blocks):
        return [
            lax.ppermute(blocks[step], ("row", "core"), self.within(self.group - step))
            for step in range(1, self.group)
        ]


class Line:
    def __init__(self, axis, size):
        self.axis, self.size, self.here = axis, size, lax.axis_index(axis)

    def sends(self, step):
        last = self.size - 1
        return (
            (True, (self.here < step) & (self.here < last), self.size - step + self.here, self.here > 0),
            (False, (last - self.here < step) & (self.here > 0), step - self.size + self.here, self.here < last),
        )

    def gets(self, step):
        last = self.size - 1
        return (
            (True, (self.here >= 1) & (self.here <= step)),
            (False, (last - self.here >= 1) & (last - self.here <= step)),
        )

    def neighbour(self, right):
        return {self.axis: self.here + (1 if right else -1)}


def greet(lines, pairs, members=()):
    barrier = pltpu.get_barrier_semaphore()
    count = 0
    for line in lines:
        for right, there in ((True, line.here < line.size - 1), (False, line.here > 0)):

            @pl.when(there)
            def _(line=line, right=right):
                pl.semaphore_signal(barrier, 1, device_id=line.neighbour(right), device_id_type=MESH)

            count = count + there.astype(jnp.int32)
    for axis in pairs:
        pl.semaphore_signal(barrier, 1, device_id={axis: 1 - lax.axis_index(axis)}, device_id_type=MESH)
        count = count + 1
    for member in members:
        pl.semaphore_signal(barrier, 1, device_id=member, device_id_type=MESH)
        count = count + 1
    pl.semaphore_wait(barrier, count)


def add_into(target, other):
    lead = target.shape[:-2]
    rows = target.shape[-2]
    total = 1
    for size in lead:
        total *= size
    if total == 1:
        target[...] = target[...] + other[...]
        return

    @pl.loop(0, total)
    def _(i):
        index = []
        for size in reversed(lead):
            index.insert(0, lax.rem(i, size))
            i = lax.div(i, size)
        index = tuple(index)
        target[index] = target[index] + other[index]


class Scatter:
    def __init__(self, pieces, refs, highs, rows):
        self.pieces = pieces
        (self.landing, self.work, self.got, self.from_high, self.got_high, self.from_row, self.out, *sems) = refs
        self.sem_core, self.sem_load, self.sem_high, self.sem_row = sems
        self.high, self.row = Line("high", highs), Line("row", rows)
        self.core = lax.axis_index("core")
        self.slots = self.work.shape[0]
        self.sent = [[] for _ in pieces]

    def slot(self, q):
        return q % self.slots

    def cut(self, q, ref):
        return ref.at[..., pl.ds(0, self.pieces[q][2]), :]

    def source(self, q, y, core):
        ref, first, rows = self.pieces[q]
        return ref.at[:, y, core, pl.ds(first, rows)]

    def to_core(self, q, y):
        return pltpu.make_async_remote_copy(
            self.source(q, y, 1 - self.core),
            self.cut(q, self.landing.at[q, y]),
            self.sem_core.at[q, y, 0],
            self.sem_core.at[q, y, 1],
            device_id={"core": 1 - self.core},
            device_id_type=MESH,
        )

    def load(self, q, y):
        return pltpu.make_async_copy(
            self.source(q, y, self.core), self.cut(q, self.work.at[self.slot(q), y]), self.sem_load.at[q, y, 0]
        )

    def fetch(self, q, y):
        return pltpu.make_async_copy(
            self.cut(q, self.landing.at[q, y]), self.cut(q, self.got.at[q % 2, y]), self.sem_load.at[q, y, 1]
        )

    def begin(self, q):
        if q >= self.slots:
            self.finish_sends(q - self.slots)
        for y in range(self.high.size):
            self.to_core(q, y).start()
            self.load(q, y).start()

    def arrive(self, q):
        for y in range(self.high.size):
            copy = self.to_core(q, y)
            copy.wait()
            self.fetch(q, y).start()

    def merge(self, q):
        for y in range(self.high.size):
            self.load(q, y).wait()
            self.fetch(q, y).wait()
            add_into(self.cut(q, self.work.at[self.slot(q), y]), self.cut(q, self.got.at[q % 2, y]))
        self.push(q, self.high, 1)

    def parts(self, q, line):
        work = self.work.at[self.slot(q)]
        if line is self.high:
            return (lambda t: self.cut(q, work.at[t])), self.from_high.at[q], self.sem_high.at[q]
        return (lambda t: self.cut(q, work.at[self.high.here, t])), self.from_row.at[q], self.sem_row.at[q]

    def copy(self, q, line, step, right, block):
        where, landing, sems = self.parts(q, line)
        way = 0 if right else 1
        way_slot = 0 if line.size == 2 else way
        return pltpu.make_async_remote_copy(
            where(block),
            self.cut(q, landing.at[step - 1, way_slot]),
            sems.at[step - 1, way, 0],
            sems.at[step - 1, way, 1],
            device_id=line.neighbour(right),
            device_id_type=MESH,
        )

    def landed(self, q, line, step, right):
        way = 0 if line.size == 2 or right else 1
        if line is self.high:
            return self.cut(q, self.got_high.at[q % 2, way])
        return self.cut(q, self.from_row.at[q, step - 1, way])

    def push(self, q, line, step):
        where, _, _ = self.parts(q, line)
        for right, there, block, more in line.sends(step):

            @pl.when(there)
            def _(right=right, block=block, more=more):
                if step > 1:

                    @pl.when(more)
                    def _():
                        add_into(where(block), self.landed(q, line, step - 1, right))

                self.copy(q, line, step, right, block).start()

            self.sent[q].append((line, step, right, there, block))

    def pull(self, q, line, step):
        for right, there in line.gets(step):

            @pl.when(there)
            def _(right=right):
                self.copy(q, line, step, right, 0).wait_recv()
                if line is self.high:
                    way = 0 if line.size == 2 or right else 1
                    fetch = pltpu.make_async_copy(
                        self.cut(q, self.from_high.at[q, step - 1, way]),
                        self.landed(q, line, step, right),
                        self.sem_high.at[q, step - 1, way, 2],
                    )
                    fetch.start()
                    fetch.wait()

    def close(self, q, line):
        where, _, _ = self.parts(q, line)
        for right, there in line.gets(line.size - 1):

            @pl.when(there)
            def _(right=right):
                add_into(where(line.here), self.landed(q, line, line.size - 1, right))

    def give(self, q, at):
        where, _, _ = self.parts(q, self.row)
        rows = self.pieces[q][2]
        self.out[pl.ds(at, rows)] = where(self.row.here)[...].astype(F32)

    def finish_sends(self, q):
        for line, step, right, there, block in self.sent[q]:

            @pl.when(there)
            def _(line=line, step=step, right=right, block=block):
                self.copy(q, line, step, right, block).wait_send()

        self.sent[q] = []

    def stages(self):
        stages = [self.begin, self.arrive, self.merge, lambda q: None]
        for line in (self.high, self.row):
            for step in range(1, line.size):

                def one(q, line=line, step=step):
                    self.pull(q, line, step)
                    if step < line.size - 1:
                        self.push(q, line, step + 1)
                        return
                    self.close(q, line)
                    if line is self.high:
                        self.push(q, self.row, 1)
                    else:
                        self.give(q, self.at[q])

                stages.append(one)
        return stages

    def run(self, between=None):
        self.at, at = [], 0
        for _, _, rows in self.pieces:
            self.at.append(at)
            at += rows
        stages = self.stages()
        count = len(self.pieces)
        for tick in range(count + len(stages) - 1):
            for q in range(max(0, tick - len(stages) + 1), min(tick + 1, count)):
                stages[tick - q](q)
            if between is not None:
                between(tick)
        for q in range(count):
            self.finish_sends(q)


STAGES = 3


def low_kernel(*refs, highs, rows, group):
    (ddown_hbm, act_hbm, x1_hbm, dpre_hbm, dattn_hbm, q_hbm, mixed_hbm, log_hbm, x_hbm, w_hbm, *kv_hbm) = refs[: 10 + group]
    bias_doc_q, bias_doc_k, pre_ref, sums_ref = refs[10 + group : 14 + group]
    out_ref, dx_ref, landing, high_landing = refs[14 + group : 18 + group]
    (dattn, x, q, mixed, log, w_out, w_qkv, kv, dmixed, bias, dkv_got, stage, small, left, right,
     work, got, got_high, from_row, sem_in, sem_right, sem_core, sem_load, sem_high, sem_row, sem_kv) = refs[18 + group :]
    tokens, width = dattn.shape
    narrow, deep = stage.shape[-2:]
    dq, dkv = q, kv
    cols = highs * CORES

    row_at = lax.axis_index("row")
    place = row_at * CORES + lax.axis_index("core")
    position = lax.rem(place, group)

    def member(step):
        other = place - position + lax.rem(position + step, group)
        return {"row": lax.div(other, CORES), "core": lax.rem(other, CORES)}

    units = act_hbm.shape[1]
    feed_pieces = units // cols // deep
    tail = small.shape[3]
    order = [("down", i) for i in range(feed_pieces)] + [("out", 0)]
    order += [("unit", i) for i in range(feed_pieces)] + [("qkv", 0), ("qkv", 1), ("qkv", 2), ("small", 0)]
    pieces = [(stage.at[i % STAGES], 0, narrow) for i in range(len(order) - 1)] + [(small, 0, tail)]
    scatter = Scatter(
        pieces, (landing, work, got, high_landing, got_high, from_row, out_ref, sem_core, sem_load, sem_high, sem_row), highs, rows
    )

    inputs = [
        (ddown_hbm, dattn),
        (x1_hbm, x),
        (dattn_hbm, dattn),
        (w_hbm.at[:, :, pl.ds(OUT * narrow, narrow)], w_out),
        (mixed_hbm, mixed),
        (q_hbm.at[0], q),
        (log_hbm, log),
        *[(kv_hbm[i], kv.at[i]) for i in range(group)],
        (w_hbm.at[:, :, pl.ds(QKV * narrow, 3 * narrow)], w_qkv),
        (x_hbm, x),
    ]
    loads = [pltpu.make_async_copy(a, b, sem_in.at[i]) for i, (a, b) in enumerate(inputs)]
    early = 7 + group

    def share_grads(step):
        return pltpu.make_async_remote_copy(
            dkv.at[step], dkv_got.at[step - 1], sem_kv.at[step - 1, 0], sem_kv.at[step - 1, 1],
            device_id=member(group - step), device_id_type=MESH,
        )

    take = row_blocks(rows, narrow)

    def prepare():
        for load in loads[2:early]:
            load.wait()
        bias[...] = jnp.where(bias_doc_k[...] == bias_doc_q[...], 0.0, NEG_BIG).astype(BF16)

        @pl.loop(0, rows // take)
        def _(r):
            at = pl.ds(pl.multiple_of(r * take * narrow, take * narrow), take * narrow)
            dmixed[:, at] = nt(dattn[...], side_by_side(w_out[pl.ds(r * take, take)])).astype(BF16)

    def fill(slot, block, loaded=None):
        @pl.loop(0, cols)
        def _(k):
            grad = nn(left[...], block(k)).astype(BF16)
            stage[slot, :, lax.div(k, CORES), lax.rem(k, CORES)] = grad.reshape(rows, narrow, deep)

    def column(ref):
        return lambda k: ref[:, pl.ds(pl.multiple_of(k * deep, deep), deep)]

    def fetch(q):
        name, i = order[q]
        source = act_hbm if name == "down" else dpre_hbm
        return [
            pltpu.make_async_copy(
                source.at[:, pl.ds(k * feed_pieces * deep + i * deep, deep)],
                right.at[q % 2, :, pl.ds(k * deep, deep)],
                sem_right.at[q % 2, k],
            )
            for k in range(cols)
        ]

    def is_feed(q):
        return q < len(order) and order[q][0] in ("down", "unit")

    def make(q):
        name, i = order[q]
        slot = q % STAGES
        if q == 0:
            loads[0].wait()
            left[...] = dattn[...].T
            loads[2].start()
        if name in ("down", "unit"):
            if (name, i) == ("unit", 0):
                left[...] = x[...].T
                loads[-1].start()
            for copy in fetch(q):
                copy.wait()
            if is_feed(q + 1):
                for copy in fetch(q + 1):
                    copy.start()
            fill(slot, column(right.at[q % 2]))
        elif name == "out":
            if is_feed(q + 1):
                for copy in fetch(q + 1):
                    copy.start()
            left[...] = mixed[...].T
            fill(slot, column(dattn))
        elif name == "qkv":
            if i == 0:
                loads[-1].wait()
            left[...] = grads_of(i).T
            fill(slot, column(x))
        else:
            small_sums()

    pairs = width // PAIR

    def heads(first, count):
        @pl.loop(first, first + count)
        def _(p):
            at = pl.ds(pl.multiple_of(p * PAIR, PAIR), PAIR)
            keys = jnp.concatenate([kv[i, 0, :, at] for i in range(group)], axis=0)
            values = jnp.concatenate([kv[i, 1, :, at] for i in range(group)], axis=0)
            grad_query, grad_key, grad_value = pair_back(
                q[:, at], dmixed[:, at], mixed[:, at], [log[p, h : h + 1] for h in range(2)], keys, values, bias,
                min(256, tokens),
            )
            dq[:, at] = grad_query
            for part in range(group):
                dkv[part, 0, :, at] = grad_key[part * tokens : (part + 1) * tokens]
                dkv[part, 1, :, at] = grad_value[part * tokens : (part + 1) * tokens]

    def exchange():
        for step in range(1, group):
            share_grads(step).start()

    def join():
        for step in range(1, group):
            share_grads(step).wait()
        for load in loads[early:-1]:
            load.wait()

        @pl.loop(0, tokens, step=min(SLICE, tokens))
        def _(at):
            some = pl.ds(pl.multiple_of(at, min(SLICE, tokens)), min(SLICE, tokens))
            for j in range(2):
                total = dkv[0, j, some].astype(F32)
                for step in range(1, group):
                    total += dkv_got[step - 1, j, some].astype(F32)
                dkv[0, j, some] = total.astype(BF16)

    def grads_of(j):
        return dq[...] if j == 0 else dkv[0, j - 1]

    def input_gradient():
        for k in range(cols):
            at = slice(k * deep, (k + 1) * deep)
            total = dattn[:, at].astype(F32)
            for j in range(3):
                total += nn(grads_of(j), w_qkv[:, k, j * narrow : (j + 1) * narrow].reshape(width, deep))
            dx_ref[:, at] = total.astype(BF16)

    def small_sums():
        vectors = jnp.concatenate([column_sum(grads_of(j).astype(F32)) for j in (0, 2)] + [sums_ref[...]], axis=0)
        vectors = vectors.astype(BF16)
        small[...] = jnp.zeros_like(small)
        lines = pre_ref.shape[1] // cols // deep
        for r in range(rows):
            for k in range(cols):
                small[r, k // CORES, k % CORES, 0:8, 0:narrow] = vectors[:, r * narrow : (r + 1) * narrow]
                for i in range(lines):
                    at = (k * lines + i) * deep
                    small[r, k // CORES, k % CORES, 8 + i : 9 + i] = pre_ref[:, at : at + deep].astype(BF16)

    def between(tick):
        if tick + 1 < len(order):
            make(tick + 1)
        if tick == 1:
            prepare()
        if 2 <= tick < 6:
            heads((tick - 2) * (pairs // 4), pairs // 4)
        if tick == 5:
            exchange()
        if tick == 6:
            join()
        if tick == 7:
            input_gradient()

    for i, load in enumerate(loads[:-1]):
        if i != 2:
            load.start()
    for copy in fetch(0):
        copy.start()
    greet((scatter.high, scatter.row), ("core",), [member(step) for step in range(1, group)])
    loads[1].wait()
    make(0)
    scatter.run(between)


def low_back(ddown, act, x1_bf, dpre, dattn, query, mixed, log_total, x, weight, shared, doc_query, doc_key, pre_sum, sums):
    tokens, width = dattn.shape
    rows, cols, _, deep = weight.shape
    narrow = width // rows
    units = act.shape[1]
    feed_rows = narrow * units // cols // deep
    highs, group, keys = cols // CORES, len(shared), len(shared) * tokens
    apart = (rows, highs, CORES)
    tail = 16
    lines = 8 + pre_sum.shape[1] // cols // deep
    assert lines <= tail and narrow <= deep
    count = 2 * (feed_rows // narrow) + 5
    height = 2 * feed_rows + 4 * narrow + tail
    steps = 4 + highs - 1 + rows - 1
    slots = min(count, steps)
    in_any = pl.BlockSpec(memory_space=pl.ANY)
    in_vmem = pl.BlockSpec(memory_space=pltpu.VMEM)
    ways = {2: 1}
    block = (rows, narrow, deep)
    dma = pltpu.SemaphoreType.DMA
    args = [ddown, act, x1_bf, dpre, dattn, query, mixed, log_total, x, weight, *shared]
    out, dx, _, _ = pl.pallas_call(
        functools.partial(low_kernel, highs=highs, rows=rows, group=group),
        in_specs=[in_any] * len(args) + [in_vmem] * 4,
        out_specs=[in_vmem, in_vmem, in_any, in_any],
        out_shape=[
            shaped((height, deep), F32),
            shaped((tokens, width), BF16),
            shaped((count, highs) + block, BF16),
            shaped((count, highs - 1, ways.get(highs, 2)) + block, BF16),
        ],
        scratch_shapes=[
            pltpu.VMEM((tokens, width), BF16),
            pltpu.VMEM((tokens, width), BF16),
            pltpu.VMEM((tokens, width), BF16),
            pltpu.VMEM((tokens, width), BF16),
            pltpu.VMEM(log_total.shape, F32),
            pltpu.VMEM((rows, cols, narrow, deep), BF16),
            pltpu.VMEM((rows, cols, 3 * narrow, deep), BF16),
            pltpu.VMEM((group, 2, tokens, width), BF16),
            pltpu.VMEM((tokens, width), BF16),
            pltpu.VMEM((keys, tokens), BF16),
            pltpu.VMEM((group - 1, 2, tokens, width), BF16),
            pltpu.VMEM((STAGES,) + apart + (narrow, deep), BF16),
            pltpu.VMEM(apart + (tail, deep), BF16),
            pltpu.VMEM((width, tokens), BF16),
            pltpu.VMEM((2, tokens, cols * deep), BF16),
            pltpu.VMEM((slots, highs) + block, BF16),
            pltpu.VMEM((2, highs) + block, BF16),
            pltpu.VMEM((2, ways.get(highs, 2)) + block, BF16),
            pltpu.VMEM((count, rows - 1, ways.get(rows, 2), narrow, deep), BF16),
            dma((9 + group,)),
            dma((2, cols)),
            dma((count, highs, 2)),
            dma((count, highs, 2)),
            dma((count, highs - 1, 2, 3)),
            dma((count, rows - 1, 2, 2)),
            dma((max(1, group - 1), 2)),
        ],
        name="low_back",
        compiler_params=pltpu.CompilerParams(collective_id=1, has_side_effects=True, vmem_limit_bytes=LOW_VMEM),
        cost_estimate=pl.CostEstimate(
            flops=64 * tokens * width * width, bytes_accessed=height * deep * rows * cols * 4, transcendentals=0
        ),
    )(*args, doc_query, doc_key, pre_sum, sums)
    return dx, out


class Spread:
    def __init__(self, axis, size):
        self.axis, self.size, self.here = axis, size, lax.axis_index(axis)

    def sends(self, step):
        last = self.size - 1
        return (
            (True, (self.here < last) & (self.here >= step - 1), self.here - step + 1),
            (False, (self.here > 0) & (self.here + step - 1 <= last), self.here + step - 1),
        )

    def gets(self, step):
        last = self.size - 1
        return ((True, self.here >= step), (False, self.here + step <= last))

    def neighbour(self, right):
        return {self.axis: self.here + (1 if right else -1)}


class Gather:
    def __init__(self, pieces, sems, highs, rows):
        self.pieces = pieces
        self.sem_row, self.sem_high, self.sem_core = sems
        self.row, self.high = Spread("row", rows), Spread("high", highs)
        self.core = lax.axis_index("core")
        self.sent = []

    def block(self, q, line, i):
        ref, first, count, row_first = self.pieces[q]
        some = pl.ds(first, count)
        if line is self.row:
            return ref.at[i, self.high.here if row_first else slice(None), self.core, some]
        return ref.at[slice(None) if row_first else self.row.here, i, self.core, some]

    def copy(self, q, line, step, right, i):
        sems = (self.sem_row if line is self.row else self.sem_high).at[q, step - 1, 0 if right else 1]
        ref = self.block(q, line, i)
        return pltpu.make_async_remote_copy(
            ref, ref, sems.at[0], sems.at[1], device_id=line.neighbour(right), device_id_type=MESH
        )

    def push(self, q, line, step):
        for right, there, i in line.sends(step):

            @pl.when(there)
            def _(right=right, i=i):
                self.copy(q, line, step, right, i).start()

            self.sent.append((q, line, step, right, there, i))

    def pull(self, q, line, step):
        for right, there in line.gets(step):

            @pl.when(there)
            def _(right=right):
                self.copy(q, line, step, right, line.here).wait_recv()

    def to_core(self, q):
        ref, first, count, _ = self.pieces[q]
        ref = ref.at[:, :, self.core, pl.ds(first, count)]
        return pltpu.make_async_remote_copy(
            ref, ref, self.sem_core.at[q, 0], self.sem_core.at[q, 1],
            device_id={"core": 1 - self.core}, device_id_type=MESH,
        )

    def stages(self, q):
        first, second = (self.row, self.high) if self.pieces[q][3] else (self.high, self.row)
        steps = [lambda: self.push(q, first, 1)]
        lines = [(first, i) for i in range(1, first.size)] + [(second, i) for i in range(1, second.size)]
        for n, (line, step) in enumerate(lines):

            def one(n=n, line=line, step=step):
                self.pull(q, line, step)
                if n + 1 < len(lines):
                    self.push(q, *lines[n + 1])
                else:
                    self.to_core(q).start()

            if n == len(lines) - 1:
                steps.append(lambda: None)
            steps.append(one)
        steps.append(lambda: self.to_core(q).wait())
        return steps

    def run(self, between):
        stages = [self.stages(q) for q in range(len(self.pieces))]
        depth, count = len(stages[0]), len(stages)
        for tick in range(count + depth - 1):
            for q in range(max(0, tick - depth + 1), min(tick + 1, count)):
                stages[q][tick - q]()
            between(tick, tick - depth + 1)

    def finish(self):
        for q, line, step, right, there, i in self.sent:

            @pl.when(there)
            def _(q=q, line=line, step=step, right=right, i=i):
                self.copy(q, line, step, right, i).wait_send()


class Group:
    def __init__(self, size):
        self.size = size
        self.place = lax.axis_index("row") * CORES + lax.axis_index("core")
        self.position = lax.rem(self.place, size)

    def member(self, step):
        other = self.place - self.position + lax.rem(self.position + step, self.size)
        return {"row": lax.div(other, CORES), "core": lax.rem(other, CORES)}

    def members(self):
        return [self.member(step) for step in range(1, self.size)]


class Front:
    def __init__(self, w, vectors, shift, x, q, kv, mixed, mask, x1, x1_bf, acc, log=None):
        self.w, self.vectors, self.shift, self.x, self.q, self.kv = w, vectors, shift, x, q, kv
        self.mixed, self.mask, self.x1, self.x1_bf, self.acc, self.log = mixed, mask, x1, x1_bf, acc, log
        self.tokens, self.width = x.shape
        self.rows, self.highs, _, _, self.deep = w.shape
        self.cols = self.highs * CORES
        self.narrow = self.width // self.rows
        self.group = kv.shape[0]
        self.pairs = self.width // PAIR
        self.blocks = shift.shape[1] // self.cols // self.deep

    def matrix(self, block, k):
        at = pl.ds(block * self.narrow, self.narrow)
        return self.w[:, k // CORES, k % CORES, at].reshape(self.width, self.deep)

    def project(self, j):
        take = row_blocks(self.rows, self.narrow)
        for r in range(0, self.rows, take):
            at = slice(r * self.narrow, (r + take) * self.narrow)
            some = pl.ds((QKV + j) * self.narrow, self.narrow)
            weight = jnp.concatenate(
                [
                    self.w[r : r + take, k // CORES, k % CORES, some].reshape(take * self.narrow, self.deep)
                    for k in range(self.cols)
                ],
                axis=1,
            )
            out = nt(self.x[...], weight)
            if j == 0:
                self.q[:, at] = ((out + self.vectors[0:1, at]) * HD**-0.5).astype(BF16)
            elif j == 1:
                self.kv[0, 0, :, at] = out.astype(BF16)
            else:
                self.kv[0, 1, :, at] = (out + self.vectors[1:2, at]).astype(BF16)

    def attend(self, first, count):
        @pl.loop(first, first + count)
        def _(p):
            at = pl.ds(pl.multiple_of(p * PAIR, PAIR), PAIR)
            keys = jnp.concatenate([self.kv[i, 0, :, at] for i in range(self.group)], axis=0)
            values = jnp.concatenate([self.kv[i, 1, :, at] for i in range(self.group)], axis=0)
            mixed, log_rows = pair_front(self.q[:, at], keys, values, self.mask)
            self.mixed[:, at] = mixed
            if self.log is not None:
                for h in range(2):
                    self.log[p, h : h + 1] = log_rows[h]

    def out(self):
        for k in range(self.cols):
            at = slice(k * self.deep, (k + 1) * self.deep)
            self.acc[:, at] = nn(self.mixed[...], self.matrix(OUT, k))

    def norm_one(self, keep=None):
        def some(at):
            attn = self.acc[at] + self.vectors[2:3]
            normed, scale = normed_of(self.x[at].astype(F32) + attn)
            x1 = normed * self.vectors[6:7] + self.vectors[3:4]
            self.x1[at] = x1
            self.x1_bf[at] = x1.astype(BF16)
            if keep is not None:
                keep(at, normed, scale)

        by_tokens(self.tokens, some)

    def feed(self, block, ks, start, keep=None, at=slice(None)):
        up = jnp.concatenate([self.matrix(UNIT + block, k) for k in ks], axis=1)
        down = jnp.concatenate([self.matrix(UNIT + self.blocks + block, k) for k in ks], axis=1)
        hidden = self.blocks * self.deep
        begins = [k * hidden + block * self.deep for k in ks]
        shift = jnp.concatenate([self.shift[:, b : b + self.deep] for b in begins], axis=1)
        act, slope = gelu_parts(nn(self.x1_bf[at], up) + shift)
        act = act.astype(BF16)
        if keep is not None:
            keep(act, slope.astype(BF16))
        more = nt(act, down)
        if start:
            self.acc[at] = more
        else:
            self.acc[at] += more

    def norm_two(self, at, keep=None):
        normed, scale = normed_of(self.x1[at] + (self.acc[at] + self.vectors[4:5]))
        if keep is not None:
            keep(at, normed, scale)
        return normed * self.vectors[7:8] + self.vectors[5:6]


def share_keys(group, kv, sems):
    def copy(step):
        return pltpu.make_async_remote_copy(
            kv.at[0], kv.at[step], sems.at[step - 1, 0], sems.at[step - 1, 1],
            device_id=group.member(step), device_id_type=MESH,
        )

    return [copy(step) for step in range(1, group.size)]


def first_kernel(*refs, highs, rows, group, micro, seq_here, seq_len):
    (small_ref, tokens_hbm, cot_hbm, qkv_ref, out_ref, unit_ref, down_ref) = refs[:7]
    (next_hbm, start_ref, w_hbm, vectors, shift, doc_q, doc_k) = refs[7:14]
    (w, small, turned, x, q, kv, mixed, mask, x1, x1_bf, acc, y,
     sem_row, sem_high, sem_core, sem_x, sem_kv, sem_y, sem_w, sem_next) = refs[14:]
    tokens, width = x.shape
    narrow, deep = width // rows, w.shape[-1]
    cols = highs * CORES
    hidden = unit_ref.shape[2]
    blocks = hidden // deep
    row, high, core = lax.axis_index("row"), lax.axis_index("high"), lax.axis_index("core")
    section = lax.axis_index("section")
    sharing = Group(group)
    sequence = lax.div(sharing.place, group)
    front = Front(w, vectors, shift, x, q, kv, mixed, mask, x1, x1_bf, acc)

    w[row, high, core, 0 : 3 * narrow] = qkv_ref[0].reshape(3 * narrow, deep).astype(BF16)
    w[row, high, core, 3 * narrow : 4 * narrow] = out_ref[0].astype(BF16)
    for i in range(blocks):
        at = slice(i * deep, (i + 1) * deep)
        for j, ref in enumerate((unit_ref, down_ref)):
            first = (UNIT + j * blocks + i) * narrow
            w[row, high, core, first : first + narrow] = ref[0, :, at].astype(BF16)
    small[row, high, core] = small_ref[...]

    def goes(j):
        place = ((j // group) * CORES + core) * group + j % group
        return lax.div(place, CORES), lax.rem(place, CORES)

    source_core = lax.rem(sequence, CORES)
    mine_too = source_core == core

    def block_of(ref, j):
        m, rest = divmod(j // group, seq_here)
        return ref.at[m, :, pl.ds(rest * seq_len + (j % group) * tokens, tokens)]

    def send_block(ref, j):
        there_row, there_core = goes(j)
        return pltpu.make_async_remote_copy(
            block_of(ref, j), turned.at[row], sem_x.at[j, 0], sem_x.at[row, 1],
            device_id={"row": there_row, "core": there_core}, device_id_type=MESH,
        )

    def is_here(j):
        there_row, there_core = goes(j)
        return (there_row == row) & (there_core == core)

    barrier = pltpu.get_barrier_semaphore()
    count = 0
    for line in (Spread("row", rows), Spread("high", highs)):
        for right, there in ((True, line.here < line.size - 1), (False, line.here > 0)):

            @pl.when(there)
            def _(line=line, right=right):
                pl.semaphore_signal(barrier, 1, device_id=line.neighbour(right), device_id_type=MESH)

            count = count + there.astype(jnp.int32)
    others = [{"core": 1 - core}, {"section": 1 - section}] + sharing.members()
    for other in others:
        pl.semaphore_signal(barrier, 1, device_id=other, device_id_type=MESH)
    for r in range(rows):

        @pl.when(jnp.logical_not(mine_too & (row == r)))
        def _(r=r):
            pl.semaphore_signal(barrier, 1, device_id={"row": r, "core": source_core}, device_id_type=MESH)

    pl.semaphore_wait(barrier, count + len(others) + rows - mine_too.astype(jnp.int32))

    row_first = [True] * (4 + 2 * blocks)
    for i in (4, 4 + blocks):
        row_first[i] = False
    order = [0, 1, 2, 3] + [UNIT + j * blocks + i for i in range(blocks) for j in range(2)]
    pieces = [(small, 0, small.shape[3], True)]
    pieces += [(w, i * narrow, narrow, row_first[n]) for n, i in enumerate(order)]
    gather = Gather(pieces, (sem_row, sem_high, sem_core), highs, rows)

    def to_hbm(q):
        at = pl.ds(order[q - 1] * narrow, narrow)
        return pltpu.make_async_copy(w.at[:, :, :, at], w_hbm.at[:, :, :, at], sem_w.at[q])

    keys = share_keys(sharing, kv, sem_kv)

    def begin():
        for j in range(rows):
            for which, ref in ((0, tokens_hbm), (1, cot_hbm)):

                @pl.when((section == which) & is_here(j))
                def _(ref=ref, j=j):
                    pltpu.make_async_copy(block_of(ref, j), turned.at[row], sem_x.at[row, 1]).start()

                @pl.when((section == which) & jnp.logical_not(is_here(j)))
                def _(ref=ref, j=j):
                    send_block(ref, j).start()

    def use_small():
        for r in range(rows):
            vectors[:, r * narrow : (r + 1) * narrow] = small[r, 0, 0, 0:8, 0:narrow]
        for k in range(cols):
            for i in range(blocks):
                at = k * hidden + i * deep
                shift[:, at : at + deep] = small[0, k // CORES, k % CORES, 8 + i : 9 + i]
        lines = tokens // deep
        for slot in range(group):
            part = lax.rem(sharing.position + group - slot, group)
            base = 8 + blocks + (lax.div(sequence, CORES) * group + part) * lines
            doc = jnp.concatenate([small[row, high, source_core, pl.ds(base + i, 1)] for i in range(lines)], axis=1)
            if slot == 0:
                doc_q[...] = doc
            doc_k[slot * tokens : (slot + 1) * tokens] = jnp.broadcast_to(doc, (128, tokens)).T[:, :1]
        mask[...] = jnp.where(doc_k[...] == doc_q[...], 0.0, NEG_BIG)

    def turn():
        for r in range(rows):
            pltpu.make_async_copy(turned.at[r], turned.at[r], sem_x.at[r, 1]).wait()
        for r in range(rows):
            x[:, r * narrow : (r + 1) * narrow] = turned[r].T
        start_ref[...] = x[...]

    half = max(1, cols // 2)
    chunks = min(4, tokens // 8)
    chunk = tokens // chunks

    def send_out(i):
        at = pl.ds(i * chunk, chunk)
        return pltpu.make_async_remote_copy(
            y.at[at], next_hbm.at[at], sem_y.at[i, 0], sem_y.at[i, 1],
            device_id={"section": 1 - section}, device_id_type=MESH,
        )

    stay = pltpu.make_async_copy(x, next_hbm, sem_next.at[0])
    base = 3

    def between(tick, done):
        if done >= 1:
            to_hbm(done).start()
        if done == 0:
            use_small()
        if done == 1:
            turn()

            @pl.when(section == 0)
            def _():
                stay.start()

            front.project(0)
        if done == 2:
            front.project(1)
        if done == base:
            front.project(2)
            for copy in keys:
                copy.start()
        if done == base + 1:
            for copy in keys:
                copy.wait()
        if base + 1 <= done < base + 5:
            front.attend((done - base - 1) * (front.pairs // 4), front.pairs // 4)
        if done == base + 5:
            front.out()
            front.norm_one()
        if done >= base + 5:
            first = done == base + 5
            ready = (done - 4) // 2
            from_block = 0 if first else (done - 1 - 4) // 2
            for block in range(from_block, min(ready, blocks)):
                if block < blocks - 1:
                    for k in range(0, cols, half):
                        front.feed(block, range(k, k + half), block == 0 and k == 0)

    begin()
    gather.run(between)
    for i in range(chunks):
        at = pl.ds(i * chunk, chunk)
        for k in range(0, cols, half):
            front.feed(blocks - 1, range(k, k + half), blocks == 1 and k == 0, at=at)
        y[at] = front.norm_two(at).astype(BF16)

        @pl.when(section == 0)
        def _(i=i):
            send_out(i).start()

    gather.finish()
    for j in range(rows):

        @pl.when(jnp.logical_not(is_here(j)))
        def _(j=j):
            send_block(tokens_hbm, j).wait_send()

    for q in range(1, len(pieces)):
        to_hbm(q).wait()

    @pl.when(section == 0)
    def _():
        stay.wait()
        for i in range(chunks):
            send_out(i).wait_send()

    @pl.when(section == 1)
    def _():
        for i in range(chunks):
            send_out(i).wait_recv()


def first_forward(small, tokens_in, cotangent, qkv, out, unit, down, rows, highs, group, seq_here, seq_len):
    micro, narrow, _ = tokens_in.shape
    deep, hidden = out.shape[2], unit.shape[2]
    width, cols, blocks = narrow * rows, highs * CORES, hidden // deep
    tokens = seq_len // group
    tall = (4 + 2 * blocks) * narrow
    apart = (rows, highs, CORES)
    in_any = pl.BlockSpec(memory_space=pl.ANY)
    in_vmem = pl.BlockSpec(memory_space=pltpu.VMEM)
    count = 1 + 4 + 2 * blocks
    dma = pltpu.SemaphoreType.DMA
    flat, flat_f32 = pltpu.VMEM((tokens, width), BF16), pltpu.VMEM((tokens, width), F32)
    return pl.pallas_call(
        functools.partial(
            first_kernel, highs=highs, rows=rows, group=group, micro=micro, seq_here=seq_here, seq_len=seq_len
        ),
        in_specs=[in_vmem, in_any, in_any] + [in_vmem] * 4,
        out_specs=[in_any, in_vmem, in_any] + [in_vmem] * 4,
        out_shape=[
            shaped((tokens, width), BF16),
            shaped((tokens, width), BF16),
            shaped(apart + (tall, deep), BF16),
            shaped((8, width), F32),
            shaped((1, hidden * cols), F32),
            shaped((1, tokens), F32),
            shaped((group * tokens, 1), F32),
        ],
        scratch_shapes=[
            pltpu.VMEM(apart + (tall, deep), BF16),
            pltpu.VMEM(apart + small.shape, F32),
            pltpu.VMEM((rows, narrow, tokens), BF16),
            flat,
            flat,
            pltpu.VMEM((group, 2, tokens, width), BF16),
            flat,
            pltpu.VMEM((group * tokens, tokens), F32),
            flat_f32,
            flat,
            flat_f32,
            flat,
            dma((count, rows - 1, 2, 2)),
            dma((count, highs - 1, 2, 2)),
            dma((count, 2)),
            dma((rows, 2)),
            dma((max(1, group - 1), 2)),
            dma((4, 2)),
            dma((count,)),
            dma((1,)),
        ],
        name="first_forward",
        compiler_params=pltpu.CompilerParams(collective_id=2, has_side_effects=True, vmem_limit_bytes=LOW_VMEM),
        cost_estimate=pl.CostEstimate(
            flops=24 * tokens * width * width, bytes_accessed=2 * tall * deep * rows * cols, transcendentals=0
        ),
    )(small, tokens_in, cotangent, qkv, out, unit, down)


def local(tokens_in, doc_ids, cotangent, qkv_master, out_master, unit_master, down_master, unit_bias, width_bias, norm_gain):
    at = Layout(tokens_in, doc_ids)
    section = lax.axis_index("section")
    rows, cols, width, narrow = at.rows, at.cols, at.width, at.narrow
    deep, hidden = out_master.shape[2], unit_master.shape[2]

    vectors = jnp.concatenate([width_bias[0], norm_gain[0]])
    vectors = jnp.pad(vectors, ((0, 0), (0, deep - narrow)))
    small = jnp.concatenate([vectors, unit_bias.reshape(-1, deep), doc_ids.astype(F32).reshape(-1, deep)])
    small = jnp.pad(small, ((0, -small.shape[0] % 8), (0, 0)))
    second_in, start, weights, vectors, unit_shift, doc_query, doc_key = first_forward(
        small, tokens_in, cotangent, qkv_master, out_master, unit_master, down_master, rows, cols // CORES, at.group,
        at.seq_here, at.seq_len,
    )
    weights = weights.reshape(rows, cols, -1, deep)
    bias, gain = vectors[:6], vectors[6:]
    kv_bias = jnp.stack([jnp.zeros_like(bias[1]), bias[1]])[:, None]

    def forward(layer_in, saving):
        kv = project(layer_in, weights, kv_bias, 1, 2, 1.0)
        shared = at.share(kv)
        query = project(layer_in, weights, bias[0:1][None], 0, 1, HD**-0.5)
        mixed, log_total = attend(query, shared, doc_query, doc_key)
        x1, x1_bf, hat_one, scale_one = out_norm(mixed, weights, layer_in, bias, gain)
        y, *rest = feed(x1_bf, weights, unit_shift, x1, bias, gain, saving)
        return y, (layer_in, query, shared, mixed, log_total, x1_bf, hat_one, scale_one, *rest)

    def backward(dy, saved, weights_too):
        layer_in, query, shared, mixed, log_total, x1_bf, hat_one, scale_one, act, slope, hat_two, scale_two = saved
        dh2, ddown, *top = top_back(dy, hat_two, scale_two, gain, weights_too)
        dattn, *fed = feed_back(dh2, ddown, hat_one, scale_one, slope, weights, gain, weights_too)
        if not weights_too:
            dmixed = mixed_back(dattn, weights)
            dq, dkv = attend_back(query, dmixed, mixed, log_total, shared, doc_query, doc_key)
            others = at.give_back([dkv[j] for j in range(at.group)])
            return input_back(dq, dkv, others, weights, dattn)
        (top_sums,), (dpre, pre_sum, feed_sums) = top, fed
        sums = jnp.concatenate([feed_sums[:2], top_sums[:2], feed_sums[2:3], top_sums[2:3]])
        return low_back(
            ddown, act, x1_bf, dpre, dattn, query, mixed, log_total, layer_in, weights, shared, doc_query, doc_key,
            pre_sum, sums,
        )

    layer_out, saved = forward(second_in, True)
    early_grad = backward(start, saved, False)
    passed = lax.ppermute(early_grad, "section", [(1, 0)])
    input_grad, total = backward(jnp.where(section == 0, passed, start), saved, True)

    def whole_columns(grad):
        return grad.reshape(-1, narrow, deep).transpose(1, 0, 2).reshape(narrow, hidden)

    feed_rows = narrow * hidden // deep
    heights = (feed_rows, narrow, feed_rows, 3 * narrow, 16)
    ends = [0]
    for height in heights:
        ends.append(ends[-1] + height)
    down_sum, out_sum, unit_sum, qkv_sum, sums = (total[a:b] for a, b in zip(ends, ends[1:]))
    vectors, pre_sum = sums[:8, :narrow], sums[8 : 8 + hidden // deep].reshape(-1)
    layer_out = at.to_features(layer_out).astype(F32)
    input_grad = at.to_features(input_grad).astype(F32)
    return (
        layer_out[None],
        input_grad[None],
        qkv_sum.reshape(qkv_master.shape),
        out_sum[None],
        whole_columns(unit_sum)[None],
        whole_columns(down_sum)[None],
        pre_sum[None],
        vectors[:6][None],
        vectors[6:][None],
    )


def solution(mesh):
    sections, rows, cols = (mesh.shape[name] for name in ("section", "row", "col"))
    fine = Mesh(
        mesh.devices.reshape(sections, rows, cols // CORES, CORES), ("section", "row", "high", "core")
    )
    col = ("high", "core")
    block = P("section", "row", col)
    stream = P("section", None, "row", col)
    return jax.shard_map(
        local,
        mesh=fine,
        in_specs=(
            P(None, "row", col),
            P(None, col, None),
            P(None, "row", col),
            P("section", None, "row", col),
            block,
            block,
            block,
            P("section", col),
            P("section", None, "row"),
            P("section", None, "row"),
        ),
        out_specs=(
            stream,
            stream,
            stream,
            block,
            block,
            block,
            P("section", col),
            P("section", None, "row"),
            P("section", None, "row"),
        ),
        check_vma=False,
    )
```

time: 1210 us -> 630 us (0.52)
  Pallas kernels: 0 us -> 515 us
  matrix products: 375 us -> 0 us
  waiting for transfers between devices: 255 us -> 30.1 us
  local copies, waits for them, and re-layouts: 251 us -> 41.2 us
  other arithmetic: 175 us -> 8.71 us
  blocking collectives: 98 us -> 0 us
  between operations: 15.8 us -> 1.41 us
    pallas_call x0 -> x14, Pallas kernels: none -> 515 us  [the longest x1 196 us: first_forward(): pl.pallas_call(functools.partial(first_kernel, highs=highs, rows=rows, gr...]
    dot_general x30 -> x0, matrix products: 375 us -> none  [dot(): return jnp.einsum(pattern, left, right, preferred_element_type=F32)]
    reduce_scatter x4 -> x0, waiting for transfers between devices: 121 us -> none  [the longest x3 121 us: scattered(): lax.psum_scatter(blocks, PLANE, scatter_dimension=0, tiled=True)[0]]
    reshape x12 -> x2, local copies, waits for them, and re-layouts: 96.4 us -> 0.02 us  [the longest x1 0.01 us: local(): doc_ids.astype(F32).reshape(-1, deep)]
    convert_element_type x16 -> x3, other arithmetic: 80.3 us -> 1.28 us  [the longest x1 0.73 us: local(): doc_ids.astype(F32).reshape(-1, deep)]
    ppermute x15 -> x2, waiting for transfers between devices: 81.3 us -> 3.79 us  [the longest x1 3.79 us: give_back(): lax.ppermute(blocks[step], ('row', 'core'), self.within(self.group - step))]
    psum x1 -> x0, blocking collectives: 54.1 us -> none  [local(): pre_sum, sums = lax.psum((pre_sum, sums), PLANE)]
    all_gather x2 -> x0, blocking collectives: 43.9 us -> none  [the longest x1 37 us: local(): lax.all_gather(jnp.concatenate([width_bias[0], norm_gain[0]]), 'row', axi...]
  transfers between devices with their start and end apart: 35 -> 11, of which waited for: 10 -> 6; matrix products, arithmetic and copies ran while one was open for 39% -> 3% of each run, Pallas kernels for 0% -> 1%
where the time goes in v2:
time: 630 us; the launch traced here: 619 us
  Pallas kernels  515 us (82%)
  local copies, waits for them, and re-layouts  41.2 us (7%)
  waiting for transfers between devices  30.1 us (5%)
  starting transfers between devices  22.2 us (4%)
  other arithmetic  8.71 us (1%)
    pallas_call x1, Pallas kernels, first_forward(): pl.pallas_call(functools.partial(first_kernel, highs=highs, rows=rows, gr...  196 us
    pallas_call x1, Pallas kernels, low_back(): pl.pallas_call(functools.partial(low_kernel, highs=highs, rows=rows, grou...  174 us
    pallas_call x12, Pallas kernels, call(): pl.pallas_call(kernel, grid=grid, in_specs=in_specs, out_specs=out_specs,...  145 us
    ppermute x8, waiting for transfers between devices, to_features(): got.append(lax.ppermute(block, ('row', 'core'), pairs))  26.3 us
    ppermute x8, starting transfers between devices, to_features(): got.append(lax.ppermute(block, ('row', 'core'), pairs))  20.2 us
  transfers between devices with their start and end apart: 11, of which 6 were waited for; matrix products, arithmetic and copies ran while one was open for 3% of the time, Pallas kernels for 1%

profile of v2, /device:TPU:10, one launch (start us, length us, event | category | flops | bytes accessed | tf_op | source)
XLA Modules:
  0.0 619.0 jit_solution(5732260105398702775)
XLA Ops:
  5.3 196.4 %first_forward.1 = (bf16[512,1024]{1,0:T(8,128)(2,1)}, bf16[512,1024]{1,0:T(8,128)(2,1)}, bf16[4,2,2,3072,256]{4,3,2,1,0:T(8,128)(2,1)}, f32[8,1024]{1,0:T(8,128...) custom-call(f32[24,256]{1,0:T(8,128)} %select_maximum_fusion.refs_0_, bf16[2,256,1024]{2,1,0:T(8,128)(2,1)} %refs_1_.1, ...), custom_call_target="tpu_custom_call" | custom-call | flops 12884901888 | bytes 25165824 | tf_op jit(solution)/shard_map/first_forward/pallas_call | solution.py:1552
  203.7 8.2 %project.3.refs_1_.refs_4_.refs_10_ = bf16[2,512,1024]{2,1,0:T(8,128)(2,1)} custom-call(bf16[512,1024]{1,0:T(8,128)(2,1)} %get-tuple-element.41.x_ref.refs_8_, bf16[4,4,3072,256]{3,2,1,0:T(8,128)(2,1)} %bitcast.65, f32[2,1,1024]{2,1,0:T(1,128)} %broadcast_in_dim.27.b_ref), custom_call_target="tpu_custom_call" | custom-call | flops 2147483648 | bytes 4194304 | tf_op jit(solution)/shard_map/project/pallas_call | solution.py:37
  213.2 4.8 project.2.refs_0_.refs_5_
  219.4 18.2 %attend.1 = (bf16[512,1024]{1,0:T(8,128)(2,1)}, f32[8,2,512]{2,1,0:T(2,128)}) custom-call(bf16[1,512,1024]{2,1,0:T(8,128)(2,1)} %project.2.refs_0_.refs_5_, bf16[2,512,1024]{2,1,0:T(8,128)(2,1)} %project.3.refs_1_.refs_4_.refs_10_, bf16[2,512,1024]{2,1,0:T(8,128)(2,1)} %copy-done.7, f32[1,512]{1,0:T(1,128)} %get-tuple-element.44.refs_3_.refs_6_.refs_12_, ...), custom_call_target="tpu_custom_call" | custom-call | flops 8589934592 | bytes 5242880 | tf_op jit(solution)/shard_map/attend/pallas_call | solution.py:37
  237.5 7.5 %out_norm.1 = (f32[512,1024]{1,0:T(8,128)}, bf16[512,1024]{1,0:T(8,128)(2,1)}, f32[512,1024]{1,0:T(8,128)}, f32[512,128]{1,0:T(8,128)}) custom-call(bf16[512,1024]{1,0:T(8,128)(2,1)} %get-tuple-element.46.m_ref.refs_2_.refs_6_, bf16[4,4,3072,256]{3,2,1,0:T(8,128)(2,1)} %bitcast.67, bf16[512,1024]{1,0:T(8,128)(2,1)} %get-tuple-element.41.x_ref.refs_8_, ...), custom_call_target="tpu_custom_call" | custom-call | flops 1073741824 | bytes 8388608 | tf_op jit(solution)/shard_map/out_norm/pallas_call | solution.py:37
  245.1 19.9 %feed.1 = (bf16[512,1024]{1,0:T(8,128)(2,1)}, bf16[512,4096]{1,0:T(8,128)(2,1)}, bf16[512,4096]{1,0:T(8,128)(2,1)}, f32[512,1024]{1,0:T(8,128)}, f32[512,128]{1,0:T(8,128)}) custom-call(bf16[512,1024]{1,0:T(8,128)(2,1)} %get-tuple-element.47.xb_ref.refs_2_, bf16[4,4,3072,256]{3,2,1,0:T(8,128)(2,1)} %bitcast.68, bf16[4,4,3072,256]{3,2,1,0:T(8,128)(2,1)} %bitcast.69, ...), custom_call_target="tpu_custom_call" | custom-call | flops 8589934592 | bytes 16777216 | tf_op jit(solution)/shard_map/feed/pallas_call | solution.py:37
  265.0 4.5 top_back.2
  269.4 18.0 %feed_back.2.g_ref.refs_4_ = bf16[512,1024]{1,0:T(8,128)(2,1)} custom-call(f32[512,1024]{1,0:T(8,128)} %get-tuple-element.54.refs_0_, bf16[512,1024]{1,0:T(8,128)(2,1)} %get-tuple-element.55.refs_1_, f32[512,1024]{1,0:T(8,128)} %get-tuple-element.56.refs_2_, f32[512,128]{1,0:T(8,128)} %get-tuple-element.57.refs_3_, ...), custom_call_target="tpu_custom_call" | custom-call | flops 8589934592 | bytes 16777216 | tf_op jit(solution)/shard_map/feed_back/pallas_call | solution.py:37
  287.5 4.9 mixed_back.1.refs_1_
  292.3 25.7 %attend_back.1 = (bf16[512,1024]{1,0:T(8,128)(2,1)}, bf16[2,2,512,1024]{3,2,1,0:T(8,128)(2,1)}) custom-call(bf16[1,512,1024]{2,1,0:T(8,128)(2,1)} %project.2.refs_0_.refs_5_, bf16[512,1024]{1,0:T(8,128)(2,1)} %mixed_back.1.refs_1_, bf16[512,1024]{1,0:T(8,128)(2,1)} %get-tuple-element.46.m_ref.refs_2_.refs_6_, ...), custom_call_target="tpu_custom_call" | custom-call | flops 21474836480 | bytes 10485760 | tf_op jit(solution)/shard_map/attend_back/pallas_call | solution.py:37
  320.4 3.8 collective-permute-done.5.refs_2_
  325.5 9.0 %input_back.1 = bf16[512,1024]{1,0:T(8,128)(2,1)} custom-call(bf16[512,1024]{1,0:T(8,128)(2,1)} %get-tuple-element.60.refs_0_, bf16[2,2,512,1024]{3,2,1,0:T(8,128)(2,1)} %get-tuple-element.61.refs_1_, bf16[2,512,1024]{2,1,0:T(8,128)(2,1)} %copy-done.2, bf16[4,4,3072,256]{3,2,1,0:T(8,128)(2,1)} %bitcast.73, bf16[512,1024]{1,0:T(8,128)(2,1)} %feed_back.2.g_ref.refs_4_), custom_call_target="tpu_custom_call" | custom-call | flops 3221225472 | bytes 6291456 | tf_op jit(solution)/shard_map/input_back/pallas_call | solution.py:37
  337.1 9.2 %collective-permute-start.3 = (bf16[256,512]{1,0:T(8,128)(2,1)S(1)}, bf16[256,512]{1,0:T(8,128)(2,1)S(1)}, u32[]{:S(2)}, u32[]{:S(2)}) collective-permute-start(bf16[256,512]{1,0:T(8,128)(2,1)S(1)} %get-tuple-element.107), channel_id=1, source_target_pairs={{8,0},{12,1},{9,4},{13,5},{0,8},{4,9},{1,12},{5,13},{10,2},{14,3},... | collective-permute-start | bytes 786440 | tf_op jit(solution)/shard_map/ppermute | solution.py:594
  347.5 4.0 collective-permute-start.1
  352.1 16.7 %collective-permute-done.3 = bf16[256,512]{1,0:T(8,128)(2,1)S(1)} collective-permute-done((bf16[256,512]{1,0:T(8,128)(2,1)S(1)}, bf16[256,512]{1,0:T(8,128)(2,1)S(1)}, u32[]{:S(2)}, u32[]{:S(2)}) %collective-permute-start.3) | collective-permute-done | bytes 262176 | tf_op jit(solution)/shard_map/ppermute | solution.py:594
  374.9 4.9 top_back.3
  381.3 19.4 %feed_back.3 = (bf16[512,1024]{1,0:T(8,128)(2,1)}, bf16[512,4096]{1,0:T(8,128)(2,1)}, f32[1,4096]{1,0:T(1,128)}, f32[8,1024]{1,0:T(8,128)}) custom-call(f32[512,1024]{1,0:T(8,128)} %get-tuple-element.64.refs_0_, bf16[512,1024]{1,0:T(8,128)(2,1)} %get-tuple-element.62.refs_1_.refs_0_, f32[512,1024]{1,0:T(8,128)} %get-tuple-element.56.refs_2_, ...), custom_call_target="tpu_custom_call" | custom-call | flops 8589934592 | bytes 16777216 | tf_op jit(solution)/shard_map/feed_back/pallas_call | solution.py:37
  402.8 174.2 %low_back.1 = (f32[3088,256]{1,0:T(8,128)}, bf16[512,1024]{1,0:T(8,128)(2,1)}, bf16[13,2,4,256,256]{4,3,2,1,0:T(8,128)(2,1)}, bf16[13,1,1,4,256,256]{5,4,3,2,1,0:T(8,128)(2,1)}) custom-call(bf16[512,1024]{1,0:T(8,128)(2,1)} %get-tuple-element.62.refs_1_.refs_0_, bf16[512,4096]{1,0:T(8,128)(2,1)} %get-tuple-element.63.refs_1_, ...), custom_call_target="tpu_custom_call" | custom-call | flops 34359738368 | bytes 50593792 | tf_op jit(solution)/shard_map/low_back/pallas_call | solution.py:1079
  582.5 2.6 collective-permute-start.9
  585.1 2.9 collective-permute-start.7
  589.2 2.1 slice.65
  598.5 7.6 %collective-permute-done.9 = bf16[256,512]{1,0:T(8,128)(2,1)} collective-permute-done((bf16[256,512]{1,0:T(8,128)(2,1)}, bf16[256,512]{1,0:T(8,128)(2,1)}, u32[]{:S(2)}, u32[]{:S(2)}) %collective-permute-start.9) | collective-permute-done | bytes 262176 | tf_op jit(solution)/shard_map/ppermute | solution.py:594
  610.7 2.9 copy.45
  615.7 2.9 copy.46
  (76 shorter events, 47.6 us)
Async XLA Ops:
  211.8 6.2 %collective-permute-start = (bf16[2,512,1024]{2,1,0:T(8,128)(2,1)}, bf16[2,512,1024]{2,1,0:T(8,128)(2,1)S(1)}, u32[]{:S(2)}, u32[]{:S(2)}) collective-permute-start(bf16[2,512,1024]{2,1,0:T(8,128)(2,1)} %project.3.refs_1_.refs_4_.refs_10_), channel_id=1, source_target_pairs={{0,1},{1,0},{4,5},{5,4},{8,9},{9,8},{12,13},{13,12},{2,3},{3,2},{6... | collective-permute-start | bytes 6291464 | tf_op jit(solution)/shard_map/ppermute | solution.py:608
  218.0 1.3 copy-start.7
  319.8 4.4 collective-permute-start.5
  324.2 1.3 copy-start.2
  325.5 10.6 %copy-start.3 = (bf16[512,1024]{1,0:T(8,128)(2,1)S(1)}, bf16[512,1024]{1,0:T(8,128)(2,1)}, u32[]{:S(2)}) copy-start(bf16[512,1024]{1,0:T(8,128)(2,1)} %get-tuple-element.50) | copy-start | bytes 3145732
  334.5 39.3 %collective-permute-start.6 = (bf16[512,1024]{1,0:T(8,128)(2,1)}, bf16[512,1024]{1,0:T(8,128)(2,1)S(1)}, u32[]{:S(2)}, u32[]{:S(2)}) collective-permute-start(bf16[512,1024]{1,0:T(8,128)(2,1)} %input_back.1), channel_id=1, source_target_pairs={{16,0},{17,1},{18,2},{19,3},{20,4},{21,5},{22,6},{23,7},{24,8},{25... | collective-permute-start | bytes 3145736 | tf_op jit(solution)/shard_map/ppermute | solution.py:1642
  336.7 15.4 %collective-permute-start.4 = (bf16[256,512]{1,0:T(8,128)(2,1)S(1)}, bf16[256,512]{1,0:T(8,128)(2,1)S(1)}, u32[]{:S(2)}, u32[]{:S(2)}) collective-permute-start(bf16[256,512]{1,0:T(8,128)(2,1)S(1)} %get-tuple-element.106), channel_id=1, source_target_pairs={{9,0},{13,1},{0,4},{4,5},{1,8},{5,9},{8,12},{12,13},{11,2},{15,3},... | collective-permute-start | bytes 786440 | tf_op jit(solution)/shard_map/ppermute | solution.py:594
  337.1 31.7 %collective-permute-start.3 = (bf16[256,512]{1,0:T(8,128)(2,1)S(1)}, bf16[256,512]{1,0:T(8,128)(2,1)S(1)}, u32[]{:S(2)}, u32[]{:S(2)}) collective-permute-start(bf16[256,512]{1,0:T(8,128)(2,1)S(1)} %get-tuple-element.107), channel_id=1, source_target_pairs={{8,0},{12,1},{9,4},{13,5},{0,8},{4,9},{1,12},{5,13},{10,2},{14,3},... | collective-permute-start | bytes 786440 | tf_op jit(solution)/shard_map/ppermute | solution.py:594
  346.3 23.8 %collective-permute-start.2 = (bf16[256,512]{1,0:T(8,128)(2,1)S(1)}, bf16[256,512]{1,0:T(8,128)(2,1)S(1)}, u32[]{:S(2)}, u32[]{:S(2)}) collective-permute-start(bf16[256,512]{1,0:T(8,128)(2,1)S(1)} %get-tuple-element.108), channel_id=1, source_target_pairs={{1,0},{5,1},{8,4},{12,5},{9,8},{13,9},{0,12},{4,13},{3,2},{7,3},{1... | collective-permute-start | bytes 786440 | tf_op jit(solution)/shard_map/ppermute | solution.py:594
  347.5 22.6 %collective-permute-start.1 = (bf16[256,512]{1,0:T(8,128)(2,1)S(1)}, bf16[256,512]{1,0:T(8,128)(2,1)S(1)}, u32[]{:S(2)}, u32[]{:S(2)}) collective-permute-start(bf16[256,512]{1,0:T(8,128)(2,1)S(1)} %get-tuple-element.105), channel_id=1, source_target_pairs={{0,0},{4,1},{1,4},{5,5},{8,8},{12,9},{9,12},{13,13},{2,2},{6,3},{3... | collective-permute-start | bytes 786440 | tf_op jit(solution)/shard_map/ppermute | solution.py:594
  368.8 1.2 copy-start.4
  370.0 0.7 copy-start.5
  370.0 0.8 copy-start.6
  370.8 3.0 copy-start.1
  582.5 16.1 %collective-permute-start.10 = (bf16[256,512]{1,0:T(8,128)(2,1)}, bf16[256,512]{1,0:T(8,128)(2,1)}, u32[]{:S(2)}, u32[]{:S(2)}) collective-permute-start(bf16[256,512]{1,0:T(8,128)(2,1)} %get-tuple-element.102), channel_id=1, source_target_pairs={{9,0},{13,1},{0,4},{4,5},{1,8},{5,9},{8,12},{12,13},{11,2},{15,3},... | collective-permute-start | bytes 786440 | tf_op jit(solution)/shard_map/ppermute | solution.py:594
  582.5 23.7 %collective-permute-start.9 = (bf16[256,512]{1,0:T(8,128)(2,1)}, bf16[256,512]{1,0:T(8,128)(2,1)}, u32[]{:S(2)}, u32[]{:S(2)}) collective-permute-start(bf16[256,512]{1,0:T(8,128)(2,1)} %get-tuple-element.103), channel_id=1, source_target_pairs={{8,0},{12,1},{9,4},{13,5},{0,8},{4,9},{1,12},{5,13},{10,2},{14,3},... | collective-permute-start | bytes 786440 | tf_op jit(solution)/shard_map/ppermute | solution.py:594
  585.1 21.2 %collective-permute-start.8 = (bf16[256,512]{1,0:T(8,128)(2,1)}, bf16[256,512]{1,0:T(8,128)(2,1)}, u32[]{:S(2)}, u32[]{:S(2)}) collective-permute-start(bf16[256,512]{1,0:T(8,128)(2,1)} %get-tuple-element.104), channel_id=1, source_target_pairs={{1,0},{5,1},{8,4},{12,5},{9,8},{13,9},{0,12},{4,13},{3,2},{7,3},{1... | collective-permute-start | bytes 786440 | tf_op jit(solution)/shard_map/ppermute | solution.py:594
  585.1 21.2 %collective-permute-start.7 = (bf16[256,512]{1,0:T(8,128)(2,1)S(1)}, bf16[256,512]{1,0:T(8,128)(2,1)}, u32[]{:S(2)}, u32[]{:S(2)}) collective-permute-start(bf16[256,512]{1,0:T(8,128)(2,1)S(1)} %get-tuple-element.101), channel_id=1, source_target_pairs={{0,0},{4,1},{1,4},{5,5},{8,8},{12,9},{9,12},{13,13},{2,2},{6,3},{3... | collective-permute-start | bytes 786440 | tf_op jit(solution)/shard_map/ppermute | solution.py:594
  606.3 2.0 copy-start

commit v3 on v2

v3 whole, which is shorter than its diff:
```python
import functools

import jax
import jax.numpy as jnp
from jax import lax
from jax.experimental import pallas as pl
from jax.experimental.pallas import tpu as pltpu
from jax.sharding import Mesh
from jax.sharding import PartitionSpec as P

HD = 64
EPSILON = 1e-05
NEG_BIG = -1e30
CORES = 2
PAIR = 128
PLANE = ("row", "high", "core")
MESH = pl.DeviceIdType.MESH

QKV, OUT, UNIT = 0, 3, 4
FEED_BLOCKS = 2

F32 = jnp.float32
BF16 = jnp.bfloat16
VMEM_BYTES = 56 * 1024 * 1024
LOW_VMEM = 63 * 1024 * 1024


def nn(left, right):
    return lax.dot_general(left, right, (((1,), (0,)), ((), ())), preferred_element_type=F32)


def nt(left, right):
    return lax.dot_general(left, right, (((1,), (1,)), ((), ())), preferred_element_type=F32)


def held(shape):
    return pl.BlockSpec(shape, lambda *_: (0,) * len(shape), pipeline_mode=pl.Buffered(1))


def call(kernel, grid, in_specs, out_specs, out_shape, scratch, name, flops, moved, args):
    return pl.pallas_call(
        kernel,
        grid=grid,
        in_specs=in_specs,
        out_specs=out_specs,
        out_shape=out_shape,
        scratch_shapes=scratch,
        name=name,
        compiler_params=pltpu.CompilerParams(
            vmem_limit_bytes=VMEM_BYTES, dimension_semantics=("arbitrary",) * len(grid)
        ),
        cost_estimate=pl.CostEstimate(flops=flops, bytes_accessed=moved, transcendentals=0),
    )(*args)


def shaped(shape, dtype):
    return jax.ShapeDtypeStruct(shape, dtype)


def row_blocks(rows, narrow):
    take = min(rows, max(1, 256 // narrow))
    while rows % take:
        take += 1
    return take


def side_by_side(blocks):
    take, cols, narrow, deep = blocks.shape
    return jnp.concatenate([blocks[:, k].reshape(take * narrow, deep) for k in range(cols)], axis=1)


def head_lanes(shape, axis):
    return lax.broadcasted_iota(jnp.int32, shape, axis) < HD


def pair_front(query, keys, values, bias_ref):
    values_t = values.T
    lanes = head_lanes(query.shape, 1)
    outs, log_rows = [], []
    for h in range(2):
        mine = jnp.where(lanes if h == 0 else ~lanes, query, 0)
        scores = nt(keys, mine) + bias_ref[...]
        top = jnp.max(scores, axis=0, keepdims=True)
        expo = jnp.exp(scores - top)
        total = jnp.sum(expo, axis=0, keepdims=True)
        outs.append(nn(values_t, expo.astype(BF16)) / total)
        log_rows.append(top + jnp.log(total))
    mixed_t = jnp.where(head_lanes(outs[0].shape, 0), outs[0], outs[1])
    return mixed_t.T.astype(BF16), log_rows


def pair_back(query, grad, mixed, log_rows, keys, values, bias_ref, tile):
    tokens = query.shape[0]
    keys_t = keys.T
    lanes = head_lanes((tile, PAIR), 1)
    low_t = head_lanes(keys_t.shape, 0)
    products = (grad.astype(F32) * mixed.astype(F32)).T
    grad_query = []
    grad_key = jnp.zeros(keys.shape, F32)
    grad_value = jnp.zeros(keys.shape, F32)
    for at in range(0, tokens, tile):
        some = slice(at, at + tile)
        grad_some = jnp.zeros((PAIR, tile), F32)
        for h in range(2):
            here = lanes if h == 0 else ~lanes
            mine = jnp.where(here, query[some], 0)
            grad_mine = jnp.where(here, grad[some], 0)
            inner = jnp.sum(products[h * HD : (h + 1) * HD, some], axis=0, keepdims=True)
            prob = jnp.exp(nt(keys, mine) + bias_ref[:, some] - log_rows[h][:, some])
            grad_value += nn(prob.astype(BF16), grad_mine)
            grad_scores = (prob * (nt(values, grad_mine) - inner)).astype(BF16)
            grad_key += nn(grad_scores, mine)
            keys_mine = jnp.where(low_t if h == 0 else ~low_t, keys_t, 0)
            grad_some += nn(keys_mine, grad_scores)
        grad_query.append(grad_some)
    grad_query = jnp.concatenate(grad_query, axis=1).T.astype(BF16) * HD**-0.5
    return grad_query, grad_key.astype(BF16), grad_value.astype(BF16)


def normed_of(hidden):
    center = hidden - jnp.mean(hidden, axis=1, keepdims=True)
    scale = lax.rsqrt(jnp.mean(center * center, axis=1, keepdims=True) + EPSILON)
    return center * scale, scale


def norm_back(grad_out, normed, scale, gain):
    scaled = grad_out * gain
    first = jnp.mean(scaled, axis=1, keepdims=True)
    second = jnp.mean(scaled * normed, axis=1, keepdims=True)
    return scale * (scaled - first - normed * second)


SLICE = 128


def by_tokens(tokens, body):
    step = min(SLICE, tokens)
    for at in range(0, tokens, step):
        body(pl.ds(at, step))


def gelu_parts(pre):
    below = 0.5 * (1.0 + lax.erf(pre * 0.5**0.5))
    return pre * below, below + pre * jnp.exp(-0.5 * pre * pre) * (2.0 * jnp.pi) ** -0.5


def hidden_columns(block, width):
    rows, _, tall, deep = block.shape
    narrow = width // rows
    parts = [block[:, 0, i * narrow : (i + 1) * narrow].reshape(width, deep) for i in range(FEED_BLOCKS)]
    return jnp.concatenate(parts, axis=1)


def feed_specs(weight, tokens, width, units):
    rows, cols, _, deep = weight.shape
    tall = FEED_BLOCKS * (width // rows)
    block = FEED_BLOCKS * deep
    per = units // cols // block

    def at(first):
        return pl.BlockSpec((rows, 1, tall, deep), lambda s: (0, s // per, first // FEED_BLOCKS + s % per, 0))

    wide = pl.BlockSpec((tokens, block), lambda s: (0, s))
    line = pl.BlockSpec((1, block), lambda s: (0, s))
    return cols * per, at(UNIT), at(UNIT + per * FEED_BLOCKS), wide, line


def column_sum(value):
    return jnp.sum(value, axis=0, keepdims=True)


def top_back_kernel(dy_ref, hat_ref, scale_ref, n_ref, dh2_ref, ddown_ref, *sums_ref):
    for ref in sums_ref:
        ref[...] = jnp.zeros_like(ref)

    def some(at):
        dy, hat = dy_ref[at].astype(F32), hat_ref[at]
        dh2 = norm_back(dy, hat, scale_ref[at][:, :1], n_ref[1:2])
        dh2_ref[at] = dh2
        ddown = dh2.astype(BF16)
        ddown_ref[at] = ddown
        for ref in sums_ref:
            ref[0:1] += column_sum(ddown.astype(F32))
            ref[1:2] += column_sum(dy)
            ref[2:3] += column_sum(dy * hat)

    by_tokens(dy_ref.shape[0], some)


def top_back(dy, hat2, scale2, gain, sums_too):
    tokens, width = hat2.shape
    flat = held((tokens, width))
    return call(
        top_back_kernel,
        (1,),
        [flat, flat, held((tokens, 128)), held(gain.shape)],
        [flat, flat] + [held((8, width))] * sums_too,
        [shaped((tokens, width), F32), shaped((tokens, width), BF16)] + [shaped((8, width), F32)] * sums_too,
        [],
        "top_back",
        20 * tokens * width,
        12 * tokens * width,
        (dy, hat2, scale2, gain),
    )


def feed_back_kernel(*refs, steps, sums_too):
    dh2_ref, ddown_ref, hat1_ref, scale1_ref, slope_ref, wu_ref, wd_ref, n_ref, dattn_ref = refs[:9]
    acc_ref = refs[-1]
    s = pl.program_id(0)
    tokens, width = dh2_ref.shape
    dact = nn(ddown_ref[...], hidden_columns(wd_ref[...], width))
    dpre = (dact * slope_ref[...].astype(F32)).astype(BF16)
    back = nt(dpre, hidden_columns(wu_ref[...], width))
    if sums_too:
        dpre_ref, pre_ref, sums_ref = refs[9:12]
        dpre_ref[...] = dpre
        pre_ref[...] = column_sum(dpre.astype(F32))

    @pl.when(s == 0)
    def _():
        acc_ref[...] = back

    @pl.when(s > 0)
    def _():
        acc_ref[...] += back

    @pl.when(s == steps - 1)
    def _():
        if sums_too:
            sums_ref[...] = jnp.zeros_like(sums_ref)

        def some(at):
            dx1, hat = dh2_ref[at] + acc_ref[at], hat1_ref[at]
            dattn = norm_back(dx1, hat, scale1_ref[at][:, :1], n_ref[0:1]).astype(BF16)
            dattn_ref[at] = dattn
            if sums_too:
                sums_ref[0:1] += column_sum(dattn.astype(F32))
                sums_ref[1:2] += column_sum(dx1)
                sums_ref[2:3] += column_sum(dx1 * hat)

        by_tokens(tokens, some)


def feed_back(dh2, ddown, hat1, scale1, slope, weight, gain, sums_too):
    tokens, width = dh2.shape
    units = slope.shape[1]
    steps, first, second, wide, line = feed_specs(weight, tokens, width, units)
    flat = held((tokens, width))
    out_specs, out_shape = [flat], [shaped((tokens, width), BF16)]
    if sums_too:
        out_specs += [wide, line, held((8, width))]
        out_shape += [shaped((tokens, units), BF16), shaped((1, units), F32), shaped((8, width), F32)]
    return call(
        functools.partial(feed_back_kernel, steps=steps, sums_too=sums_too),
        (steps,),
        [flat, flat, flat, held((tokens, 128)), wide, first, second, held(gain.shape)],
        out_specs,
        out_shape,
        [pltpu.VMEM((tokens, width), F32)],
        "feed_back",
        4 * tokens * width * units,
        4 * width * units,
        (dh2, ddown, hat1, scale1, slope, weight, weight, gain),
    )


class Layout:
    def __init__(self, tokens_in, doc_ids):
        self.micro, self.narrow, _ = tokens_in.shape
        self.seq_here, self.seq_len = doc_ids.shape[1:]
        self.rows = lax.axis_size("row")
        self.cols = lax.axis_size("high") * CORES
        self.width = self.narrow * self.rows
        self.places = self.rows * CORES
        self.sequences = self.micro * self.seq_here * CORES
        self.group = self.places // self.sequences
        self.part = self.seq_len // self.group
        self.row = lax.axis_index("row")
        place = self.row * CORES + lax.axis_index("core")
        self.sequence = place // self.group
        self.position = place % self.group
        self.block = (self.sequence // CORES) * self.group + self.position


class Line:
    def __init__(self, axis, size):
        self.axis, self.size, self.here = axis, size, lax.axis_index(axis)

    def sends(self, step):
        last = self.size - 1
        return (
            (True, (self.here < step) & (self.here < last), self.size - step + self.here, self.here > 0),
            (False, (last - self.here < step) & (self.here > 0), step - self.size + self.here, self.here < last),
        )

    def gets(self, step):
        last = self.size - 1
        return (
            (True, (self.here >= 1) & (self.here <= step)),
            (False, (last - self.here >= 1) & (last - self.here <= step)),
        )

    def neighbour(self, right):
        return {self.axis: self.here + (1 if right else -1)}


def greet(lines, pairs, members=(), some=()):
    barrier = pltpu.get_barrier_semaphore()
    count = 0
    for line in lines:
        for right, there in ((True, line.here < line.size - 1), (False, line.here > 0)):

            @pl.when(there)
            def _(line=line, right=right):
                pl.semaphore_signal(barrier, 1, device_id=line.neighbour(right), device_id_type=MESH)

            count = count + there.astype(jnp.int32)
    for axis in pairs:
        pl.semaphore_signal(barrier, 1, device_id={axis: 1 - lax.axis_index(axis)}, device_id_type=MESH)
        count = count + 1
    for member in members:
        pl.semaphore_signal(barrier, 1, device_id=member, device_id_type=MESH)
        count = count + 1
    for member, there in some:

        @pl.when(there)
        def _(member=member):
            pl.semaphore_signal(barrier, 1, device_id=member, device_id_type=MESH)

        count = count + there.astype(jnp.int32)
    pl.semaphore_wait(barrier, count)


def add_into(target, other):
    lead = target.shape[:-2]
    rows = target.shape[-2]
    total = 1
    for size in lead:
        total *= size
    if total == 1:
        target[...] = target[...] + other[...]
        return

    @pl.loop(0, total)
    def _(i):
        index = []
        for size in reversed(lead):
            index.insert(0, lax.rem(i, size))
            i = lax.div(i, size)
        index = tuple(index)
        target[index] = target[index] + other[index]


class Scatter:
    def __init__(self, pieces, refs, highs, rows, give):
        self.pieces, self.give = pieces, give
        (self.landing, self.work, self.got, self.from_high, self.got_high, self.from_row, self.from_wide, *sems) = refs
        self.sem_core, self.sem_load, self.sem_high, self.sem_row = sems
        self.high, self.row = Line("high", highs), Line("row", rows)
        self.core = lax.axis_index("core")
        self.slots = self.work.shape[0]
        self.sent = [[] for _ in pieces]
        self.place, wide, thin = [], 0, 0
        for _, _, row_last in pieces:
            self.place.append(thin if row_last else wide)
            thin, wide = thin + row_last, wide + (not row_last)

    def slot(self, q):
        return q % self.slots

    def cut(self, q, ref):
        return ref.at[..., pl.ds(0, self.pieces[q][1]), :]

    def to_core(self, q, y):
        return pltpu.make_async_remote_copy(
            self.pieces[q][0].at[:, y, 1 - self.core],
            self.cut(q, self.landing.at[q, y]),
            self.sem_core.at[q, y, 0],
            self.sem_core.at[q, y, 1],
            device_id={"core": 1 - self.core},
            device_id_type=MESH,
        )

    def load(self, q, y):
        return pltpu.make_async_copy(
            self.pieces[q][0].at[:, y, self.core],
            self.cut(q, self.work.at[self.slot(q), y]),
            self.sem_load.at[q, y, 0],
        )

    def fetch(self, q, y):
        return pltpu.make_async_copy(
            self.cut(q, self.landing.at[q, y]), self.cut(q, self.got.at[q % 2, y]), self.sem_load.at[q, y, 1]
        )

    def begin(self, q):
        if q >= self.slots:
            self.finish_sends(q - self.slots)
        for y in range(self.high.size):
            self.to_core(q, y).start()
            self.load(q, y).start()

    def arrive(self, q):
        for y in range(self.high.size):
            self.to_core(q, y).wait()
            self.fetch(q, y).start()

    def merge(self, q):
        for y in range(self.high.size):
            self.load(q, y).wait()
            self.fetch(q, y).wait()
            add_into(self.cut(q, self.work.at[self.slot(q), y]), self.cut(q, self.got.at[q % 2, y]))

    def lines(self, q):
        return (self.high, self.row) if self.pieces[q][2] else (self.row, self.high)

    def block(self, q, line, i):
        first = line is self.lines(q)[0]
        if line is self.high:
            ref = self.work.at[self.slot(q), i, slice(None) if first else self.row.here]
        else:
            ref = self.work.at[self.slot(q), slice(None) if first else self.high.here, i]
        return self.cut(q, ref)

    def arrival(self, q, line, step, right):
        way = 0 if line.size == 2 or right else 1
        first = line is self.lines(q)[0]
        if line is self.high:
            index = (slice(None),) if first else (0,)
            return (
                self.cut(q, self.from_high.at[(q, step - 1, way) + index]),
                self.cut(q, self.got_high.at[(q % 2, way) + index]),
            )
        ref = (self.from_wide if first else self.from_row).at[self.place[q], step - 1, way]
        return (self.cut(q, ref),) * 2

    def copy(self, q, line, step, right, i):
        sems = (self.sem_high if line is self.high else self.sem_row).at[q, step - 1, 0 if right else 1]
        return pltpu.make_async_remote_copy(
            self.block(q, line, i),
            self.arrival(q, line, step, right)[0],
            sems.at[0],
            sems.at[1],
            device_id=line.neighbour(right),
            device_id_type=MESH,
        )

    def push(self, q, line, step):
        for right, there, i, more in line.sends(step):

            @pl.when(there)
            def _(right=right, i=i, more=more):
                if step > 1:

                    @pl.when(more)
                    def _():
                        add_into(self.block(q, line, i), self.arrival(q, line, step - 1, right)[1])

                self.copy(q, line, step, right, i).start()

            self.sent[q].append((line, step, right, there, i))

    def pull(self, q, line, step):
        for right, there in line.gets(step):

            @pl.when(there)
            def _(right=right):
                self.copy(q, line, step, right, 0).wait_recv()
                if line is self.high:
                    landed, got = self.arrival(q, line, step, right)
                    way = 0 if line.size == 2 or right else 1
                    fetch = pltpu.make_async_copy(landed, got, self.sem_high.at[q, step - 1, way, 2])
                    fetch.start()
                    fetch.wait()

    def close(self, q, line):
        for right, there in line.gets(line.size - 1):

            @pl.when(there)
            def _(right=right):
                add_into(self.block(q, line, line.here), self.arrival(q, line, line.size - 1, right)[1])

    def finish_sends(self, q):
        for line, step, right, there, i in self.sent[q]:

            @pl.when(there)
            def _(line=line, step=step, right=right, i=i):
                self.copy(q, line, step, right, i).wait_send()

        self.sent[q] = []

    def stages(self, q):
        lines = [(line, step) for line in self.lines(q) for step in range(1, line.size)]

        def merge():
            self.merge(q)
            self.push(q, *lines[0])

        stages = [lambda: self.begin(q), lambda: self.arrive(q), merge]
        for n, (line, step) in enumerate(lines):

            def one(n=n, line=line, step=step):
                self.pull(q, line, step)
                if step == line.size - 1:
                    self.close(q, line)
                if n + 1 < len(lines):
                    self.push(q, *lines[n + 1])
                else:
                    self.give(q, self.block(q, line, line.here))

            if line is self.high and step == 1:
                stages.append(lambda: None)
            stages.append(one)
        return stages

    def run(self, between):
        stages = [self.stages(q) for q in range(len(self.pieces))]
        depth, count = len(stages[0]), len(stages)
        for tick in range(count + depth - 1):
            for q in range(max(0, tick - depth + 1), min(tick + 1, count)):
                stages[q][tick - q]()
            between(tick)
        for q in range(count):
            self.finish_sends(q)


class Spread:
    def __init__(self, axis, size):
        self.axis, self.size, self.here = axis, size, lax.axis_index(axis)

    def sends(self, step):
        last = self.size - 1
        return (
            (True, (self.here < last) & (self.here >= step - 1), self.here - step + 1),
            (False, (self.here > 0) & (self.here + step - 1 <= last), self.here + step - 1),
        )

    def gets(self, step):
        last = self.size - 1
        return ((True, self.here >= step), (False, self.here + step <= last))

    def neighbour(self, right):
        return {self.axis: self.here + (1 if right else -1)}


class Gather:
    def __init__(self, pieces, sems, highs, rows):
        self.pieces = pieces
        self.sem_row, self.sem_high, self.sem_core = sems
        self.row, self.high = Spread("row", rows), Spread("high", highs)
        self.core = lax.axis_index("core")
        self.sent = []

    def block(self, q, line, i):
        ref, first, count, row_first = self.pieces[q]
        some = pl.ds(first, count)
        if line is self.row:
            return ref.at[i, self.high.here if row_first else slice(None), self.core, some]
        return ref.at[slice(None) if row_first else self.row.here, i, self.core, some]

    def copy(self, q, line, step, right, i):
        sems = (self.sem_row if line is self.row else self.sem_high).at[q, step - 1, 0 if right else 1]
        ref = self.block(q, line, i)
        return pltpu.make_async_remote_copy(
            ref, ref, sems.at[0], sems.at[1], device_id=line.neighbour(right), device_id_type=MESH
        )

    def push(self, q, line, step):
        for right, there, i in line.sends(step):

            @pl.when(there)
            def _(right=right, i=i):
                self.copy(q, line, step, right, i).start()

            self.sent.append((q, line, step, right, there, i))

    def pull(self, q, line, step):
        for right, there in line.gets(step):

            @pl.when(there)
            def _(right=right):
                self.copy(q, line, step, right, line.here).wait_recv()

    def to_core(self, q):
        ref, first, count, _ = self.pieces[q]
        ref = ref.at[:, :, self.core, pl.ds(first, count)]
        return pltpu.make_async_remote_copy(
            ref, ref, self.sem_core.at[q, 0], self.sem_core.at[q, 1],
            device_id={"core": 1 - self.core}, device_id_type=MESH,
        )

    def stages(self, q):
        first, second = (self.row, self.high) if self.pieces[q][3] else (self.high, self.row)
        steps = [lambda: self.push(q, first, 1)]
        lines = [(first, i) for i in range(1, first.size)] + [(second, i) for i in range(1, second.size)]
        for n, (line, step) in enumerate(lines):

            def one(n=n, line=line, step=step):
                self.pull(q, line, step)
                if n + 1 < len(lines):
                    self.push(q, *lines[n + 1])
                else:
                    self.to_core(q).start()

            steps.append(lambda: None)
            steps.append(one)
        steps.append(lambda: self.to_core(q).wait())
        return steps

    def run(self, between):
        stages = [self.stages(q) for q in range(len(self.pieces))]
        depth, count = len(stages[0]), len(stages)
        for tick in range(count + depth - 1):
            for q in range(max(0, tick - depth + 1), min(tick + 1, count)):
                stages[q][tick - q]()
            between(tick, tick - depth + 1)

    def finish(self):
        for q, line, step, right, there, i in self.sent:

            @pl.when(there)
            def _(q=q, line=line, step=step, right=right, i=i):
                self.copy(q, line, step, right, i).wait_send()


class Group:
    def __init__(self, size):
        self.size = size
        self.place = lax.axis_index("row") * CORES + lax.axis_index("core")
        self.position = lax.rem(self.place, size)

    def member(self, step):
        other = self.place - self.position + lax.rem(self.position + step, self.size)
        return {"row": lax.div(other, CORES), "core": lax.rem(other, CORES)}

    def members(self):
        return [self.member(step) for step in range(1, self.size)]


class Front:
    def __init__(self, w, vectors, shift, x, q, kv, mixed, mask, x1, x1_bf, acc, log=None):
        self.w, self.vectors, self.shift, self.x, self.q, self.kv = w, vectors, shift, x, q, kv
        self.mixed, self.mask, self.x1, self.x1_bf, self.acc, self.log = mixed, mask, x1, x1_bf, acc, log
        self.tokens, self.width = x.shape
        self.rows, self.highs, _, _, self.deep = w.shape
        self.cols = self.highs * CORES
        self.narrow = self.width // self.rows
        self.group = kv.shape[0]
        self.pairs = self.width // PAIR
        self.blocks = shift.shape[1] // self.cols // self.deep

    def matrix(self, block, k):
        at = pl.ds(block * self.narrow, self.narrow)
        return self.w[:, k // CORES, k % CORES, at].reshape(self.width, self.deep)

    def project(self, j):
        take = row_blocks(self.rows, self.narrow)
        for r in range(0, self.rows, take):
            at = slice(r * self.narrow, (r + take) * self.narrow)
            some = pl.ds((QKV + j) * self.narrow, self.narrow)
            weight = jnp.concatenate(
                [
                    self.w[r : r + take, k // CORES, k % CORES, some].reshape(take * self.narrow, self.deep)
                    for k in range(self.cols)
                ],
                axis=1,
            )
            out = nt(self.x[...], weight)
            if j == 0:
                self.q[:, at] = ((out + self.vectors[0:1, at]) * HD**-0.5).astype(BF16)
            elif j == 1:
                self.kv[0, 0, :, at] = out.astype(BF16)
            else:
                self.kv[0, 1, :, at] = (out + self.vectors[1:2, at]).astype(BF16)

    def attend(self, first, count):
        @pl.loop(first, first + count)
        def _(p):
            at = pl.ds(pl.multiple_of(p * PAIR, PAIR), PAIR)
            keys = jnp.concatenate([self.kv[i, 0, :, at] for i in range(self.group)], axis=0)
            values = jnp.concatenate([self.kv[i, 1, :, at] for i in range(self.group)], axis=0)
            mixed, log_rows = pair_front(self.q[:, at], keys, values, self.mask)
            self.mixed[:, at] = mixed
            if self.log is not None:
                for h in range(2):
                    self.log[p, h : h + 1] = log_rows[h]

    def out(self):
        for k in range(self.cols):
            at = slice(k * self.deep, (k + 1) * self.deep)
            self.acc[:, at] = nn(self.mixed[...], self.matrix(OUT, k))

    def norm_one(self, keep=None):
        def some(at):
            attn = self.acc[at] + self.vectors[2:3]
            normed, scale = normed_of(self.x[at].astype(F32) + attn)
            x1 = normed * self.vectors[6:7] + self.vectors[3:4]
            self.x1[at] = x1
            self.x1_bf[at] = x1.astype(BF16)
            if keep is not None:
                keep(at, normed, scale)

        by_tokens(self.tokens, some)

    def feed(self, block, ks, start, keep=None, at=slice(None)):
        up = jnp.concatenate([self.matrix(UNIT + block, k) for k in ks], axis=1)
        down = jnp.concatenate([self.matrix(UNIT + self.blocks + block, k) for k in ks], axis=1)
        hidden = self.blocks * self.deep
        begins = [k * hidden + block * self.deep for k in ks]
        shift = jnp.concatenate([self.shift[:, b : b + self.deep] for b in begins], axis=1)
        act, slope = gelu_parts(nn(self.x1_bf[at], up) + shift)
        act = act.astype(BF16)
        if keep is not None:
            keep(act, slope.astype(BF16))
        more = nt(act, down)
        if start:
            self.acc[at] = more
        else:
            self.acc[at] += more

    def norm_two(self, at, keep=None):
        normed, scale = normed_of(self.x1[at] + (self.acc[at] + self.vectors[4:5]))
        if keep is not None:
            keep(at, normed, scale)
        return normed * self.vectors[7:8] + self.vectors[5:6]


def share_keys(group, kv, sems):
    def copy(step):
        return pltpu.make_async_remote_copy(
            kv.at[0], kv.at[step], sems.at[step - 1, 0], sems.at[step - 1, 1],
            device_id=group.member(step), device_id_type=MESH,
        )

    return [copy(step) for step in range(1, group.size)]


def first_kernel(*refs, highs, rows, group, micro, seq_here, seq_len):
    (small_ref, tokens_hbm, cot_hbm, qkv_ref, out_ref, unit_ref, down_ref) = refs[:7]
    (next_hbm, start_ref, w_hbm, vectors, shift, doc_q, doc_k) = refs[7:14]
    (w, small, turned, x, q, kv, mixed, mask, x1, x1_bf, acc, y,
     sem_row, sem_high, sem_core, sem_x, sem_kv, sem_y, sem_w, sem_next) = refs[14:]
    tokens, width = x.shape
    narrow, deep = width // rows, w.shape[-1]
    cols = highs * CORES
    hidden = unit_ref.shape[2]
    blocks = hidden // deep
    row, high, core = lax.axis_index("row"), lax.axis_index("high"), lax.axis_index("core")
    section = lax.axis_index("section")
    sharing = Group(group)
    sequence = lax.div(sharing.place, group)
    front = Front(w, vectors, shift, x, q, kv, mixed, mask, x1, x1_bf, acc)

    w[row, high, core, 0 : 3 * narrow] = qkv_ref[0].reshape(3 * narrow, deep).astype(BF16)
    w[row, high, core, 3 * narrow : 4 * narrow] = out_ref[0].astype(BF16)
    for i in range(blocks):
        at = slice(i * deep, (i + 1) * deep)
        for j, ref in enumerate((unit_ref, down_ref)):
            first = (UNIT + j * blocks + i) * narrow
            w[row, high, core, first : first + narrow] = ref[0, :, at].astype(BF16)
    small[row, high, core] = small_ref[...]

    def goes(j):
        place = ((j // group) * CORES + core) * group + j % group
        return lax.div(place, CORES), lax.rem(place, CORES)

    source_core = lax.rem(sequence, CORES)
    mine_too = source_core == core

    def block_of(ref, j):
        m, rest = divmod(j // group, seq_here)
        return ref.at[m, :, pl.ds(rest * seq_len + (j % group) * tokens, tokens)]

    def send_block(ref, j):
        there_row, there_core = goes(j)
        return pltpu.make_async_remote_copy(
            block_of(ref, j), turned.at[row], sem_x.at[j, 0], sem_x.at[row, 1],
            device_id={"row": there_row, "core": there_core}, device_id_type=MESH,
        )

    def is_here(j):
        there_row, there_core = goes(j)
        return (there_row == row) & (there_core == core)

    barrier = pltpu.get_barrier_semaphore()
    count = 0
    for line in (Spread("row", rows), Spread("high", highs)):
        for right, there in ((True, line.here < line.size - 1), (False, line.here > 0)):

            @pl.when(there)
            def _(line=line, right=right):
                pl.semaphore_signal(barrier, 1, device_id=line.neighbour(right), device_id_type=MESH)

            count = count + there.astype(jnp.int32)
    others = [{"core": 1 - core}, {"section": 1 - section}] + sharing.members()
    for other in others:
        pl.semaphore_signal(barrier, 1, device_id=other, device_id_type=MESH)
    for r in range(rows):

        @pl.when(jnp.logical_not(mine_too & (row == r)))
        def _(r=r):
            pl.semaphore_signal(barrier, 1, device_id={"row": r, "core": source_core}, device_id_type=MESH)

    pl.semaphore_wait(barrier, count + len(others) + rows - mine_too.astype(jnp.int32))

    row_first = [True] * (4 + 2 * blocks)
    row_first[4 + blocks] = False
    order = [0, 1, 2, 3] + [UNIT + j * blocks + i for i in range(blocks) for j in range(2)]
    pieces = [(small, 0, small.shape[3], True)]
    pieces += [(w, i * narrow, narrow, row_first[n]) for n, i in enumerate(order)]
    gather = Gather(pieces, (sem_row, sem_high, sem_core), highs, rows)

    def to_hbm(q):
        at = pl.ds(order[q - 1] * narrow, narrow)
        return pltpu.make_async_copy(w.at[:, :, :, at], w_hbm.at[:, :, :, at], sem_w.at[q])

    keys = share_keys(sharing, kv, sem_kv)

    def begin():
        for j in range(rows):
            for which, ref in ((0, tokens_hbm), (1, cot_hbm)):

                @pl.when((section == which) & is_here(j))
                def _(ref=ref, j=j):
                    pltpu.make_async_copy(block_of(ref, j), turned.at[row], sem_x.at[row, 1]).start()

                @pl.when((section == which) & jnp.logical_not(is_here(j)))
                def _(ref=ref, j=j):
                    send_block(ref, j).start()

    def use_small():
        for r in range(rows):
            vectors[:, r * narrow : (r + 1) * narrow] = small[r, 0, 0, 0:8, 0:narrow]
        for k in range(cols):
            for i in range(blocks):
                at = k * hidden + i * deep
                shift[:, at : at + deep] = small[0, k // CORES, k % CORES, 8 + i : 9 + i]
        lines = tokens // deep
        for slot in range(group):
            part = lax.rem(sharing.position + group - slot, group)
            base = 8 + blocks + (lax.div(sequence, CORES) * group + part) * lines
            doc = jnp.concatenate([small[row, high, source_core, pl.ds(base + i, 1)] for i in range(lines)], axis=1)
            if slot == 0:
                doc_q[...] = doc
            doc_k[slot * tokens : (slot + 1) * tokens] = jnp.broadcast_to(doc, (128, tokens)).T[:, :1]
        mask[...] = jnp.where(doc_k[...] == doc_q[...], 0.0, NEG_BIG)

    def turn():
        for r in range(rows):
            pltpu.make_async_copy(turned.at[r], turned.at[r], sem_x.at[r, 1]).wait()
        for r in range(rows):
            x[:, r * narrow : (r + 1) * narrow] = turned[r].T
        start_ref[...] = x[...]

    half = max(1, cols // 2)
    chunks = min(4, tokens // 8)
    chunk = tokens // chunks

    def send_out(i):
        at = pl.ds(i * chunk, chunk)
        return pltpu.make_async_remote_copy(
            y.at[at], next_hbm.at[at], sem_y.at[i, 0], sem_y.at[i, 1],
            device_id={"section": 1 - section}, device_id_type=MESH,
        )

    stay = pltpu.make_async_copy(x, next_hbm, sem_next.at[0])
    base = 3

    def between(tick, done):
        if done >= 1:
            to_hbm(done).start()
        if done == 0:
            use_small()
        if done == 1:
            turn()

            @pl.when(section == 0)
            def _():
                stay.start()

            front.project(0)
        if done == 2:
            front.project(1)
        if done == base:
            front.project(2)
            for copy in keys:
                copy.start()
        if done == base + 1:
            for copy in keys:
                copy.wait()
        if base + 1 <= done < base + 5:
            front.attend((done - base - 1) * (front.pairs // 4), front.pairs // 4)
        if done == base + 5:
            front.out()
            front.norm_one()
        if done >= base + 5:
            first = done == base + 5
            ready = (done - 4) // 2
            from_block = 0 if first else (done - 1 - 4) // 2
            for block in range(from_block, min(ready, blocks)):
                if block < blocks - 1:
                    for k in range(0, cols, half):
                        front.feed(block, range(k, k + half), block == 0 and k == 0)

    begin()
    gather.run(between)
    for i in range(chunks):
        at = pl.ds(i * chunk, chunk)
        for k in range(0, cols, half):
            front.feed(blocks - 1, range(k, k + half), blocks == 1 and k == 0, at=at)
        y[at] = front.norm_two(at).astype(BF16)

        @pl.when(section == 0)
        def _(i=i):
            send_out(i).start()

    gather.finish()
    for j in range(rows):

        @pl.when(jnp.logical_not(is_here(j)))
        def _(j=j):
            send_block(tokens_hbm, j).wait_send()

    for q in range(1, len(pieces)):
        to_hbm(q).wait()

    @pl.when(section == 0)
    def _():
        stay.wait()
        for i in range(chunks):
            send_out(i).wait_send()

    @pl.when(section == 1)
    def _():
        for i in range(chunks):
            send_out(i).wait_recv()


def first_forward(small, tokens_in, cotangent, qkv, out, unit, down, rows, highs, group, seq_here, seq_len):
    micro, narrow, _ = tokens_in.shape
    deep, hidden = out.shape[2], unit.shape[2]
    width, cols, blocks = narrow * rows, highs * CORES, hidden // deep
    tokens = seq_len // group
    tall = (4 + 2 * blocks) * narrow
    apart = (rows, highs, CORES)
    in_any = pl.BlockSpec(memory_space=pl.ANY)
    in_vmem = pl.BlockSpec(memory_space=pltpu.VMEM)
    count = 1 + 4 + 2 * blocks
    dma = pltpu.SemaphoreType.DMA
    flat, flat_f32 = pltpu.VMEM((tokens, width), BF16), pltpu.VMEM((tokens, width), F32)
    return pl.pallas_call(
        functools.partial(
            first_kernel, highs=highs, rows=rows, group=group, micro=micro, seq_here=seq_here, seq_len=seq_len
        ),
        in_specs=[in_vmem, in_any, in_any] + [in_vmem] * 4,
        out_specs=[in_any, in_vmem, in_any] + [in_vmem] * 4,
        out_shape=[
            shaped((tokens, width), BF16),
            shaped((tokens, width), BF16),
            shaped(apart + (tall, deep), BF16),
            shaped((8, width), F32),
            shaped((1, hidden * cols), F32),
            shaped((1, tokens), F32),
            shaped((group * tokens, 1), F32),
        ],
        scratch_shapes=[
            pltpu.VMEM(apart + (tall, deep), BF16),
            pltpu.VMEM(apart + small.shape, F32),
            pltpu.VMEM((rows, narrow, tokens), BF16),
            flat,
            flat,
            pltpu.VMEM((group, 2, tokens, width), BF16),
            flat,
            pltpu.VMEM((group * tokens, tokens), F32),
            flat_f32,
            flat,
            flat_f32,
            flat,
            dma((count, rows - 1, 2, 2)),
            dma((count, highs - 1, 2, 2)),
            dma((count, 2)),
            dma((rows, 2)),
            dma((max(1, group - 1), 2)),
            dma((4, 2)),
            dma((count,)),
            dma((1,)),
        ],
        name="first_forward",
        compiler_params=pltpu.CompilerParams(collective_id=2, has_side_effects=True, vmem_limit_bytes=LOW_VMEM),
        cost_estimate=pl.CostEstimate(
            flops=24 * tokens * width * width, bytes_accessed=2 * tall * deep * rows * cols, transcendentals=0
        ),
    )(small, tokens_in, cotangent, qkv, out, unit, down)


class Streams:
    def __init__(self, landing, sems, group):
        self.landing, self.sems, self.rows = landing, sems, landing.shape[0]
        self.row, self.core = lax.axis_index("row"), lax.axis_index("core")
        self.place, self.size = group.place, group.size
        sequence = lax.div(group.place, group.size)
        self.to = lax.rem(sequence, CORES)
        self.slot = lax.div(sequence, CORES) * group.size + group.position

    def here(self, r):
        return (self.to == self.core) & (self.row == r)

    def sources(self):
        found = []
        for r in range(self.rows):
            place = ((r // self.size) * CORES + self.core) * self.size + r % self.size
            found.append(({"row": lax.div(place, CORES), "core": lax.rem(place, CORES)}, place != self.place))
        return found

    def copy(self, ref, r):
        return pltpu.make_async_remote_copy(
            ref.at[r], self.landing.at[self.slot], self.sems.at[r, 0], self.sems.at[self.slot, 1],
            device_id={"row": r, "core": self.to}, device_id_type=MESH,
        )

    def start(self, ref):
        for r in range(self.rows):

            @pl.when(self.here(r))
            def _(r=r):
                pltpu.make_async_copy(ref.at[r], self.landing.at[self.slot], self.sems.at[self.slot, 1]).start()

            @pl.when(jnp.logical_not(self.here(r)))
            def _(r=r):
                self.copy(ref, r).start()

    def wait_sent(self, ref):
        for r in range(self.rows):

            @pl.when(jnp.logical_not(self.here(r)))
            def _(r=r):
                self.copy(ref, r).wait_send()

    def wait_here(self):
        for r in range(self.rows):
            pltpu.make_async_copy(self.landing.at[r], self.landing.at[r], self.sems.at[r, 1]).wait()


def share_key_grads(group, dkv, got, sems):
    def copy(step):
        return pltpu.make_async_remote_copy(
            dkv.at[step], got.at[step - 1], sems.at[step - 1, 0], sems.at[step - 1, 1],
            device_id=group.member(group.size - step), device_id_type=MESH,
        )

    return [copy(step) for step in range(1, group.size)]


def join_key_grads(dkv, got):
    group, _, tokens, _ = dkv.shape
    step = min(SLICE, tokens)

    @pl.loop(0, tokens, step=step)
    def _(at):
        some = pl.ds(pl.multiple_of(at, step), step)
        for j in range(2):
            total = dkv[0, j, some].astype(F32)
            for i in range(group - 1):
                total += got[i, j, some].astype(F32)
            dkv[0, j, some] = total.astype(BF16)


def heads_back(q, dmixed, mixed, log, kv, mask, first, count):
    group, _, tokens, _ = kv.shape

    @pl.loop(first, first + count)
    def _(p):
        at = pl.ds(pl.multiple_of(p * PAIR, PAIR), PAIR)
        keys = jnp.concatenate([kv[i, 0, :, at] for i in range(group)], axis=0)
        values = jnp.concatenate([kv[i, 1, :, at] for i in range(group)], axis=0)
        grad_query, grad_key, grad_value = pair_back(
            q[:, at], dmixed[:, at], mixed[:, at], [log[p, h : h + 1] for h in range(2)], keys, values, mask,
            min(256, tokens),
        )
        q[:, at] = grad_query
        for part in range(group):
            kv[part, 0, :, at] = grad_key[part * tokens : (part + 1) * tokens]
            kv[part, 1, :, at] = grad_value[part * tokens : (part + 1) * tokens]


def middle_kernel(*refs, group):
    (in_hbm, start_hbm, w_hbm, vectors, shift, doc_q, doc_k) = refs[:7]
    (next_hbm, q_hbm, kv_hbm, mixed_hbm, log_hbm, x1_hbm, hat1_hbm, scale1_hbm, hat2_hbm, scale2_hbm, act_hbm, slope_hbm,
     landing) = refs[7:20]
    (w, x, q, kv, mixed, log, mask, x1, x1_bf, acc, slope, act, hat1, hat2, scale1, scale2, y_t, got,
     sem_w, sem_in, sem_kv, sem_dkv, sem_keep, sem_act, sem_next, sem_out) = refs[20:]
    tokens, width = x.shape
    rows, highs, _, _, deep = w.shape
    narrow, cols = width // rows, highs * CORES
    section = lax.axis_index("section")
    sharing = Group(group)
    front = Front(w, vectors, shift, x, q, kv, mixed, mask, x1, x1_bf, acc, log)
    blocks = front.blocks
    hidden = blocks * deep
    streams = Streams(landing, sem_out, sharing)

    cuts = [(QKV, 3), (OUT, 1)] + [(UNIT + j * blocks + i, 1) for i in range(blocks) for j in range(2)]

    def load_w(i):
        first, count = cuts[i]
        at = pl.ds(first * narrow, count * narrow)
        return pltpu.make_async_copy(w_hbm.at[:, :, :, at], w.at[:, :, :, at], sem_w.at[i])

    get_x = pltpu.make_async_copy(in_hbm, x, sem_in.at[0])
    get_dy = pltpu.make_async_copy(start_hbm, x, sem_in.at[1])
    get_x.start()
    for i in range(len(cuts)):
        load_w(i).start()
    kept = {}

    def keep(i, ref, there):
        kept[i] = pltpu.make_async_copy(ref, there, sem_keep.at[i])
        kept[i].start()

    greet((), ("section",), sharing.members(), streams.sources())
    mask[...] = jnp.where(doc_k[...] == doc_q[...], 0.0, NEG_BIG)
    get_x.wait()
    load_w(0).wait()
    front.project(1)
    front.project(2)
    keys = share_keys(sharing, kv, sem_kv)
    for copy in keys:
        copy.start()
    front.project(0)
    keep(0, q, q_hbm)
    for copy in keys:
        copy.wait()
    keep(1, kv, kv_hbm)
    front.attend(0, front.pairs)
    keep(2, mixed, mixed_hbm)
    keep(3, log, log_hbm)
    load_w(1).wait()
    front.out()

    def keep_one(at, normed, scale):
        hat1[at] = normed.astype(BF16)
        scale1[at] = jnp.broadcast_to(scale, scale1[at].shape)

    front.norm_one(keep_one)
    get_dy.start()
    keep(4, x1_bf, x1_hbm)
    keep(5, hat1, hat1_hbm)
    keep(6, scale1, scale1_hbm)
    half = max(1, cols // 2)
    turns = [(block, range(k, k + half)) for block in range(blocks) for k in range(0, cols, half)]

    def keep_act(n):
        block, ks = turns[n]
        return [
            pltpu.make_async_copy(
                act.at[n % 2, :, pl.ds(i * deep, deep)],
                act_hbm.at[:, pl.ds(k * hidden + block * deep, deep)],
                sem_act.at[n % 2, i],
            )
            for i, k in enumerate(ks)
        ]

    for n, (block, ks) in enumerate(turns):
        if n % (cols // half) == 0:
            load_w(2 + 2 * block).wait()
            load_w(3 + 2 * block).wait()

        def keep_both(value, value_slope, n=n, block=block, ks=ks):
            if n >= 2:
                for copy in keep_act(n - 2):
                    copy.wait()
            act[n % 2] = value
            for copy in keep_act(n):
                copy.start()
            for i, k in enumerate(ks):
                begin = k * hidden + block * deep
                slope[:, begin : begin + deep] = value_slope[:, i * deep : (i + 1) * deep]

        front.feed(block, ks, n == 0, keep_both)
    keep(7, slope, slope_hbm)

    def keep_two(at, normed, scale):
        hat2[at] = normed.astype(BF16)
        scale2[at] = jnp.broadcast_to(scale, scale2[at].shape)

    step = min(SLICE, tokens)
    for begin in range(0, tokens, step):
        y = front.norm_two(pl.ds(begin, step), keep_two)
        y_t[:, :, begin : begin + step] = y.T.astype(BF16).reshape(rows, narrow, step)
    streams.start(y_t)
    keep(8, hat2, hat2_hbm)
    keep(9, scale2, scale2_hbm)

    for i in (4, 5):
        kept[i].wait()
    get_dy.wait()
    ddown, dattn, dmixed, dx = x1_bf, x, hat2, hat1

    def top(at):
        ddown[at] = norm_back(x[at].astype(F32), hat2[at].astype(F32), scale2[at][:, :1], vectors[7:8]).astype(BF16)

    by_tokens(tokens, top)
    for n, (block, ks) in enumerate(turns):
        up = jnp.concatenate([front.matrix(UNIT + block, k) for k in ks], axis=1)
        down = jnp.concatenate([front.matrix(UNIT + blocks + block, k) for k in ks], axis=1)
        begins = [k * hidden + block * deep for k in ks]
        slopes = jnp.concatenate([slope[:, b : b + deep] for b in begins], axis=1)
        dpre = (nn(ddown[...], down) * slopes.astype(F32)).astype(BF16)
        more = nt(dpre, up)
        if n == 0:
            acc[...] = more
        else:
            acc[...] += more
    kept[8].wait()

    def bottom(at):
        dx1 = ddown[at].astype(F32) + acc[at]
        dattn[at] = norm_back(dx1, hat1[at].astype(F32), scale1[at][:, :1], vectors[6:7]).astype(BF16)

    by_tokens(tokens, bottom)
    take = row_blocks(rows, narrow)
    for r in range(0, rows, take):
        some = pl.ds(OUT * narrow, narrow)
        weight = jnp.concatenate(
            [w[r : r + take, k // CORES, k % CORES, some].reshape(take * narrow, deep) for k in range(cols)], axis=1
        )
        dmixed[:, r * narrow : (r + take) * narrow] = nt(dattn[...], weight).astype(BF16)
    kept[0].wait()
    kept[1].wait()
    heads_back(q, dmixed, mixed, log, kv, mask, 0, front.pairs)
    grads = share_key_grads(sharing, kv, got, sem_dkv)
    for copy in grads:
        copy.start()
    for copy in grads:
        copy.wait()
    join_key_grads(kv, got)
    chunks = 2
    chunk = tokens // chunks

    def send_on(i):
        at = pl.ds(i * chunk, chunk)
        return pltpu.make_async_remote_copy(
            dx.at[at], next_hbm.at[at], sem_next.at[i, 0], sem_next.at[i, 1],
            device_id={"section": 1 - section}, device_id_type=MESH,
        )

    stay = pltpu.make_async_copy(start_hbm, next_hbm, sem_in.at[0])

    @pl.when(section == 1)
    def _():
        stay.start()

    for i in range(chunks):
        at = pl.ds(i * chunk, chunk)
        for k in range(cols):
            there = slice(k * deep, (k + 1) * deep)
            total = dattn[at, there].astype(F32)
            for j in range(3):
                total += nn(q[at] if j == 0 else kv[0, j - 1, at], front.matrix(QKV + j, k))
            dx[at, there] = total.astype(BF16)

        @pl.when(section == 1)
        def _(i=i):
            send_on(i).start()

    for n in range(len(turns) - 2, len(turns)):
        for copy in keep_act(n):
            copy.wait()
    for i in (2, 3, 6, 7, 9):
        kept[i].wait()
    streams.wait_sent(y_t)
    streams.wait_here()

    @pl.when(section == 1)
    def _():
        stay.wait()
        for i in range(chunks):
            send_on(i).wait_send()

    @pl.when(section == 0)
    def _():
        for i in range(chunks):
            send_on(i).wait_recv()


def middle(second_in, start, weight, vectors, shift, doc_query, doc_key, group):
    tokens, width = second_in.shape
    rows, highs, _, tall, deep = weight.shape
    cols, narrow, units = highs * CORES, width // rows, shift.shape[1]
    pairs, blocks = width // PAIR, units // cols // deep
    in_any = pl.BlockSpec(memory_space=pl.ANY)
    in_vmem = pl.BlockSpec(memory_space=pltpu.VMEM)
    dma = pltpu.SemaphoreType.DMA
    flat = shaped((tokens, width), BF16)
    thin = shaped((tokens, 128), F32)
    kv = shaped((group, 2, tokens, width), BF16)
    log = shaped((pairs, 2, tokens), F32)
    wide = shaped((tokens, units), BF16)
    turned = shaped((rows, narrow, tokens), BF16)
    half = max(1, cols // 2)

    def vmem(shape):
        return pltpu.VMEM(shape.shape, shape.dtype)

    whole = pltpu.VMEM((tokens, width), F32)
    return pl.pallas_call(
        functools.partial(middle_kernel, group=group),
        in_specs=[in_any] * 3 + [in_vmem] * 4,
        out_specs=[in_any] * 13,
        out_shape=[flat, flat, kv, flat, log, flat, flat, thin, flat, thin, wide, wide, turned],
        scratch_shapes=[
            vmem(weight), vmem(flat), vmem(flat), vmem(kv), vmem(flat), vmem(log),
            pltpu.VMEM((group * tokens, tokens), F32),
            whole, vmem(flat), whole, vmem(wide),
            pltpu.VMEM((2, tokens, half * deep), BF16),
            vmem(flat), vmem(flat), vmem(thin), vmem(thin), vmem(turned),
            pltpu.VMEM((max(1, group - 1), 2, tokens, width), BF16),
            dma((2 + 2 * blocks,)), dma((2,)), dma((max(1, group - 1), 2)), dma((max(1, group - 1), 2)), dma((10,)),
            dma((2, half)), dma((2, 2)), dma((rows, 2)),
        ],
        name="middle",
        compiler_params=pltpu.CompilerParams(collective_id=3, has_side_effects=True, vmem_limit_bytes=LOW_VMEM),
        cost_estimate=pl.CostEstimate(
            flops=72 * tokens * width * width, bytes_accessed=2 * tall * deep * rows * cols, transcendentals=0
        ),
    )(second_in, start, weight, vectors, shift, doc_query, doc_key)


STAGES = 3


def low_kernel(*refs, highs, rows, group):
    (y_hbm, ddown_hbm, act_hbm, x1_hbm, dpre_hbm, dattn_hbm, q_hbm, mixed_hbm, log_hbm, x_hbm, w_hbm, kv_hbm) = refs[:12]
    bias_doc_q, bias_doc_k, pre_ref, sums_ref = refs[12:16]
    down_out, out_out, unit_out, qkv_out, small_out, layer_out, input_out, landed, landing, high_landing = refs[16:26]
    (dattn, x, q, mixed, log, w_out, w_qkv, kv, dmixed, bias, dkv_got, dx, stage, small, left, right,
     work, got, got_high, from_row, from_wide, sem_in, sem_right, sem_core, sem_load, sem_high, sem_row, sem_kv, sem_out, block, block_f32, sem_block) = refs[26:]
    tokens, width = dattn.shape
    narrow, deep = stage.shape[-2:]
    dq, dkv = q, kv
    cols = highs * CORES

    sharing = Group(group)
    streams = Streams(landed, sem_out, sharing)

    def emit(ref, out, r):
        load = pltpu.make_async_copy(ref.at[r], block, sem_block.at[0])
        load.start()
        load.wait()
        block_f32[...] = block[...].astype(F32)
        m, rest = divmod(r, rows // out.shape[1])
        store = pltpu.make_async_copy(block_f32, out.at[0, m, :, pl.ds(rest * tokens, tokens)], sem_block.at[1])
        store.start()
        store.wait()

    units = act_hbm.shape[1]
    feed_pieces = units // cols // deep
    tail = small.shape[3]
    order = [("down", i) for i in range(feed_pieces)] + [("out", 0)]
    order += [("unit", i) for i in range(feed_pieces)] + [("qkv", 0), ("qkv", 1), ("qkv", 2), ("small", 0)]
    row_first = (("down", 1), ("unit", 1))
    pieces = [(stage.at[i % STAGES], narrow, order[i] not in row_first) for i in range(len(order) - 1)]
    pieces += [(small, tail, True)]

    def give(q, ref):
        name, i = order[q]
        value = ref[...].astype(F32)
        if name in ("down", "unit"):
            (down_out if name == "down" else unit_out)[0, :, i * deep : (i + 1) * deep] = value
        elif name == "out":
            out_out[0] = value
        elif name == "qkv":
            qkv_out[0, i] = value
        else:
            small_out[...] = value

    scatter = Scatter(
        pieces, (landing, work, got, high_landing, got_high, from_row, from_wide, sem_core, sem_load, sem_high, sem_row), highs, rows, give,
    )

    inputs = [
        (ddown_hbm, dattn),
        (x1_hbm, x),
        (dattn_hbm, dattn),
        (w_hbm.at[:, :, pl.ds(OUT * narrow, narrow)], w_out),
        (mixed_hbm, mixed),
        (q_hbm, q),
        (log_hbm, log),
        (kv_hbm, kv),
        (w_hbm.at[:, :, pl.ds(QKV * narrow, 3 * narrow)], w_qkv),
        (x_hbm, x),
    ]
    loads = [pltpu.make_async_copy(a, b, sem_in.at[i]) for i, (a, b) in enumerate(inputs)]
    early = 8

    key_grads = share_key_grads(sharing, kv, dkv_got, sem_kv)
    take = row_blocks(rows, narrow)

    def prepare():
        for load in loads[2:early]:
            load.wait()
        bias[...] = jnp.where(bias_doc_k[...] == bias_doc_q[...], 0.0, NEG_BIG).astype(BF16)

        @pl.loop(0, rows // take)
        def _(r):
            at = pl.ds(pl.multiple_of(r * take * narrow, take * narrow), take * narrow)
            dmixed[:, at] = nt(dattn[...], side_by_side(w_out[pl.ds(r * take, take)])).astype(BF16)

    def fill(slot, block, loaded=None):
        @pl.loop(0, cols)
        def _(k):
            grad = nn(left[...], block(k)).astype(BF16)
            stage[slot, :, lax.div(k, CORES), lax.rem(k, CORES)] = grad.reshape(rows, narrow, deep)

    def column(ref):
        return lambda k: ref[:, pl.ds(pl.multiple_of(k * deep, deep), deep)]

    def fetch(q):
        name, i = order[q]
        source = act_hbm if name == "down" else dpre_hbm
        return [
            pltpu.make_async_copy(
                source.at[:, pl.ds(k * feed_pieces * deep + i * deep, deep)],
                right.at[q % 2, :, pl.ds(k * deep, deep)],
                sem_right.at[q % 2, k],
            )
            for k in range(cols)
        ]

    def is_feed(q):
        return q < len(order) and order[q][0] in ("down", "unit")

    def make(q):
        name, i = order[q]
        slot = q % STAGES
        if q == 0:
            loads[0].wait()
            left[...] = dattn[...].T
            loads[2].start()
        if name in ("down", "unit"):
            if (name, i) == ("unit", 0):
                left[...] = x[...].T
                loads[-1].start()
            for copy in fetch(q):
                copy.wait()
            if is_feed(q + 1):
                for copy in fetch(q + 1):
                    copy.start()
            fill(slot, column(right.at[q % 2]))
        elif name == "out":
            if is_feed(q + 1):
                for copy in fetch(q + 1):
                    copy.start()
            left[...] = mixed[...].T
            fill(slot, column(dattn))
        elif name == "qkv":
            if i == 0:
                loads[-1].wait()
            left[...] = grads_of(i).T
            fill(slot, column(x))
        else:
            small_sums()

    pairs = width // PAIR

    def heads(first, count):
        heads_back(q, dmixed, mixed, log, kv, bias, first, count)

    def exchange():
        for copy in key_grads:
            copy.start()

    def join():
        for copy in key_grads:
            copy.wait()
        for load in loads[early:-1]:
            load.wait()
        join_key_grads(kv, dkv_got)

    def grads_of(j):
        return dq[...] if j == 0 else dkv[0, j - 1]

    def input_gradient():
        for k in range(cols):
            at = slice(k * deep, (k + 1) * deep)
            total = dattn[:, at].astype(F32)
            for j in range(3):
                total += nn(grads_of(j), w_qkv[:, k, j * narrow : (j + 1) * narrow].reshape(width, deep))
            for piece in range(0, deep, min(narrow, deep)):
                r, inside = divmod(k * deep + piece, narrow)
                dx[r, inside : inside + min(narrow, deep)] = total[:, piece : piece + min(narrow, deep)].T.astype(BF16)

    def small_sums():
        vectors = jnp.concatenate([column_sum(grads_of(j).astype(F32)) for j in (0, 2)] + [sums_ref[...]], axis=0)
        vectors = vectors.astype(BF16)
        small[...] = jnp.zeros_like(small)
        lines = pre_ref.shape[1] // cols // deep
        for r in range(rows):
            for k in range(cols):
                small[r, k // CORES, k % CORES, 0:8, 0:narrow] = vectors[:, r * narrow : (r + 1) * narrow]
                for i in range(lines):
                    at = (k * lines + i) * deep
                    small[r, k // CORES, k % CORES, 8 + i : 9 + i] = pre_ref[:, at : at + deep].astype(BF16)

    def between(tick):
        if tick + 1 < len(order):
            make(tick + 1)
        if tick == 1:
            prepare()
        if 2 <= tick < 6:
            heads((tick - 2) * (pairs // 4), pairs // 4)
        if tick == 5:
            exchange()
        if tick == 6:
            join()
        if tick == 7:
            input_gradient()
            streams.start(dx)
        if tick in (8, 9, 10, 11):
            for r in range((tick - 8) * rows // 4, (tick - 7) * rows // 4):
                emit(y_hbm, layer_out, r)
        if tick == 13:
            streams.wait_here()
        if tick in (13, 14, 15, 16):
            for r in range((tick - 13) * rows // 4, (tick - 12) * rows // 4):
                emit(landed, input_out, r)

    for i, load in enumerate(loads[:-1]):
        if i != 2:
            load.start()
    for copy in fetch(0):
        copy.start()
    greet((scatter.high, scatter.row), ("core",), sharing.members(), streams.sources())
    loads[1].wait()
    make(0)
    scatter.run(between)
    streams.wait_sent(dx)


def low_back(stream, ddown, act, x1_bf, dpre, dattn, query, mixed, log_total, x, weight, shared, doc_query, doc_key, pre_sum, sums, micro):
    tokens, width = dattn.shape
    rows, cols, _, deep = weight.shape
    narrow = width // rows
    units = act.shape[1]
    feed_rows = narrow * units // cols // deep
    highs, group = cols // CORES, shared.shape[0]
    keys = group * tokens
    apart = (rows, highs, CORES)
    tail = 16
    lines = 8 + pre_sum.shape[1] // cols // deep
    assert lines <= tail and narrow <= deep
    count = 2 * (feed_rows // narrow) + 5
    wide = 2
    steps = 4 + highs - 1 + rows - 1
    slots = min(count, steps)
    in_any = pl.BlockSpec(memory_space=pl.ANY)
    in_vmem = pl.BlockSpec(memory_space=pltpu.VMEM)
    ways = {2: 1}
    block = (rows, narrow, deep)
    dma = pltpu.SemaphoreType.DMA
    args = [stream, ddown, act, x1_bf, dpre, dattn, query, mixed, log_total, x, weight, shared]
    *outs, _, _, _ = pl.pallas_call(
        functools.partial(low_kernel, highs=highs, rows=rows, group=group),
        in_specs=[in_any] * len(args) + [in_vmem] * 4,
        out_specs=[in_vmem] * 5 + [in_any] * 5,
        out_shape=[
            shaped((1, narrow, units // cols), F32),
            shaped((1, narrow, deep), F32),
            shaped((1, narrow, units // cols), F32),
            shaped((1, 3, narrow, deep), F32),
            shaped((tail, deep), F32),
            shaped((1, micro, narrow, rows // micro * tokens), F32),
            shaped((1, micro, narrow, rows // micro * tokens), F32),
            shaped((rows, narrow, tokens), BF16),
            shaped((count, highs) + block, BF16),
            shaped((count, highs - 1, ways.get(highs, 2)) + block, BF16),
        ],
        scratch_shapes=[
            pltpu.VMEM((tokens, width), BF16),
            pltpu.VMEM((tokens, width), BF16),
            pltpu.VMEM((tokens, width), BF16),
            pltpu.VMEM((tokens, width), BF16),
            pltpu.VMEM(log_total.shape, F32),
            pltpu.VMEM((rows, cols, narrow, deep), BF16),
            pltpu.VMEM((rows, cols, 3 * narrow, deep), BF16),
            pltpu.VMEM((group, 2, tokens, width), BF16),
            pltpu.VMEM((tokens, width), BF16),
            pltpu.VMEM((keys, tokens), BF16),
            pltpu.VMEM((group - 1, 2, tokens, width), BF16),
            pltpu.VMEM((rows, narrow, tokens), BF16),
            pltpu.VMEM((STAGES,) + apart + (narrow, deep), BF16),
            pltpu.VMEM(apart + (tail, deep), BF16),
            pltpu.VMEM((width, tokens), BF16),
            pltpu.VMEM((2, tokens, cols * deep), BF16),
            pltpu.VMEM((slots, highs) + block, BF16),
            pltpu.VMEM((2, highs) + block, BF16),
            pltpu.VMEM((2, ways.get(highs, 2)) + block, BF16),
            pltpu.VMEM((count - wide, rows - 1, ways.get(rows, 2), narrow, deep), BF16),
            pltpu.VMEM((wide, rows - 1, ways.get(rows, 2), highs, narrow, deep), BF16),
            dma((10,)),
            dma((2, cols)),
            dma((count, highs, 2)),
            dma((count, highs, 2)),
            dma((count, highs - 1, 2, 3)),
            dma((count, rows - 1, 2, 2)),
            dma((max(1, group - 1), 2)),
            dma((rows, 2)),
            pltpu.VMEM((narrow, tokens), BF16),
            pltpu.VMEM((narrow, tokens), F32),
            dma((2,)),
        ],
        name="low_back",
        compiler_params=pltpu.CompilerParams(collective_id=1, has_side_effects=True, vmem_limit_bytes=LOW_VMEM),
        cost_estimate=pl.CostEstimate(
            flops=64 * tokens * width * width, bytes_accessed=12 * width * units, transcendentals=0
        ),
    )(*args, doc_query, doc_key, pre_sum, sums)
    return outs


def local(tokens_in, doc_ids, cotangent, qkv_master, out_master, unit_master, down_master, unit_bias, width_bias, norm_gain):
    at = Layout(tokens_in, doc_ids)
    rows, cols, narrow = at.rows, at.cols, at.narrow
    deep, hidden = out_master.shape[2], unit_master.shape[2]

    vectors = jnp.concatenate([width_bias[0], norm_gain[0]])
    vectors = jnp.pad(vectors, ((0, 0), (0, deep - narrow)))
    small = jnp.concatenate([vectors, unit_bias.reshape(-1, deep), doc_ids.astype(F32).reshape(-1, deep)])
    small = jnp.pad(small, ((0, -small.shape[0] % 8), (0, 0)))
    second_in, start, weights, vectors, unit_shift, doc_query, doc_key = first_forward(
        small, tokens_in, cotangent, qkv_master, out_master, unit_master, down_master, rows, cols // CORES, at.group,
        at.seq_here, at.seq_len,
    )
    (
        dy, query, shared, mixed, log_total, x1_bf, hat_one, scale_one, hat_two, scale_two, act, slope, stream,
    ) = middle(second_in, start, weights, vectors, unit_shift, doc_query, doc_key, at.group)
    weights = weights.reshape(rows, cols, -1, deep)
    gain = vectors[6:]
    dh2, ddown, top_sums = top_back(dy, hat_two, scale_two, gain, True)
    dattn, dpre, pre_sum, feed_sums = feed_back(dh2, ddown, hat_one, scale_one, slope, weights, gain, True)
    sums = jnp.concatenate([feed_sums[:2], top_sums[:2], feed_sums[2:3], top_sums[2:3]])
    down_sum, out_sum, unit_sum, qkv_sum, sums, layer_out, input_grad = low_back(
        stream, ddown, act, x1_bf, dpre, dattn, query, mixed, log_total, second_in, weights, shared, doc_query, doc_key,
        pre_sum, sums, at.micro,
    )
    vectors, pre_sum = sums[:8, :narrow], sums[8 : 8 + hidden // deep].reshape(-1)
    return (
        layer_out,
        input_grad,
        qkv_sum,
        out_sum,
        unit_sum,
        down_sum,
        pre_sum[None],
        vectors[:6][None],
        vectors[6:][None],
    )


def solution(mesh):
    sections, rows, cols = (mesh.shape[name] for name in ("section", "row", "col"))
    fine = Mesh(
        mesh.devices.reshape(sections, rows, cols // CORES, CORES), ("section", "row", "high", "core")
    )
    col = ("high", "core")
    block = P("section", "row", col)
    stream = P("section", None, "row", col)
    return jax.shard_map(
        local,
        mesh=fine,
        in_specs=(
            P(None, "row", col),
            P(None, col, None),
            P(None, "row", col),
            P("section", None, "row", col),
            block,
            block,
            block,
            P("section", col),
            P("section", None, "row"),
            P("section", None, "row"),
        ),
        out_specs=(
            stream,
            stream,
            stream,
            block,
            block,
            block,
            P("section", col),
            P("section", None, "row"),
            P("section", None, "row"),
        ),
        check_vma=False,
    )
```

time: 630 us -> 579 us (0.919)
  Pallas kernels: 515 us -> 546 us
  waiting for transfers between devices: 30.1 us -> 0 us
  local copies, waits for them, and re-layouts: 41.2 us -> 17.8 us
  starting transfers between devices: 22.2 us -> 0 us
    pallas_call x0 -> x1, Pallas kernels: none -> 130 us  [middle(): pl.pallas_call(functools.partial(middle_kernel, group=group), in_specs=[i...]
    pallas_call x12 -> x2, Pallas kernels: 145 us -> 23.6 us  [call(): pl.pallas_call(kernel, grid=grid, in_specs=in_specs, out_specs=out_specs,...]
    ppermute x11 -> x0, waiting for transfers between devices: 30.1 us -> none  [the longest x8 26.3 us: to_features(): got.append(lax.ppermute(block, ('row', 'core'), pairs))]
    ppermute x11 -> x0, starting transfers between devices: 22.2 us -> none  [the longest x8 20.2 us: to_features(): got.append(lax.ppermute(block, ('row', 'core'), pairs))]
    pallas_call x1, Pallas kernels: 174 us -> 186 us  [low_back(): pl.pallas_call(functools.partial(low_kernel, highs=highs, rows=rows, grou...]
    pallas_call x1, Pallas kernels: 196 us -> 207 us  [first_forward(): pl.pallas_call(functools.partial(first_kernel, highs=highs, rows=rows, gr...]
  transfers between devices with their start and end apart: 11 -> 0, of which waited for: 6 -> 0; matrix products, arithmetic and copies ran while one was open for 3% -> 0% of each run, Pallas kernels for 1% -> 0%
where the time goes in v3:
time: 579 us; the launch traced here: 569 us
  Pallas kernels  546 us (94%)
  local copies, waits for them, and re-layouts  17.8 us (3%)
    pallas_call x1, Pallas kernels, first_forward(): pl.pallas_call(functools.partial(first_kernel, highs=highs, rows=rows, gr...  207 us
    pallas_call x1, Pallas kernels, low_back(): pl.pallas_call(functools.partial(low_kernel, highs=highs, rows=rows, grou...  186 us
    pallas_call x1, Pallas kernels, middle(): pl.pallas_call(functools.partial(middle_kernel, group=group), in_specs=[i...  130 us
    pallas_call x2, Pallas kernels, call(): pl.pallas_call(kernel, grid=grid, in_specs=in_specs, out_specs=out_specs,...  23.6 us

profile of v3, /device:TPU:10, one launch (start us, length us, event | category | flops | bytes accessed | tf_op | source)
XLA Modules:
  0.0 569.1 jit_solution(9905138090130745069)
XLA Ops:
  1.2 1.3 reduce.5
  2.5 0.7 convert_reduce_fusion
  3.3 0.7 copy.23
  4.0 1.3 select_maximum_fusion.refs_0_
  5.3 207.2 %first_forward.1 = (bf16[512,1024]{1,0:T(8,128)(2,1)}, bf16[512,1024]{1,0:T(8,128)(2,1)}, bf16[4,2,2,3072,256]{4,3,2,1,0:T(8,128)(2,1)}, f32[8,1024]{1,0:T(8,128...) custom-call(f32[24,256]{1,0:T(8,128)} %select_maximum_fusion.refs_0_, bf16[2,256,1024]{2,1,0:T(8,128)(2,1)} %refs_1_.1, ...), custom_call_target="tpu_custom_call" | custom-call | flops 12884901888 | bytes 25165824 | tf_op jit(solution)/shard_map/first_forward/pallas_call | solution.py:952
  212.4 1.4 slice.27.n_ref.refs_7_
  213.8 129.8 %middle.1 = (bf16[512,1024]{1,0:T(8,128)(2,1)}, bf16[512,1024]{1,0:T(8,128)(2,1)}, bf16[2,2,512,1024]{3,2,1,0:T(8,128)(2,1)}, bf16[512,1024]{1,0:T(8,128)(2,1)},...) custom-call(bf16[512,1024]{1,0:T(8,128)(2,1)} %get-tuple-element.43., ...), custom_call_target="tpu_custom_call" | custom-call | flops 38654705664 | bytes 25165824 | tf_op jit(solution)/shard_map/middle/pallas_call | solution.py:1307
  343.6 4.6 top_back.1
  348.2 19.0 %feed_back.1 = (bf16[512,1024]{1,0:T(8,128)(2,1)}, bf16[512,4096]{1,0:T(8,128)(2,1)}, f32[1,4096]{1,0:T(1,128)}, f32[8,1024]{1,0:T(8,128)}) custom-call(f32[512,1024]{1,0:T(8,128)} %get-tuple-element.57.refs_0_, bf16[512,1024]{1,0:T(8,128)(2,1)} %get-tuple-element.54.refs_1_, bf16[512,1024]{1,0:T(8,128)(2,1)} %get-tuple-element.58.refs_2_, ...), custom_call_target="tpu_custom_call" | custom-call | flops 8589934592 | bytes 16777216 | tf_op jit(solution)/shard_map/feed_back/pallas_call | solution.py:41
  367.3 0.8 slice.30
  368.0 0.8 slice.28
  368.8 0.8 slice.31
  369.6 0.8 slice.29
  370.3 0.6 pad_maximum_fusion.refs_15_
  371.0 185.6 %low_back.1 = (f32[1,256,1024]{2,1,0:T(8,128)}, f32[1,256,256]{2,1,0:T(8,128)}, f32[1,256,1024]{2,1,0:T(8,128)}, f32[1,3,256,256]{3,2,1,0:T(8,128)}, f32[16,256]...) custom-call(bf16[4,256,512]{2,1,0:T(8,128)(2,1)} %get-tuple-element., ...), custom_call_target="tpu_custom_call" | custom-call | flops 34359738368 | bytes 50331648 | tf_op jit(solution)/shard_map/low_back/pallas_call | solution.py:1563
  556.6 1.4 slice_bitcast_fusion.2
  558.0 0.7 slice_bitcast_fusion.1
  558.7 0.7 slice_bitcast_fusion
  560.6 3.2 copy.30
  563.9 1.3 copy.31
  565.2 0.9 copy.32
  566.1 0.7 copy.33
  566.8 1.0 copy.34
  567.7 1.0 copy.35
  (15 shorter events, 1.8 us)
Async XLA Ops:
  556.6 7.3 %copy-start = (f32[1,2,256,1024]{3,2,1,0:T(8,128)S(1)}, f32[1,2,256,1024]{3,2,1,0:T(8,128)}, u32[]{:S(2)}) copy-start(f32[1,2,256,1024]{3,2,1,0:T(8,128)} %get-tuple-element.96) | copy-start | bytes 6291460
  560.6 4.6 copy-start.3
  560.6 5.5 copy-start.4
  563.8 2.9 copy-start.2
  563.8 3.9 copy-start.1

commit v4 on v3

--- a/solution.py
+++ b/solution.py
@@ -17,7 +17,7 @@
 MESH = pl.DeviceIdType.MESH
 
 QKV, OUT, UNIT = 0, 3, 4
-FEED_BLOCKS = 2
+FEED_BLOCKS = 4
 
 F32 = jnp.float32
 BF16 = jnp.bfloat16
@@ -169,53 +169,32 @@
     return jnp.sum(value, axis=0, keepdims=True)
 
 
-def top_back_kernel(dy_ref, hat_ref, scale_ref, n_ref, dh2_ref, ddown_ref, *sums_ref):
-    for ref in sums_ref:
-        ref[...] = jnp.zeros_like(ref)
-
-    def some(at):
-        dy, hat = dy_ref[at].astype(F32), hat_ref[at]
-        dh2 = norm_back(dy, hat, scale_ref[at][:, :1], n_ref[1:2])
-        dh2_ref[at] = dh2
-        ddown = dh2.astype(BF16)
-        ddown_ref[at] = ddown
-        for ref in sums_ref:
-            ref[0:1] += column_sum(ddown.astype(F32))
-            ref[1:2] += column_sum(dy)
-            ref[2:3] += column_sum(dy * hat)
-
-    by_tokens(dy_ref.shape[0], some)
-
-
-def top_back(dy, hat2, scale2, gain, sums_too):
-    tokens, width = hat2.shape
-    flat = held((tokens, width))
-    return call(
-        top_back_kernel,
-        (1,),
-        [flat, flat, held((tokens, 128)), held(gain.shape)],
-        [flat, flat] + [held((8, width))] * sums_too,
-        [shaped((tokens, width), F32), shaped((tokens, width), BF16)] + [shaped((8, width), F32)] * sums_too,
-        [],
-        "top_back",
-        20 * tokens * width,
-        12 * tokens * width,
-        (dy, hat2, scale2, gain),
-    )
-
-
-def feed_back_kernel(*refs, steps, sums_too):
-    dh2_ref, ddown_ref, hat1_ref, scale1_ref, slope_ref, wu_ref, wd_ref, n_ref, dattn_ref = refs[:9]
-    acc_ref = refs[-1]
+def feed_back_kernel(*refs, steps):
+    (dy_ref, hat2_ref, scale2_ref, hat1_ref, scale1_ref, slope_ref, wu_ref, wd_ref, v_ref) = refs[:9]
+    (ddown_ref, dattn_ref, dpre_ref, pre_ref, top_ref, feed_ref, acc_ref) = refs[9:]
     s = pl.program_id(0)
-    tokens, width = dh2_ref.shape
+    tokens, width = dy_ref.shape
+
+    @pl.when(s == 0)
+    def _():
+        top_ref[...] = jnp.zeros_like(top_ref)
+        feed_ref[...] = jnp.zeros_like(feed_ref)
+
+        def some(at):
+            dy, hat = dy_ref[at].astype(F32), hat2_ref[at].astype(F32)
+            ddown = norm_back(dy, hat, scale2_ref[at][:, :1], v_ref[7:8]).astype(BF16)
+            ddown_ref[at] = ddown
+            top_ref[0:1] += column_sum(ddown.astype(F32))
+            top_ref[1:2] += column_sum(dy)
+            top_ref[2:3] += column_sum(dy * hat)
+
+        by_tokens(tokens, some)
+
     dact = nn(ddown_ref[...], hidden_columns(wd_ref[...], width))
     dpre = (dact * slope_ref[...].astype(F32)).astype(BF16)
     back = nt(dpre, hidden_columns(wu_ref[...], width))
-    if sums_too:
-        dpre_ref, pre_ref, sums_ref = refs[9:12]
-        dpre_ref[...] = dpre
-        pre_ref[...] = column_sum(dpre.astype(F32))
+    dpre_ref[...] = dpre
+    pre_ref[...] = column_sum(dpre.astype(F32))
 
     @pl.when(s == 0)
     def _():
@@ -227,41 +206,40 @@
 
     @pl.when(s == steps - 1)
     def _():
-        if sums_too:
-            sums_ref[...] = jnp.zeros_like(sums_ref)
-
         def some(at):
-            dx1, hat = dh2_ref[at] + acc_ref[at], hat1_ref[at]
-            dattn = norm_back(dx1, hat, scale1_ref[at][:, :1], n_ref[0:1]).astype(BF16)
+            dx1, hat = ddown_ref[at].astype(F32) + acc_ref[at], hat1_ref[at].astype(F32)
+            dattn = norm_back(dx1, hat, scale1_ref[at][:, :1], v_ref[6:7]).astype(BF16)
             dattn_ref[at] = dattn
-            if sums_too:
-                sums_ref[0:1] += column_sum(dattn.astype(F32))
-                sums_ref[1:2] += column_sum(dx1)
-                sums_ref[2:3] += column_sum(dx1 * hat)
+            feed_ref[0:1] += column_sum(dattn.astype(F32))
+            feed_ref[1:2] += column_sum(dx1)
+            feed_ref[2:3] += column_sum(dx1 * hat)
 
         by_tokens(tokens, some)
 
 
-def feed_back(dh2, ddown, hat1, scale1, slope, weight, gain, sums_too):
-    tokens, width = dh2.shape
+def feed_back(dy, hat2, scale2, hat1, scale1, slope, weight, vectors):
+    tokens, width = dy.shape
     units = slope.shape[1]
     steps, first, second, wide, line = feed_specs(weight, tokens, width, units)
-    flat = held((tokens, width))
-    out_specs, out_shape = [flat], [shaped((tokens, width), BF16)]
-    if sums_too:
-        out_specs += [wide, line, held((8, width))]
-        out_shape += [shaped((tokens, units), BF16), shaped((1, units), F32), shaped((8, width), F32)]
+    flat, thin = held((tokens, width)), held((tokens, 128))
     return call(
-        functools.partial(feed_back_kernel, steps=steps, sums_too=sums_too),
+        functools.partial(feed_back_kernel, steps=steps),
         (steps,),
-        [flat, flat, flat, held((tokens, 128)), wide, first, second, held(gain.shape)],
-        out_specs,
-        out_shape,
+        [flat, flat, thin, flat, thin, wide, first, second, held(vectors.shape)],
+        [flat, flat, wide, line, held((8, width)), held((8, width))],
+        [
+            shaped((tokens, width), BF16),
+            shaped((tokens, width), BF16),
+            shaped((tokens, units), BF16),
+            shaped((1, units), F32),
+            shaped((8, width), F32),
+            shaped((8, width), F32),
+        ],
         [pltpu.VMEM((tokens, width), F32)],
         "feed_back",
         4 * tokens * width * units,
         4 * width * units,
-        (dh2, ddown, hat1, scale1, slope, weight, weight, gain),
+        (dy, hat2, scale2, hat1, scale1, slope, weight, weight, vectors),
     )
 
 
@@ -547,7 +525,7 @@
 class Gather:
     def __init__(self, pieces, sems, highs, rows):
         self.pieces = pieces
-        self.sem_row, self.sem_high, self.sem_core = sems
+        self.sem_row, self.sem_high, self.sem_core, self.sem_one = sems
         self.row, self.high = Spread("row", rows), Spread("high", highs)
         self.core = lax.axis_index("core")
         self.sent = []
@@ -566,21 +544,45 @@
             ref, ref, sems.at[0], sems.at[1], device_id=line.neighbour(right), device_id_type=MESH
         )
 
+    def one(self, q, right, i):
+        ref, first, count, _ = self.pieces[q]
+        ref = ref.at[i, self.high.here, self.core, pl.ds(first, count)]
+        sems = self.sem_one.at[q, i, 0 if right else 1]
+        return pltpu.make_async_remote_copy(
+            ref, ref, sems.at[0], sems.at[1], device_id=self.high.neighbour(right), device_id_type=MESH
+        )
+
+    def start(self, there, copy):
+        @pl.when(there)
+        def _():
+            copy().start()
+
+        self.sent.append((there, copy))
+
+    def over(self, q, i, there=True):
+        for right, also, _ in self.high.sends(1):
+            self.start(also & there, functools.partial(self.one, q, right, i))
+
     def push(self, q, line, step):
+        if line is self.high and step == 1 and self.pieces[q][3]:
+            return
         for right, there, i in line.sends(step):
-
-            @pl.when(there)
-            def _(right=right, i=i):
-                self.copy(q, line, step, right, i).start()
-
-            self.sent.append((q, line, step, right, there, i))
+            self.start(there, functools.partial(self.copy, q, line, step, right, i))
 
     def pull(self, q, line, step):
+        row_first = self.pieces[q][3]
         for right, there in line.gets(step):
 
             @pl.when(there)
             def _(right=right):
-                self.copy(q, line, step, right, line.here).wait_recv()
+                if line is self.high and step == 1 and row_first:
+                    for i in range(self.row.size):
+                        self.one(q, right, i).wait_recv()
+                else:
+                    self.copy(q, line, step, right, line.here).wait_recv()
+
+            if line is self.row and row_first:
+                self.over(q, line.here - step if right else line.here + step, there)
 
     def to_core(self, q):
         ref, first, count, _ = self.pieces[q]
@@ -592,7 +594,12 @@
 
     def stages(self, q):
         first, second = (self.row, self.high) if self.pieces[q][3] else (self.high, self.row)
-        steps = [lambda: self.push(q, first, 1)]
+        def begin():
+            self.push(q, first, 1)
+            if first is self.row:
+                self.over(q, self.row.here)
+
+        steps = [begin]
         lines = [(first, i) for i in range(1, first.size)] + [(second, i) for i in range(1, second.size)]
         for n, (line, step) in enumerate(lines):
 
@@ -617,11 +624,11 @@
             between(tick, tick - depth + 1)
 
     def finish(self):
-        for q, line, step, right, there, i in self.sent:
+        for there, copy in self.sent:
 
             @pl.when(there)
-            def _(q=q, line=line, step=step, right=right, i=i):
-                self.copy(q, line, step, right, i).wait_send()
+            def _(copy=copy):
+                copy().wait_send()
 
 
 class Group:
@@ -737,10 +744,10 @@
 
 
 def first_kernel(*refs, highs, rows, group, micro, seq_here, seq_len):
-    (small_ref, tokens_hbm, cot_hbm, qkv_ref, out_ref, unit_ref, down_ref) = refs[:7]
-    (next_hbm, start_ref, w_hbm, vectors, shift, doc_q, doc_k) = refs[7:14]
+    (tokens_hbm, cot_hbm, qkv_ref, out_ref, unit_ref, down_ref, unit_bias, width_bias, gain, docs) = refs[:10]
+    (next_hbm, start_ref, w_hbm, vectors, shift, doc_q, doc_k) = refs[10:17]
     (w, small, turned, x, q, kv, mixed, mask, x1, x1_bf, acc, y,
-     sem_row, sem_high, sem_core, sem_x, sem_kv, sem_y, sem_w, sem_next) = refs[14:]
+     sem_row, sem_high, sem_core, sem_one, sem_x, sem_kv, sem_y, sem_w, sem_next) = refs[17:]
     tokens, width = x.shape
     narrow, deep = width // rows, w.shape[-1]
     cols = highs * CORES
@@ -759,7 +766,16 @@
         for j, ref in enumerate((unit_ref, down_ref)):
             first = (UNIT + j * blocks + i) * narrow
             w[row, high, core, first : first + narrow] = ref[0, :, at].astype(BF16)
-    small[row, high, core] = small_ref[...]
+    small[row, high, core, 0:6, 0:narrow] = width_bias[0]
+    small[row, high, core, 6:8, 0:narrow] = gain[0]
+    for i in range(blocks):
+        small[row, high, core, 8 + i : 9 + i] = unit_bias[:, i * deep : (i + 1) * deep]
+    lines = seq_len // deep
+    for m in range(micro):
+        for i in range(seq_here):
+            for j in range(lines):
+                at = 8 + blocks + (m * seq_here + i) * lines + j
+                small[row, high, core, at : at + 1] = docs[m, i : i + 1, j * deep : (j + 1) * deep].astype(F32)
 
     def goes(j):
         place = ((j // group) * CORES + core) * group + j % group
@@ -809,7 +825,7 @@
     order = [0, 1, 2, 3] + [UNIT + j * blocks + i for i in range(blocks) for j in range(2)]
     pieces = [(small, 0, small.shape[3], True)]
     pieces += [(w, i * narrow, narrow, row_first[n]) for n, i in enumerate(order)]
-    gather = Gather(pieces, (sem_row, sem_high, sem_core), highs, rows)
+    gather = Gather(pieces, (sem_row, sem_high, sem_core, sem_one), highs, rows)
 
     def to_hbm(q):
         at = pl.ds(order[q - 1] * narrow, narrow)
@@ -868,6 +884,8 @@
     base = 3
 
     def between(tick, done):
+        if tick == 2:
+            begin()
         if done >= 1:
             to_hbm(done).start()
         if done == 0:
@@ -903,7 +921,6 @@
                     for k in range(0, cols, half):
                         front.feed(block, range(k, k + half), block == 0 and k == 0)
 
-    begin()
     gather.run(between)
     for i in range(chunks):
         at = pl.ds(i * chunk, chunk)
@@ -937,8 +954,9 @@
             send_out(i).wait_recv()
 
 
-def first_forward(small, tokens_in, cotangent, qkv, out, unit, down, rows, highs, group, seq_here, seq_len):
+def first_forward(tokens_in, cotangent, qkv, out, unit, down, unit_bias, width_bias, gain, docs, rows, highs, group):
     micro, narrow, _ = tokens_in.shape
+    _, seq_here, seq_len = docs.shape
     deep, hidden = out.shape[2], unit.shape[2]
     width, cols, blocks = narrow * rows, highs * CORES, hidden // deep
     tokens = seq_len // group
@@ -947,13 +965,15 @@
     in_any = pl.BlockSpec(memory_space=pl.ANY)
     in_vmem = pl.BlockSpec(memory_space=pltpu.VMEM)
     count = 1 + 4 + 2 * blocks
+    small_rows = 8 + blocks + micro * seq_here * seq_len // deep
+    small_rows += -small_rows % 8
     dma = pltpu.SemaphoreType.DMA
     flat, flat_f32 = pltpu.VMEM((tokens, width), BF16), pltpu.VMEM((tokens, width), F32)
     return pl.pallas_call(
         functools.partial(
             first_kernel, highs=highs, rows=rows, group=group, micro=micro, seq_here=seq_here, seq_len=seq_len
         ),
-        in_specs=[in_vmem, in_any, in_any] + [in_vmem] * 4,
+        in_specs=[in_any] * 2 + [in_vmem] * 8,
         out_specs=[in_any, in_vmem, in_any] + [in_vmem] * 4,
         out_shape=[
             shaped((tokens, width), BF16),
@@ -966,7 +986,7 @@
         ],
         scratch_shapes=[
             pltpu.VMEM(apart + (tall, deep), BF16),
-            pltpu.VMEM(apart + small.shape, F32),
+            pltpu.VMEM(apart + (small_rows, deep), F32),
             pltpu.VMEM((rows, narrow, tokens), BF16),
             flat,
             flat,
@@ -980,6 +1000,7 @@
             dma((count, rows - 1, 2, 2)),
             dma((count, highs - 1, 2, 2)),
             dma((count, 2)),
+            dma((count, rows, 2, 2)),
             dma((rows, 2)),
             dma((max(1, group - 1), 2)),
             dma((4, 2)),
@@ -991,7 +1012,7 @@
         cost_estimate=pl.CostEstimate(
             flops=24 * tokens * width * width, bytes_accessed=2 * tall * deep * rows * cols, transcendentals=0
         ),
-    )(small, tokens_in, cotangent, qkv, out, unit, down)
+    )(tokens_in, cotangent, qkv, out, unit, down, unit_bias, width_bias, gain, docs)
 
 
 class Streams:
@@ -1147,7 +1168,7 @@
     keep(4, x1_bf, x1_hbm)
     keep(5, hat1, hat1_hbm)
     keep(6, scale1, scale1_hbm)
-    half = max(1, cols // 2)
+    half = cols if tokens * cols * deep <= 1 << 19 else max(1, cols // 2)
     turns = [(block, range(k, k + half)) for block in range(blocks) for k in range(0, cols, half)]
 
     def keep_act(n):
@@ -1298,7 +1319,7 @@
     log = shaped((pairs, 2, tokens), F32)
     wide = shaped((tokens, units), BF16)
     turned = shaped((rows, narrow, tokens), BF16)
-    half = max(1, cols // 2)
+    half = cols if tokens * cols * deep <= 1 << 19 else max(1, cols // 2)
 
     def vmem(shape):
         return pltpu.VMEM(shape.shape, shape.dtype)
@@ -1331,11 +1352,11 @@
 
 
 def low_kernel(*refs, highs, rows, group):
-    (y_hbm, ddown_hbm, act_hbm, x1_hbm, dpre_hbm, dattn_hbm, q_hbm, mixed_hbm, log_hbm, x_hbm, w_hbm, kv_hbm) = refs[:12]
-    bias_doc_q, bias_doc_k, pre_ref, sums_ref = refs[12:16]
-    down_out, out_out, unit_out, qkv_out, small_out, layer_out, input_out, landed, landing, high_landing = refs[16:26]
+    (ddown_hbm, act_hbm, x1_hbm, dpre_hbm, dattn_hbm, q_hbm, mixed_hbm, log_hbm, x_hbm, w_hbm, kv_hbm) = refs[:11]
+    bias_doc_q, bias_doc_k, pre_ref, top_sums, feed_sums = refs[11:16]
+    down_out, out_out, unit_out, qkv_out, small_out, landed, landing, high_landing = refs[16:24]
     (dattn, x, q, mixed, log, w_out, w_qkv, kv, dmixed, bias, dkv_got, dx, stage, small, left, right,
-     work, got, got_high, from_row, from_wide, sem_in, sem_right, sem_core, sem_load, sem_high, sem_row, sem_kv, sem_out, block, block_f32, sem_block) = refs[26:]
+     work, got, got_high, from_row, from_wide, sem_in, sem_right, sem_core, sem_load, sem_high, sem_row, sem_kv, sem_out) = refs[24:]
     tokens, width = dattn.shape
     narrow, deep = stage.shape[-2:]
     dq, dkv = q, kv
@@ -1343,29 +1364,19 @@
 
     sharing = Group(group)
     streams = Streams(landed, sem_out, sharing)
-
-    def emit(ref, out, r):
-        load = pltpu.make_async_copy(ref.at[r], block, sem_block.at[0])
-        load.start()
-        load.wait()
-        block_f32[...] = block[...].astype(F32)
-        m, rest = divmod(r, rows // out.shape[1])
-        store = pltpu.make_async_copy(block_f32, out.at[0, m, :, pl.ds(rest * tokens, tokens)], sem_block.at[1])
-        store.start()
-        store.wait()
 
     units = act_hbm.shape[1]
     feed_pieces = units // cols // deep
     tail = small.shape[3]
     order = [("down", i) for i in range(feed_pieces)] + [("out", 0)]
     order += [("unit", i) for i in range(feed_pieces)] + [("qkv", 0), ("qkv", 1), ("qkv", 2), ("small", 0)]
-    row_first = (("down", 1), ("unit", 1))
+    row_first = (("unit", 0),)
     pieces = [(stage.at[i % STAGES], narrow, order[i] not in row_first) for i in range(len(order) - 1)]
     pieces += [(small, tail, True)]
 
     def give(q, ref):
         name, i = order[q]
-        value = ref[...].astype(F32)
+        value = ref[...]
         if name in ("down", "unit"):
             (down_out if name == "down" else unit_out)[0, :, i * deep : (i + 1) * deep] = value
         elif name == "out":
@@ -1492,7 +1503,9 @@
                 dx[r, inside : inside + min(narrow, deep)] = total[:, piece : piece + min(narrow, deep)].T.astype(BF16)
 
     def small_sums():
-        vectors = jnp.concatenate([column_sum(grads_of(j).astype(F32)) for j in (0, 2)] + [sums_ref[...]], axis=0)
+        vectors = [column_sum(grads_of(j).astype(F32)) for j in (0, 2)]
+        vectors += [feed_sums[0:2], top_sums[0:2], feed_sums[2:3], top_sums[2:3]]
+        vectors = jnp.concatenate(vectors, axis=0)
         vectors = vectors.astype(BF16)
         small[...] = jnp.zeros_like(small)
         lines = pre_ref.shape[1] // cols // deep
@@ -1503,28 +1516,22 @@
                     at = (k * lines + i) * deep
                     small[r, k // CORES, k % CORES, 8 + i : 9 + i] = pre_ref[:, at : at + deep].astype(BF16)
 
+    share = max(1, pairs // 8)
+
     def between(tick):
+        if tick == 1:
+            prepare()
+        if 2 <= tick < 9:
+            heads((tick - 2) * share, share if tick < 8 else pairs - 6 * share)
+        if tick == 8:
+            exchange()
+        if tick == 9:
+            join()
         if tick + 1 < len(order):
             make(tick + 1)
-        if tick == 1:
-            prepare()
-        if 2 <= tick < 6:
-            heads((tick - 2) * (pairs // 4), pairs // 4)
-        if tick == 5:
-            exchange()
-        if tick == 6:
-            join()
-        if tick == 7:
+        if tick == 9:
             input_gradient()
             streams.start(dx)
-        if tick in (8, 9, 10, 11):
-            for r in range((tick - 8) * rows // 4, (tick - 7) * rows // 4):
-                emit(y_hbm, layer_out, r)
-        if tick == 13:
-            streams.wait_here()
-        if tick in (13, 14, 15, 16):
-            for r in range((tick - 13) * rows // 4, (tick - 12) * rows // 4):
-                emit(landed, input_out, r)
 
     for i, load in enumerate(loads[:-1]):
         if i != 2:
@@ -1536,9 +1543,10 @@
     make(0)
     scatter.run(between)
     streams.wait_sent(dx)
-
-
-def low_back(stream, ddown, act, x1_bf, dpre, dattn, query, mixed, log_total, x, weight, shared, doc_query, doc_key, pre_sum, sums, micro):
+    streams.wait_here()
+
+
+def low_back(ddown, act, x1_bf, dpre, dattn, query, mixed, log_total, x, weight, shared, doc_query, doc_key, pre_sum, top_sums, feed_sums):
     tokens, width = dattn.shape
     rows, cols, _, deep = weight.shape
     narrow = width // rows
@@ -1551,7 +1559,7 @@
     lines = 8 + pre_sum.shape[1] // cols // deep
     assert lines <= tail and narrow <= deep
     count = 2 * (feed_rows // narrow) + 5
-    wide = 2
+    wide = 1
     steps = 4 + highs - 1 + rows - 1
     slots = min(count, steps)
     in_any = pl.BlockSpec(memory_space=pl.ANY)
@@ -1559,19 +1567,17 @@
     ways = {2: 1}
     block = (rows, narrow, deep)
     dma = pltpu.SemaphoreType.DMA
-    args = [stream, ddown, act, x1_bf, dpre, dattn, query, mixed, log_total, x, weight, shared]
-    *outs, _, _, _ = pl.pallas_call(
+    args = [ddown, act, x1_bf, dpre, dattn, query, mixed, log_total, x, weight, shared]
+    *outs, _, _ = pl.pallas_call(
         functools.partial(low_kernel, highs=highs, rows=rows, group=group),
-        in_specs=[in_any] * len(args) + [in_vmem] * 4,
-        out_specs=[in_vmem] * 5 + [in_any] * 5,
+        in_specs=[in_any] * len(args) + [in_vmem] * 5,
+        out_specs=[in_vmem] * 5 + [in_any] * 3,
         out_shape=[
-            shaped((1, narrow, units // cols), F32),
-            shaped((1, narrow, deep), F32),
-            shaped((1, narrow, units // cols), F32),
-            shaped((1, 3, narrow, deep), F32),
-            shaped((tail, deep), F32),
-            shaped((1, micro, narrow, rows // micro * tokens), F32),
-            shaped((1, micro, narrow, rows // micro * tokens), F32),
+            shaped((1, narrow, units // cols), BF16),
+            shaped((1, narrow, deep), BF16),
+            shaped((1, narrow, units // cols), BF16),
+            shaped((1, 3, narrow, deep), BF16),
+            shaped((tail, deep), BF16),
             shaped((rows, narrow, tokens), BF16),
             shaped((count, highs) + block, BF16),
             shaped((count, highs - 1, ways.get(highs, 2)) + block, BF16),
@@ -1606,56 +1612,66 @@
             dma((count, rows - 1, 2, 2)),
             dma((max(1, group - 1), 2)),
             dma((rows, 2)),
-            pltpu.VMEM((narrow, tokens), BF16),
-            pltpu.VMEM((narrow, tokens), F32),
-            dma((2,)),
         ],
         name="low_back",
         compiler_params=pltpu.CompilerParams(collective_id=1, has_side_effects=True, vmem_limit_bytes=LOW_VMEM),
         cost_estimate=pl.CostEstimate(
             flops=64 * tokens * width * width, bytes_accessed=12 * width * units, transcendentals=0
         ),
-    )(*args, doc_query, doc_key, pre_sum, sums)
+    )(*args, doc_query, doc_key, pre_sum, top_sums, feed_sums)
     return outs
+
+
+def finish_kernel(down, out, unit, qkv, small, first, second, *outs):
+    layer_out, input_grad, qkv_out, out_out, unit_out, down_out, bias_out, width_out, gain_out = outs
+    for ref, to in ((down, down_out), (out, out_out), (unit, unit_out), (qkv, qkv_out)):
+        to[...] = ref[...].astype(F32)
+    rows, narrow, tokens = first.shape
+    for ref, to in ((first, layer_out), (second, input_grad)):
+        per = rows // to.shape[1]
+        for r in range(rows):
+            to[0, r // per, :, r % per * tokens : (r % per + 1) * tokens] = ref[r].astype(F32)
+    values = small[...].astype(F32)
+    width_out[0] = values[0:6, :narrow]
+    gain_out[0] = values[6:8, :narrow]
+    deep = values.shape[1]
+    for i in range(bias_out.shape[1] // deep):
+        bias_out[:, i * deep : (i + 1) * deep] = values[8 + i : 9 + i]
+
+
+def finish(down, out, unit, qkv, small, first, second, micro):
+    rows, narrow, tokens = first.shape
+    stream = shaped((1, micro, narrow, rows // micro * tokens), F32)
+    grads = [shaped(grad.shape, F32) for grad in (qkv, out, unit, down)]
+    rest = [shaped((1, down.shape[2]), F32), shaped((1, 6, narrow), F32), shaped((1, 2, narrow), F32)]
+    return pl.pallas_call(
+        finish_kernel,
+        out_shape=[stream, stream, *grads, *rest],
+        name="finish",
+        compiler_params=pltpu.CompilerParams(vmem_limit_bytes=VMEM_BYTES),
+    )(down, out, unit, qkv, small, first, second)
 
 
 def local(tokens_in, doc_ids, cotangent, qkv_master, out_master, unit_master, down_master, unit_bias, width_bias, norm_gain):
     at = Layout(tokens_in, doc_ids)
-    rows, cols, narrow = at.rows, at.cols, at.narrow
-    deep, hidden = out_master.shape[2], unit_master.shape[2]
-
-    vectors = jnp.concatenate([width_bias[0], norm_gain[0]])
-    vectors = jnp.pad(vectors, ((0, 0), (0, deep - narrow)))
-    small = jnp.concatenate([vectors, unit_bias.reshape(-1, deep), doc_ids.astype(F32).reshape(-1, deep)])
-    small = jnp.pad(small, ((0, -small.shape[0] % 8), (0, 0)))
+    rows, cols, deep = at.rows, at.cols, out_master.shape[2]
+
     second_in, start, weights, vectors, unit_shift, doc_query, doc_key = first_forward(
-        small, tokens_in, cotangent, qkv_master, out_master, unit_master, down_master, rows, cols // CORES, at.group,
-        at.seq_here, at.seq_len,
+        tokens_in, cotangent, qkv_master, out_master, unit_master, down_master, unit_bias, width_bias, norm_gain, doc_ids,
+        rows, cols // CORES, at.group,
     )
     (
         dy, query, shared, mixed, log_total, x1_bf, hat_one, scale_one, hat_two, scale_two, act, slope, stream,
     ) = middle(second_in, start, weights, vectors, unit_shift, doc_query, doc_key, at.group)
     weights = weights.reshape(rows, cols, -1, deep)
-    gain = vectors[6:]
-    dh2, ddown, top_sums = top_back(dy, hat_two, scale_two, gain, True)
-    dattn, dpre, pre_sum, feed_sums = feed_back(dh2, ddown, hat_one, scale_one, slope, weights, gain, True)
-    sums = jnp.concatenate([feed_sums[:2], top_sums[:2], feed_sums[2:3], top_sums[2:3]])
-    down_sum, out_sum, unit_sum, qkv_sum, sums, layer_out, input_grad = low_back(
-        stream, ddown, act, x1_bf, dpre, dattn, query, mixed, log_total, second_in, weights, shared, doc_query, doc_key,
-        pre_sum, sums, at.micro,
+    ddown, dattn, dpre, pre_sum, top_sums, feed_sums = feed_back(
+        dy, hat_two, scale_two, hat_one, scale_one, slope, weights, vectors
     )
-    vectors, pre_sum = sums[:8, :narrow], sums[8 : 8 + hidden // deep].reshape(-1)
-    return (
-        layer_out,
-        input_grad,
-        qkv_sum,
-        out_sum,
-        unit_sum,
-        down_sum,
-        pre_sum[None],
-        vectors[:6][None],
-        vectors[6:][None],
+    *grads, input_grad = low_back(
+        ddown, act, x1_bf, dpre, dattn, query, mixed, log_total, second_in, weights, shared, doc_query, doc_key,
+        pre_sum, top_sums, feed_sums,
     )
+    return finish(*grads, stream, input_grad, at.micro)
 
 
 def solution(mesh):

time: 579 us -> 515 us (0.89)
  Pallas kernels: 546 us -> 504 us
  local copies, waits for them, and re-layouts: 17.8 us -> 2.59 us
    pallas_call x1, Pallas kernels: 207 us -> 178 us  [first_forward(): pl.pallas_call(functools.partial(first_kernel, highs=highs, rows=rows, gr...]
    pallas_call x1, Pallas kernels: 130 us -> 119 us  [middle(): pl.pallas_call(functools.partial(middle_kernel, group=group), in_specs=[i...]
    unnamed x21 -> x1, local copies, waits for them, and re-layouts: 11.2 us -> 1.29 us
    pallas_call x2 -> x1, Pallas kernels: 23.6 us -> 19 us  [call(): pl.pallas_call(kernel, grid=grid, in_specs=in_specs, out_specs=out_specs,...]
where the time goes in v4:
time: 515 us; the launch traced here: 508 us
  Pallas kernels  504 us (98%)
    pallas_call x1, Pallas kernels, low_back(): pl.pallas_call(functools.partial(low_kernel, highs=highs, rows=rows, grou...  183 us
    pallas_call x1, Pallas kernels, first_forward(): pl.pallas_call(functools.partial(first_kernel, highs=highs, rows=rows, gr...  178 us
    pallas_call x1, Pallas kernels, middle(): pl.pallas_call(functools.partial(middle_kernel, group=group), in_specs=[i...  119 us
    pallas_call x1, Pallas kernels, call(): pl.pallas_call(kernel, grid=grid, in_specs=in_specs, out_specs=out_specs,...  19 us

profile of v4, /device:TPU:10, one launch (start us, length us, event | category | flops | bytes accessed | tf_op | source)
XLA Modules:
  0.0 508.2 jit_solution(9544639983055284187)
XLA Ops:
  0.6 1.3 copy.19.refs_7_
  1.9 178.3 %first_forward.1 = (bf16[512,1024]{1,0:T(8,128)(2,1)}, bf16[512,1024]{1,0:T(8,128)(2,1)}, bf16[4,2,2,3072,256]{4,3,2,1,0:T(8,128)(2,1)}, f32[8,1024]{1,0:T(8,128...) custom-call(bf16[2,256,1024]{2,1,0:T(8,128)(2,1)} %refs_0_.1, bf16[2,256,1024]{2,1,0:T(8,128)(2,1)} %refs_1_.1, ...), custom_call_target="tpu_custom_call" | custom-call | flops 12884901888 | bytes 25165824 | tf_op jit(solution)/shard_map/first_forward/pallas_call | solution.py:972
  180.3 119.4 %middle.1 = (bf16[512,1024]{1,0:T(8,128)(2,1)}, bf16[512,1024]{1,0:T(8,128)(2,1)}, bf16[2,2,512,1024]{3,2,1,0:T(8,128)(2,1)}, bf16[512,1024]{1,0:T(8,128)(2,1)},...) custom-call(bf16[512,1024]{1,0:T(8,128)(2,1)} %get-tuple-element.41., ...), custom_call_target="tpu_custom_call" | custom-call | flops 38654705664 | bytes 25165824 | tf_op jit(solution)/shard_map/middle/pallas_call | solution.py:1328
  299.7 19.0 %feed_back.1 = (bf16[512,1024]{1,0:T(8,128)(2,1)}, bf16[512,1024]{1,0:T(8,128)(2,1)}, bf16[512,4096]{1,0:T(8,128)(2,1)}, f32[1,4096]{1,0:T(1,128)}, f32[8,1024]{1,0:T(8,128)}, /*index=5*/f32[8,1024]{1,0:T(8,128)}) custom-call(bf16[512,1024]{1,0:T(8,128)(2,1)} %get-tuple-element.48.refs_0_, bf16[512,1024]{1,0:T(8,128)(2,1)} %get-tuple-element.49.refs_1_, ...), custom_call_target="tpu_custom_call" | custom-call | flops 8589934592 | bytes 16777216 | tf_op jit(solution)/shard_map/feed_back/pallas_call | solution.py:41
  318.7 182.5 %low_back.1 = (bf16[1,256,1024]{2,1,0:T(8,128)(2,1)}, bf16[1,256,256]{2,1,0:T(8,128)(2,1)}, bf16[1,256,1024]{2,1,0:T(8,128)(2,1)}, bf16[1,3,256,256]{3,2,1,0:T(8...) custom-call(bf16[512,1024]{1,0:T(8,128)(2,1)} %get-tuple-element.54., ...), custom_call_target="tpu_custom_call" | custom-call | flops 34359738368 | bytes 50331648 | tf_op jit(solution)/shard_map/low_back/pallas_call | solution.py:1571
  501.2 5.2 %finish.1 = (f32[1,2,256,1024]{3,2,1,0:T(8,128)}, f32[1,2,256,1024]{3,2,1,0:T(8,128)}, f32[1,3,256,256]{3,2,1,0:T(8,128)}, f32[1,256,256]{2,1,0:T(8,128)}, f32[1...) custom-call(bf16[1,256,1024]{2,1,0:T(8,128)(2,1)} %get-tuple-element, ...), custom_call_target="tpu_custom_call" | custom-call | tf_op jit(solution)/shard_map/finish/pallas_call | solution.py:1647
  506.4 1.3 copy.20

commit v5 on v4

--- a/solution.py
+++ b/solution.py
@@ -17,12 +17,11 @@
 MESH = pl.DeviceIdType.MESH
 
 QKV, OUT, UNIT = 0, 3, 4
-FEED_BLOCKS = 4
 
 F32 = jnp.float32
 BF16 = jnp.bfloat16
 VMEM_BYTES = 56 * 1024 * 1024
-LOW_VMEM = 63 * 1024 * 1024
+LOW_VMEM = 65200 * 1024
 
 
 def nn(left, right):
@@ -31,26 +30,6 @@
 
 def nt(left, right):
     return lax.dot_general(left, right, (((1,), (1,)), ((), ())), preferred_element_type=F32)
-
-
-def held(shape):
-    return pl.BlockSpec(shape, lambda *_: (0,) * len(shape), pipeline_mode=pl.Buffered(1))
-
-
-def call(kernel, grid, in_specs, out_specs, out_shape, scratch, name, flops, moved, args):
-    return pl.pallas_call(
-        kernel,
-        grid=grid,
-        in_specs=in_specs,
-        out_specs=out_specs,
-        out_shape=out_shape,
-        scratch_shapes=scratch,
-        name=name,
-        compiler_params=pltpu.CompilerParams(
-            vmem_limit_bytes=VMEM_BYTES, dimension_semantics=("arbitrary",) * len(grid)
-        ),
-        cost_estimate=pl.CostEstimate(flops=flops, bytes_accessed=moved, transcendentals=0),
-    )(*args)
 
 
 def shaped(shape, dtype):
@@ -73,20 +52,26 @@
     return lax.broadcasted_iota(jnp.int32, shape, axis) < HD
 
 
+def both_heads(array):
+    lanes = head_lanes(array.shape, 1)
+    return jnp.concatenate([jnp.where(lanes, array, 0), jnp.where(lanes, 0, array)], axis=0)
+
+
+def own_rows(array):
+    tokens = array.shape[1] // 2
+    return jnp.where(head_lanes((PAIR, tokens), 0), array[:, :tokens], array[:, tokens:])
+
+
 def pair_front(query, keys, values, bias_ref):
-    values_t = values.T
-    lanes = head_lanes(query.shape, 1)
-    outs, log_rows = [], []
-    for h in range(2):
-        mine = jnp.where(lanes if h == 0 else ~lanes, query, 0)
-        scores = nt(keys, mine) + bias_ref[...]
-        top = jnp.max(scores, axis=0, keepdims=True)
-        expo = jnp.exp(scores - top)
-        total = jnp.sum(expo, axis=0, keepdims=True)
-        outs.append(nn(values_t, expo.astype(BF16)) / total)
-        log_rows.append(top + jnp.log(total))
-    mixed_t = jnp.where(head_lanes(outs[0].shape, 0), outs[0], outs[1])
-    return mixed_t.T.astype(BF16), log_rows
+    tokens = query.shape[0]
+    bias = bias_ref[...]
+    scores = nt(keys, both_heads(query)) + jnp.concatenate([bias, bias], axis=1)
+    top = jnp.max(scores, axis=0, keepdims=True)
+    expo = jnp.exp(scores - top)
+    total = jnp.sum(expo, axis=0, keepdims=True)
+    mixed = own_rows(nn(values.T, expo.astype(BF16)) / total)
+    log_row = top + jnp.log(total)
+    return mixed.T.astype(BF16), [log_row[:, :tokens], log_row[:, tokens:]]
 
 
 def pair_back(query, grad, mixed, log_rows, keys, values, bias_ref, tile):
@@ -144,103 +129,8 @@
     return pre * below, below + pre * jnp.exp(-0.5 * pre * pre) * (2.0 * jnp.pi) ** -0.5
 
 
-def hidden_columns(block, width):
-    rows, _, tall, deep = block.shape
-    narrow = width // rows
-    parts = [block[:, 0, i * narrow : (i + 1) * narrow].reshape(width, deep) for i in range(FEED_BLOCKS)]
-    return jnp.concatenate(parts, axis=1)
-
-
-def feed_specs(weight, tokens, width, units):
-    rows, cols, _, deep = weight.shape
-    tall = FEED_BLOCKS * (width // rows)
-    block = FEED_BLOCKS * deep
-    per = units // cols // block
-
-    def at(first):
-        return pl.BlockSpec((rows, 1, tall, deep), lambda s: (0, s // per, first // FEED_BLOCKS + s % per, 0))
-
-    wide = pl.BlockSpec((tokens, block), lambda s: (0, s))
-    line = pl.BlockSpec((1, block), lambda s: (0, s))
-    return cols * per, at(UNIT), at(UNIT + per * FEED_BLOCKS), wide, line
-
-
 def column_sum(value):
     return jnp.sum(value, axis=0, keepdims=True)
-
-
-def feed_back_kernel(*refs, steps):
-    (dy_ref, hat2_ref, scale2_ref, hat1_ref, scale1_ref, slope_ref, wu_ref, wd_ref, v_ref) = refs[:9]
-    (ddown_ref, dattn_ref, dpre_ref, pre_ref, top_ref, feed_ref, acc_ref) = refs[9:]
-    s = pl.program_id(0)
-    tokens, width = dy_ref.shape
-
-    @pl.when(s == 0)
-    def _():
-        top_ref[...] = jnp.zeros_like(top_ref)
-        feed_ref[...] = jnp.zeros_like(feed_ref)
-
-        def some(at):
-            dy, hat = dy_ref[at].astype(F32), hat2_ref[at].astype(F32)
-            ddown = norm_back(dy, hat, scale2_ref[at][:, :1], v_ref[7:8]).astype(BF16)
-            ddown_ref[at] = ddown
-            top_ref[0:1] += column_sum(ddown.astype(F32))
-            top_ref[1:2] += column_sum(dy)
-            top_ref[2:3] += column_sum(dy * hat)
-
-        by_tokens(tokens, some)
-
-    dact = nn(ddown_ref[...], hidden_columns(wd_ref[...], width))
-    dpre = (dact * slope_ref[...].astype(F32)).astype(BF16)
-    back = nt(dpre, hidden_columns(wu_ref[...], width))
-    dpre_ref[...] = dpre
-    pre_ref[...] = column_sum(dpre.astype(F32))
-
-    @pl.when(s == 0)
-    def _():
-        acc_ref[...] = back
-
-    @pl.when(s > 0)
-    def _():
-        acc_ref[...] += back
-
-    @pl.when(s == steps - 1)
-    def _():
-        def some(at):
-            dx1, hat = ddown_ref[at].astype(F32) + acc_ref[at], hat1_ref[at].astype(F32)
-            dattn = norm_back(dx1, hat, scale1_ref[at][:, :1], v_ref[6:7]).astype(BF16)
-            dattn_ref[at] = dattn
-            feed_ref[0:1] += column_sum(dattn.astype(F32))
-            feed_ref[1:2] += column_sum(dx1)
-            feed_ref[2:3] += column_sum(dx1 * hat)
-
-        by_tokens(tokens, some)
-
-
-def feed_back(dy, hat2, scale2, hat1, scale1, slope, weight, vectors):
-    tokens, width = dy.shape
-    units = slope.shape[1]
-    steps, first, second, wide, line = feed_specs(weight, tokens, width, units)
-    flat, thin = held((tokens, width)), held((tokens, 128))
-    return call(
-        functools.partial(feed_back_kernel, steps=steps),
-        (steps,),
-        [flat, flat, thin, flat, thin, wide, first, second, held(vectors.shape)],
-        [flat, flat, wide, line, held((8, width)), held((8, width))],
-        [
-            shaped((tokens, width), BF16),
-            shaped((tokens, width), BF16),
-            shaped((tokens, units), BF16),
-            shaped((1, units), F32),
-            shaped((8, width), F32),
-            shaped((8, width), F32),
-        ],
-        [pltpu.VMEM((tokens, width), F32)],
-        "feed_back",
-        4 * tokens * width * units,
-        4 * width * units,
-        (dy, hat2, scale2, hat1, scale1, slope, weight, weight, vectors),
-    )
 
 
 class Layout:
@@ -408,7 +298,7 @@
             index = (slice(None),) if first else (0,)
             return (
                 self.cut(q, self.from_high.at[(q, step - 1, way) + index]),
-                self.cut(q, self.got_high.at[(q % 2, way) + index]),
+                self.cut(q, self.got_high.at[(way,) + index]),
             )
         ref = (self.from_wide if first else self.from_row).at[self.place[q], step - 1, way]
         return (self.cut(q, ref),) * 2
@@ -496,7 +386,8 @@
         stages = [self.stages(q) for q in range(len(self.pieces))]
         depth, count = len(stages[0]), len(stages)
         for tick in range(count + depth - 1):
-            for q in range(max(0, tick - depth + 1), min(tick + 1, count)):
+            alive = range(max(0, tick - depth + 1), min(tick + 1, count))
+            for q in alive:
                 stages[q][tick - q]()
             between(tick)
         for q in range(count):
@@ -520,6 +411,9 @@
 
     def neighbour(self, right):
         return {self.axis: self.here + (1 if right else -1)}
+
+
+AHEAD = 2
 
 
 class Gather:
@@ -599,7 +493,7 @@
             if first is self.row:
                 self.over(q, self.row.here)
 
-        steps = [begin]
+        steps = [begin] + [lambda: None] * AHEAD
         lines = [(first, i) for i in range(1, first.size)] + [(second, i) for i in range(1, second.size)]
         for n, (line, step) in enumerate(lines):
 
@@ -1352,11 +1246,12 @@
 
 
 def low_kernel(*refs, highs, rows, group):
-    (ddown_hbm, act_hbm, x1_hbm, dpre_hbm, dattn_hbm, q_hbm, mixed_hbm, log_hbm, x_hbm, w_hbm, kv_hbm) = refs[:11]
-    bias_doc_q, bias_doc_k, pre_ref, top_sums, feed_sums = refs[11:16]
-    down_out, out_out, unit_out, qkv_out, small_out, landed, landing, high_landing = refs[16:24]
-    (dattn, x, q, mixed, log, w_out, w_qkv, kv, dmixed, bias, dkv_got, dx, stage, small, left, right,
-     work, got, got_high, from_row, from_wide, sem_in, sem_right, sem_core, sem_load, sem_high, sem_row, sem_kv, sem_out) = refs[24:]
+    (dy_hbm, hat2_hbm, hat1_hbm, slope_hbm, act_hbm, x1_hbm, q_hbm, mixed_hbm, log_hbm, x_hbm, w_hbm, kv_hbm) = refs[:12]
+    bias_doc_q, bias_doc_k, scale2, scale1, vectors = refs[12:17]
+    down_out, out_out, unit_out, qkv_out, small_out, landed, landing, high_landing, dpre_hbm = refs[17:26]
+    (dattn, x, q, mixed, log, w, kv, dmixed, bias, dkv_got, dx, stage, small, left, right,
+     work, got, got_high, from_row, from_wide, sem_in, sem_right, sem_core, sem_load, sem_high, sem_row, sem_kv, sem_out,
+     acc, top_sums, feed_sums, pre, sem_w, sem_slope, sem_dpre) = refs[26:]
     tokens, width = dattn.shape
     narrow, deep = stage.shape[-2:]
     dq, dkv = q, kv
@@ -1368,11 +1263,13 @@
     units = act_hbm.shape[1]
     feed_pieces = units // cols // deep
     tail = small.shape[3]
-    order = [("down", i) for i in range(feed_pieces)] + [("out", 0)]
-    order += [("unit", i) for i in range(feed_pieces)] + [("qkv", 0), ("qkv", 1), ("qkv", 2), ("small", 0)]
+    order = [("down", i) for i in range(feed_pieces)] + [("unit", i) for i in range(feed_pieces)]
+    order += [("out", 0), ("qkv", 0), ("qkv", 1), ("small", 0), ("qkv", 2)]
     row_first = (("unit", 0),)
-    pieces = [(stage.at[i % STAGES], narrow, order[i] not in row_first) for i in range(len(order) - 1)]
-    pieces += [(small, tail, True)]
+    pieces = [
+        (small, tail, True) if name == "small" else (stage.at[n % STAGES], narrow, (name, i) not in row_first)
+        for n, (name, i) in enumerate(order)
+    ]
 
     def give(q, ref):
         name, i = order[q]
@@ -1390,33 +1287,128 @@
         pieces, (landing, work, got, high_landing, got_high, from_row, from_wide, sem_core, sem_load, sem_high, sem_row), highs, rows, give,
     )
 
+    def at_block(first, count):
+        return pl.ds(first * narrow, count * narrow)
+
+    hat2, hat1, dy, dpres, slopes = kv.at[0, 0], kv.at[0, 1], kv.at[1, 0], (q, mixed), (kv.at[1, 1], dmixed)
+    first_inputs = [(dy_hbm, dy), (hat2_hbm, hat2), (x1_hbm, x), (hat1_hbm, hat1)]
     inputs = [
-        (ddown_hbm, dattn),
-        (x1_hbm, x),
-        (dattn_hbm, dattn),
-        (w_hbm.at[:, :, pl.ds(OUT * narrow, narrow)], w_out),
+        (w_hbm.at[:, :, :, at_block(OUT, 1)], w.at[:, :, :, at_block(OUT, 1)]),
         (mixed_hbm, mixed),
         (q_hbm, q),
         (log_hbm, log),
         (kv_hbm, kv),
-        (w_hbm.at[:, :, pl.ds(QKV * narrow, 3 * narrow)], w_qkv),
+        (w_hbm.at[:, :, :, at_block(QKV, 3)], w.at[:, :, :, at_block(QKV, 3)]),
         (x_hbm, x),
     ]
-    loads = [pltpu.make_async_copy(a, b, sem_in.at[i]) for i, (a, b) in enumerate(inputs)]
-    early = 8
+    first_loads = [pltpu.make_async_copy(a, b, sem_in.at[i]) for i, (a, b) in enumerate(first_inputs)]
+    loads = [pltpu.make_async_copy(a, b, sem_in.at[len(first_inputs) + i]) for i, (a, b) in enumerate(inputs)]
+    early = 5
+
+    def get_w(block):
+        slot = block % 2
+        return [
+            pltpu.make_async_copy(
+                w_hbm.at[:, :, :, at_block(UNIT + j * feed_pieces + block, 1)],
+                w.at[:, :, :, at_block(2 * slot + j, 1)],
+                sem_w.at[slot, j],
+            )
+            for j in range(2)
+        ]
+
+    def columns_of(ref, buffer, block, sems, out):
+        copies = []
+        for k in range(cols):
+            far = ref.at[:, pl.ds((k * feed_pieces + block) * deep, deep)]
+            near = buffer.at[:, pl.ds(k * deep, deep)]
+            copies.append(pltpu.make_async_copy(*((near, far) if out else (far, near)), sems.at[k]))
+        return copies
+
+    def get_slope(block):
+        return columns_of(slope_hbm, slopes[block % 2], block, sem_slope.at[block % 2], False)
+
+    def put_dpre(block):
+        return columns_of(dpre_hbm, dpres[block % 2], block, sem_dpre.at[block % 2], True)
+
+    def top():
+        top_sums[...] = jnp.zeros_like(top_sums)
+        feed_sums[...] = jnp.zeros_like(feed_sums)
+
+        def some(at):
+            grad, hat = dy[at].astype(F32), hat2[at].astype(F32)
+            ddown = norm_back(grad, hat, scale2[at][:, :1], vectors[7:8]).astype(BF16)
+            dattn[at] = ddown
+            top_sums[0:1] += column_sum(ddown.astype(F32))
+            top_sums[1:2] += column_sum(grad)
+            top_sums[2:3] += column_sum(grad * hat)
+
+        by_tokens(tokens, some)
+
+    def turn(block):
+        for copy in get_w(block) + get_slope(block):
+            copy.wait()
+        if block >= 2:
+            for copy in put_dpre(block - 2):
+                copy.wait()
+
+        for ks in (range(cols // 2), range(cols // 2, cols)):
+
+            def matrix(j):
+                some = at_block(2 * (block % 2) + j, 1)
+                parts = [w[:, k // CORES, k % CORES, some].reshape(width, deep) for k in ks]
+                return jnp.concatenate(parts, axis=1)
+
+            at = slice(ks[0] * deep, (ks[-1] + 1) * deep)
+            dpre = (nn(dattn[...], matrix(1)) * slopes[block % 2][:, at].astype(F32)).astype(BF16)
+            dpres[block % 2][:, at] = dpre
+            total = column_sum(dpre.astype(F32))
+            for i, k in enumerate(ks):
+                begin = (k * feed_pieces + block) * deep
+                pre[:, begin : begin + deep] = total[:, i * deep : (i + 1) * deep]
+            more = nt(dpre, matrix(0))
+            if block == 0 and ks[0] == 0:
+                acc[...] = more
+            else:
+                acc[...] += more
+        for copy in put_dpre(block):
+            copy.start()
+        if block + 2 < feed_pieces:
+            for copy in get_w(block + 2) + get_slope(block + 2):
+                copy.start()
+
+    def bottom():
+        def some(at):
+            dx1, hat = dattn[at].astype(F32) + acc[at], hat1[at].astype(F32)
+            grad = norm_back(dx1, hat, scale1[at][:, :1], vectors[6:7]).astype(BF16)
+            dattn[at] = grad
+            feed_sums[0:1] += column_sum(grad.astype(F32))
+            feed_sums[1:2] += column_sum(dx1)
+            feed_sums[2:3] += column_sum(dx1 * hat)
+
+        by_tokens(tokens, some)
+        for block in range(max(0, feed_pieces - 2), feed_pieces):
+            for copy in put_dpre(block):
+                copy.wait()
+        for load in loads[:-1]:
+            load.start()
 
     key_grads = share_key_grads(sharing, kv, dkv_got, sem_kv)
     take = row_blocks(rows, narrow)
 
+    def w_out(r):
+        some = w[pl.ds(r * take, take), :, :, at_block(OUT, 1)]
+        return some.reshape(take, cols, narrow, deep)
+
     def prepare():
-        for load in loads[2:early]:
+        for load in loads[:early]:
             load.wait()
-        bias[...] = jnp.where(bias_doc_k[...] == bias_doc_q[...], 0.0, NEG_BIG).astype(BF16)
+        doc_k = jnp.broadcast_to(bias_doc_k[...], (128, bias_doc_k.shape[1])).T[:, :1]
+        bias[...] = jnp.where(doc_k == bias_doc_q[...], 0.0, NEG_BIG).astype(BF16)
 
         @pl.loop(0, rows // take)
         def _(r):
             at = pl.ds(pl.multiple_of(r * take * narrow, take * narrow), take * narrow)
-            dmixed[:, at] = nt(dattn[...], side_by_side(w_out[pl.ds(r * take, take)])).astype(BF16)
+            dmixed[:, at] = nt(dattn[...], side_by_side(w_out(r))).astype(BF16)
 
     def fill(slot, block, loaded=None):
         @pl.loop(0, cols)
@@ -1446,9 +1438,7 @@
         name, i = order[q]
         slot = q % STAGES
         if q == 0:
-            loads[0].wait()
             left[...] = dattn[...].T
-            loads[2].start()
         if name in ("down", "unit"):
             if (name, i) == ("unit", 0):
                 left[...] = x[...].T
@@ -1460,9 +1450,6 @@
                     copy.start()
             fill(slot, column(right.at[q % 2]))
         elif name == "out":
-            if is_feed(q + 1):
-                for copy in fetch(q + 1):
-                    copy.start()
             left[...] = mixed[...].T
             fill(slot, column(dattn))
         elif name == "qkv":
@@ -1497,66 +1484,71 @@
             at = slice(k * deep, (k + 1) * deep)
             total = dattn[:, at].astype(F32)
             for j in range(3):
-                total += nn(grads_of(j), w_qkv[:, k, j * narrow : (j + 1) * narrow].reshape(width, deep))
+                total += nn(grads_of(j), w[:, k // CORES, k % CORES, at_block(QKV + j, 1)].reshape(width, deep))
             for piece in range(0, deep, min(narrow, deep)):
                 r, inside = divmod(k * deep + piece, narrow)
                 dx[r, inside : inside + min(narrow, deep)] = total[:, piece : piece + min(narrow, deep)].T.astype(BF16)
 
     def small_sums():
-        vectors = [column_sum(grads_of(j).astype(F32)) for j in (0, 2)]
-        vectors += [feed_sums[0:2], top_sums[0:2], feed_sums[2:3], top_sums[2:3]]
-        vectors = jnp.concatenate(vectors, axis=0)
-        vectors = vectors.astype(BF16)
+        parts = [column_sum(grads_of(j).astype(F32)) for j in (0, 2)]
+        parts += [feed_sums[0:2], top_sums[0:2], feed_sums[2:3], top_sums[2:3]]
+        rows_of = jnp.concatenate(parts, axis=0).astype(BF16)
         small[...] = jnp.zeros_like(small)
-        lines = pre_ref.shape[1] // cols // deep
+        lines = pre.shape[1] // cols // deep
         for r in range(rows):
             for k in range(cols):
-                small[r, k // CORES, k % CORES, 0:8, 0:narrow] = vectors[:, r * narrow : (r + 1) * narrow]
+                small[r, k // CORES, k % CORES, 0:8, 0:narrow] = rows_of[:, r * narrow : (r + 1) * narrow]
                 for i in range(lines):
                     at = (k * lines + i) * deep
-                    small[r, k // CORES, k % CORES, 8 + i : 9 + i] = pre_ref[:, at : at + deep].astype(BF16)
-
-    share = max(1, pairs // 8)
+                    small[r, k // CORES, k % CORES, 8 + i : 9 + i] = pre[:, at : at + deep].astype(BF16)
+
+    share = max(1, pairs // 4)
 
     def between(tick):
-        if tick == 1:
+        if tick < feed_pieces:
+            turn(tick)
+        if tick == feed_pieces:
+            bottom()
+        if tick == feed_pieces + 1:
             prepare()
-        if 2 <= tick < 9:
-            heads((tick - 2) * share, share if tick < 8 else pairs - 6 * share)
-        if tick == 8:
+        if feed_pieces + 1 <= tick < feed_pieces + 5:
+            heads((tick - feed_pieces - 1) * share, share)
+        if tick == feed_pieces + 4:
             exchange()
-        if tick == 9:
+        if tick == feed_pieces + 5:
             join()
         if tick + 1 < len(order):
             make(tick + 1)
-        if tick == 9:
+        if tick == feed_pieces + 5:
             input_gradient()
             streams.start(dx)
 
-    for i, load in enumerate(loads[:-1]):
-        if i != 2:
-            load.start()
-    for copy in fetch(0):
+    for load in first_loads:
+        load.start()
+    for copy in fetch(0) + get_w(0) + get_slope(0) + (get_w(1) + get_slope(1) if feed_pieces > 1 else []):
         copy.start()
     greet((scatter.high, scatter.row), ("core",), sharing.members(), streams.sources())
-    loads[1].wait()
+    for load in first_loads:
+        load.wait()
+    top()
     make(0)
     scatter.run(between)
     streams.wait_sent(dx)
     streams.wait_here()
 
 
-def low_back(ddown, act, x1_bf, dpre, dattn, query, mixed, log_total, x, weight, shared, doc_query, doc_key, pre_sum, top_sums, feed_sums):
-    tokens, width = dattn.shape
-    rows, cols, _, deep = weight.shape
+def low_back(dy, hat2, scale2, hat1, scale1, slope, act, x1_bf, query, mixed, log_total, x, weight, shared, doc_query, doc_key, vectors):
+    tokens, width = dy.shape
+    rows, highs, _, _, deep = weight.shape
+    cols = highs * CORES
     narrow = width // rows
     units = act.shape[1]
     feed_rows = narrow * units // cols // deep
-    highs, group = cols // CORES, shared.shape[0]
+    group = shared.shape[0]
     keys = group * tokens
     apart = (rows, highs, CORES)
     tail = 16
-    lines = 8 + pre_sum.shape[1] // cols // deep
+    lines = 8 + units // cols // deep
     assert lines <= tail and narrow <= deep
     count = 2 * (feed_rows // narrow) + 5
     wide = 1
@@ -1567,11 +1559,11 @@
     ways = {2: 1}
     block = (rows, narrow, deep)
     dma = pltpu.SemaphoreType.DMA
-    args = [ddown, act, x1_bf, dpre, dattn, query, mixed, log_total, x, weight, shared]
-    *outs, _, _ = pl.pallas_call(
+    args = [dy, hat2, hat1, slope, act, x1_bf, query, mixed, log_total, x, weight, shared]
+    *outs, _, _, _ = pl.pallas_call(
         functools.partial(low_kernel, highs=highs, rows=rows, group=group),
         in_specs=[in_any] * len(args) + [in_vmem] * 5,
-        out_specs=[in_vmem] * 5 + [in_any] * 3,
+        out_specs=[in_vmem] * 5 + [in_any] * 4,
         out_shape=[
             shaped((1, narrow, units // cols), BF16),
             shaped((1, narrow, deep), BF16),
@@ -1581,6 +1573,7 @@
             shaped((rows, narrow, tokens), BF16),
             shaped((count, highs) + block, BF16),
             shaped((count, highs - 1, ways.get(highs, 2)) + block, BF16),
+            shaped((tokens, units), BF16),
         ],
         scratch_shapes=[
             pltpu.VMEM((tokens, width), BF16),
@@ -1588,8 +1581,7 @@
             pltpu.VMEM((tokens, width), BF16),
             pltpu.VMEM((tokens, width), BF16),
             pltpu.VMEM(log_total.shape, F32),
-            pltpu.VMEM((rows, cols, narrow, deep), BF16),
-            pltpu.VMEM((rows, cols, 3 * narrow, deep), BF16),
+            pltpu.VMEM(apart + (4 * narrow, deep), BF16),
             pltpu.VMEM((group, 2, tokens, width), BF16),
             pltpu.VMEM((tokens, width), BF16),
             pltpu.VMEM((keys, tokens), BF16),
@@ -1601,10 +1593,10 @@
             pltpu.VMEM((2, tokens, cols * deep), BF16),
             pltpu.VMEM((slots, highs) + block, BF16),
             pltpu.VMEM((2, highs) + block, BF16),
-            pltpu.VMEM((2, ways.get(highs, 2)) + block, BF16),
+            pltpu.VMEM((ways.get(highs, 2),) + block, BF16),
             pltpu.VMEM((count - wide, rows - 1, ways.get(rows, 2), narrow, deep), BF16),
             pltpu.VMEM((wide, rows - 1, ways.get(rows, 2), highs, narrow, deep), BF16),
-            dma((10,)),
+            dma((11,)),
             dma((2, cols)),
             dma((count, highs, 2)),
             dma((count, highs, 2)),
@@ -1612,13 +1604,20 @@
             dma((count, rows - 1, 2, 2)),
             dma((max(1, group - 1), 2)),
             dma((rows, 2)),
+            pltpu.VMEM((tokens, width), F32),
+            pltpu.VMEM((8, width), F32),
+            pltpu.VMEM((8, width), F32),
+            pltpu.VMEM((1, units), F32),
+            dma((2, 2)),
+            dma((2, cols)),
+            dma((2, cols)),
         ],
         name="low_back",
         compiler_params=pltpu.CompilerParams(collective_id=1, has_side_effects=True, vmem_limit_bytes=LOW_VMEM),
         cost_estimate=pl.CostEstimate(
             flops=64 * tokens * width * width, bytes_accessed=12 * width * units, transcendentals=0
         ),
-    )(*args, doc_query, doc_key, pre_sum, top_sums, feed_sums)
+    )(*args, doc_query, doc_key.reshape(1, keys), scale2, scale1, vectors)
     return outs
 
 
@@ -1654,7 +1653,7 @@
 
 def local(tokens_in, doc_ids, cotangent, qkv_master, out_master, unit_master, down_master, unit_bias, width_bias, norm_gain):
     at = Layout(tokens_in, doc_ids)
-    rows, cols, deep = at.rows, at.cols, out_master.shape[2]
+    rows, cols = at.rows, at.cols
 
     second_in, start, weights, vectors, unit_shift, doc_query, doc_key = first_forward(
         tokens_in, cotangent, qkv_master, out_master, unit_master, down_master, unit_bias, width_bias, norm_gain, doc_ids,
@@ -1663,13 +1662,9 @@
     (
         dy, query, shared, mixed, log_total, x1_bf, hat_one, scale_one, hat_two, scale_two, act, slope, stream,
     ) = middle(second_in, start, weights, vectors, unit_shift, doc_query, doc_key, at.group)
-    weights = weights.reshape(rows, cols, -1, deep)
-    ddown, dattn, dpre, pre_sum, top_sums, feed_sums = feed_back(
-        dy, hat_two, scale_two, hat_one, scale_one, slope, weights, vectors
-    )
     *grads, input_grad = low_back(
-        ddown, act, x1_bf, dpre, dattn, query, mixed, log_total, second_in, weights, shared, doc_query, doc_key,
-        pre_sum, top_sums, feed_sums,
+        dy, hat_two, scale_two, hat_one, scale_one, slope, act, x1_bf, query, mixed, log_total, second_in, weights, shared,
+        doc_query, doc_key, vectors,
     )
     return finish(*grads, stream, input_grad, at.micro)
 

time: 515 us -> 500 us (0.971)
  Pallas kernels: 504 us -> 485 us
    pallas_call x1 -> x0, Pallas kernels: 19 us -> none  [call(): pl.pallas_call(kernel, grid=grid, in_specs=in_specs, out_specs=out_specs,...]
where the time goes in v5:
time: 500 us; the launch traced here: 491 us
  Pallas kernels  485 us (97%)
    pallas_call x1, Pallas kernels, first_forward(): pl.pallas_call(functools.partial(first_kernel, highs=highs, rows=rows, gr...  182 us
    pallas_call x1, Pallas kernels, low_back(): pl.pallas_call(functools.partial(low_kernel, highs=highs, rows=rows, grou...  180 us
    pallas_call x1, Pallas kernels, middle(): pl.pallas_call(functools.partial(middle_kernel, group=group), in_specs=[i...  118 us

profile of v5, /device:TPU:10, one launch (start us, length us, event | category | flops | bytes accessed | tf_op | source)
XLA Modules:
  0.0 490.9 jit_solution(7944595468589379075)
XLA Ops:
  0.6 1.3 copy.21.refs_7_
  1.9 182.1 %first_forward.1 = (bf16[512,1024]{1,0:T(8,128)(2,1)}, bf16[512,1024]{1,0:T(8,128)(2,1)}, bf16[4,2,2,3072,256]{4,3,2,1,0:T(8,128)(2,1)}, f32[8,1024]{1,0:T(8,128...) custom-call(bf16[2,256,1024]{2,1,0:T(8,128)(2,1)} %refs_0_.1, bf16[2,256,1024]{2,1,0:T(8,128)(2,1)} %refs_1_.1, ...), custom_call_target="tpu_custom_call" | custom-call | flops 12884901888 | bytes 25165824 | tf_op jit(solution)/shard_map/first_forward/pallas_call | solution.py:866
  184.0 1.8 reduce
  185.9 117.9 %middle.1 = (bf16[512,1024]{1,0:T(8,128)(2,1)}, bf16[512,1024]{1,0:T(8,128)(2,1)}, bf16[2,2,512,1024]{3,2,1,0:T(8,128)(2,1)}, bf16[512,1024]{1,0:T(8,128)(2,1)},...) custom-call(bf16[512,1024]{1,0:T(8,128)(2,1)} %get-tuple-element.35., ...), custom_call_target="tpu_custom_call" | custom-call | flops 38654705664 | bytes 25165824 | tf_op jit(solution)/shard_map/middle/pallas_call | solution.py:1222
  303.8 180.1 %low_back.1 = (bf16[1,256,1024]{2,1,0:T(8,128)(2,1)}, bf16[1,256,256]{2,1,0:T(8,128)(2,1)}, bf16[1,256,1024]{2,1,0:T(8,128)(2,1)}, bf16[1,3,256,256]{3,2,1,0:T(8...) custom-call(bf16[512,1024]{1,0:T(8,128)(2,1)} %get-tuple-element.42., ...), custom_call_target="tpu_custom_call" | custom-call | flops 34359738368 | bytes 50331648 | tf_op jit(solution)/shard_map/low_back/pallas_call | solution.py:1563
  483.9 5.2 %finish.1 = (f32[1,2,256,1024]{3,2,1,0:T(8,128)}, f32[1,2,256,1024]{3,2,1,0:T(8,128)}, f32[1,3,256,256]{3,2,1,0:T(8,128)}, f32[1,256,256]{2,1,0:T(8,128)}, f32[1...) custom-call(bf16[1,256,1024]{2,1,0:T(8,128)(2,1)} %get-tuple-element, ...), custom_call_target="tpu_custom_call" | custom-call | tf_op jit(solution)/shard_map/finish/pallas_call | solution.py:1646
  489.2 1.3 copy.22

commit v6 on v5

--- a/solution.py
+++ b/solution.py
@@ -778,7 +778,7 @@
     base = 3
 
     def between(tick, done):
-        if tick == 2:
+        if tick == 5:
             begin()
         if done >= 1:
             to_hbm(done).start()
@@ -1265,7 +1265,7 @@
     tail = small.shape[3]
     order = [("down", i) for i in range(feed_pieces)] + [("unit", i) for i in range(feed_pieces)]
     order += [("out", 0), ("qkv", 0), ("qkv", 1), ("small", 0), ("qkv", 2)]
-    row_first = (("unit", 0),)
+    row_first = ()
     pieces = [
         (small, tail, True) if name == "small" else (stage.at[n % STAGES], narrow, (name, i) not in row_first)
         for n, (name, i) in enumerate(order)
@@ -1551,7 +1551,7 @@
     lines = 8 + units // cols // deep
     assert lines <= tail and narrow <= deep
     count = 2 * (feed_rows // narrow) + 5
-    wide = 1
+    wide = 0
     steps = 4 + highs - 1 + rows - 1
     slots = min(count, steps)
     in_any = pl.BlockSpec(memory_space=pl.ANY)
@@ -1595,7 +1595,7 @@
             pltpu.VMEM((2, highs) + block, BF16),
             pltpu.VMEM((ways.get(highs, 2),) + block, BF16),
             pltpu.VMEM((count - wide, rows - 1, ways.get(rows, 2), narrow, deep), BF16),
-            pltpu.VMEM((wide, rows - 1, ways.get(rows, 2), highs, narrow, deep), BF16),
+            pltpu.VMEM((max(1, wide), rows - 1, ways.get(rows, 2), highs, narrow, deep), BF16),
             dma((11,)),
             dma((2, cols)),
             dma((count, highs, 2)),

time: 500 us -> 498 us (level)
  the two profiles are of different devices: /device:TPU:10 before, /device:TPU:2 now
where the time goes in v6:
time: 498 us; the launch traced here: 488 us
  Pallas kernels  483 us (97%)
    pallas_call x1, Pallas kernels, low_back(): pl.pallas_call(functools.partial(low_kernel, highs=highs, rows=rows, grou...  181 us
    pallas_call x1, Pallas kernels, first_forward(): pl.pallas_call(functools.partial(first_kernel, highs=highs, rows=rows, gr...  178 us
    pallas_call x1, Pallas kernels, middle(): pl.pallas_call(functools.partial(middle_kernel, group=group), in_specs=[i...  118 us

profile of v6, /device:TPU:2, one launch (start us, length us, event | category | flops | bytes accessed | tf_op | source)
XLA Modules:
  0.0 488.2 jit_solution(11831475456587764449)
XLA Ops:
  0.6 1.3 copy.21.refs_7_
  1.9 178.2 %first_forward.1 = (bf16[512,1024]{1,0:T(8,128)(2,1)}, bf16[512,1024]{1,0:T(8,128)(2,1)}, bf16[4,2,2,3072,256]{4,3,2,1,0:T(8,128)(2,1)}, f32[8,1024]{1,0:T(8,128...) custom-call(bf16[2,256,1024]{2,1,0:T(8,128)(2,1)} %refs_0_.1, bf16[2,256,1024]{2,1,0:T(8,128)(2,1)} %refs_1_.1, ...), custom_call_target="tpu_custom_call" | custom-call | flops 12884901888 | bytes 25165824 | tf_op jit(solution)/shard_map/first_forward/pallas_call | solution.py:866
  180.2 1.8 reduce
  182.0 117.9 %middle.1 = (bf16[512,1024]{1,0:T(8,128)(2,1)}, bf16[512,1024]{1,0:T(8,128)(2,1)}, bf16[2,2,512,1024]{3,2,1,0:T(8,128)(2,1)}, bf16[512,1024]{1,0:T(8,128)(2,1)},...) custom-call(bf16[512,1024]{1,0:T(8,128)(2,1)} %get-tuple-element.35., ...), custom_call_target="tpu_custom_call" | custom-call | flops 38654705664 | bytes 25165824 | tf_op jit(solution)/shard_map/middle/pallas_call | solution.py:1222
  299.9 181.3 %low_back.1 = (bf16[1,256,1024]{2,1,0:T(8,128)(2,1)}, bf16[1,256,256]{2,1,0:T(8,128)(2,1)}, bf16[1,256,1024]{2,1,0:T(8,128)(2,1)}, bf16[1,3,256,256]{3,2,1,0:T(8...) custom-call(bf16[512,1024]{1,0:T(8,128)(2,1)} %get-tuple-element.42., ...), custom_call_target="tpu_custom_call" | custom-call | flops 34359738368 | bytes 50331648 | tf_op jit(solution)/shard_map/low_back/pallas_call | solution.py:1563
  481.2 5.2 %finish.1 = (f32[1,2,256,1024]{3,2,1,0:T(8,128)}, f32[1,2,256,1024]{3,2,1,0:T(8,128)}, f32[1,3,256,256]{3,2,1,0:T(8,128)}, f32[1,256,256]{2,1,0:T(8,128)}, f32[1...) custom-call(bf16[1,256,1024]{2,1,0:T(8,128)(2,1)} %get-tuple-element, ...), custom_call_target="tpu_custom_call" | custom-call | tf_op jit(solution)/shard_map/finish/pallas_call | solution.py:1646
  486.4 1.3 copy.22
